TPU v7x, 32 devices: a whole 2x2x4 slice. The times are simulated.
32 devices in a mesh: row: 4 (over z), col: 8 (over y, x, core).
Axes of the slice: x: 2, y: 2, z: 4, core: 2. Of those that a mesh axis runs over, the one named last changes fastest.
Arguments:
- amplitudes: bfloat16 [4, 256, 4096], P('row', 'col'), may hold values from -6 to 6
- integrals: bfloat16 [512, 4096], P('col', 'row'), may hold values from -0.125 to 0.125
- panel_owner: int32 [4, 8], P('row'), may hold values from 0 to 7, each once within a row
- residual_in: float32 [4, 256, 512], P(None, 'col', 'row'), may hold values from -6 to 6
Outputs:
- residual_out: float32 [4, 256, 512], P(None, 'col', 'row')
Inputs may be any that keep to these rules, and one draw needn't show every extreme that they name: `panel_owner`: each row is a permutation of 0 to 7.
All inputs are finite; a program needn't handle non-finite values.
Results may differ from a plain program's by a relative error of at most 0.0003.
Values may be sent and summed in bfloat16 or wider, within the bound.
No kernel may reach another device: no remote copies, remote signals or barrier semaphores. Data moves between devices by JAX's collectives and lax.ppermute only.
A program may use at most 64 MiB of HBM per device.

v0:
```python
import jax
import jax.numpy as jnp
from jax import lax
from jax.sharding import PartitionSpec as P


def shards(amplitudes, integrals, panel_owner, residual_in):
    columns = lax.axis_size("col")
    contraction = lax.all_to_all(amplitudes, "row", split_axis=2, concat_axis=0, tiled=True)
    rows_total = contraction.shape[0] * contraction.shape[1]
    k_local = contraction.shape[2]
    flattened = contraction.reshape(rows_total, k_local)
    block_rows = integrals.shape[0]
    ab_width = block_rows * columns
    inverse = jnp.argsort(panel_owner[0])
    partial_value = lax.dot_general(
        flattened,
        lax.all_gather(integrals, "col", axis=0, tiled=True),
        (((1,), (1,)), ((), ())),
        preferred_element_type=jnp.float32,
    )
    ordered = jnp.take(
        partial_value.reshape(rows_total, columns, block_rows), inverse, axis=1
    ).reshape(rows_total, ab_width)
    summed = lax.psum_scatter(ordered, "row", scatter_dimension=1, tiled=True)
    return residual_in + summed.reshape(residual_in.shape)


def solution(mesh):
    placed = (P("row", "col", None), P("col", "row"), P("row", None), P(None, "col", "row"))
    return jax.shard_map(
        shards, mesh=mesh, in_specs=placed, out_specs=P(None, "col", "row"), check_vma=False
    )
```

profile of v0, /device:TPU:0, one launch (start us, length us, event | category | flops | bytes accessed | tf_op | source)
XLA Modules:
  0.0 85.5 jit_solution(7635630345062924771)
XLA Ops:
  6.5 0.0 all-gather.2.cloned.1.call-start
  6.5 0.7 all-gather.2.cloned.1.call-update
  7.3 4.5 %copy.10 = bf16[1,32,4096]{1,0,2:T(2,128)(2,1)S(1)} copy(bf16[1,32,4096]{2,1,0:T(8,128)(2,1)} %param.4) | data formatting | bytes 524288 | tf_op args[0]
  11.8 0.5 broadcast.18
  12.3 0.0 copy-start.1
  12.3 22.4 %reduce = bf16[4096,32]{1,0:T(8,128)(2,1)S(1)} reduce(bf16[4096,1,32]{2,1,0:T(2,128)(2,1)S(1)} %bitcast.16, bf16[]{:T(256)} %broadcast.18), dimensions={1}, to_apply=%bitcast.11.reduce_sub_computation | reduce | bytes 524290
  34.7 1.7 %reshape.29 = bf16[4,2,16384]{2,1,0:T(2,128)(2,1)} reshape(bf16[4096,32]{1,0:T(8,128)(2,1)S(1)} %reduce) | data formatting | bytes 524288
  36.4 6.3 %all-to-all-start = ((bf16[4,2,16384]{2,1,0:T(2,128)(2,1)}), bf16[4,2,16384]{2,1,0:T(2,128)(2,1)S(1)}, u32[]{:S(2)}, u32[]{:S(2)}) async-start(bf16[4,2,16384]{2,1,0:T(2,128)(2,1)} %reshape.29), calls=%async_computation | async-start | bytes 524288 | tf_op jit(solution)/shard_map/all_to_all | solution.py:9
  42.7 0.0 reduce-scatter.2.cloned.1.call-start
  42.7 0.0 copy-done.1
  42.7 1.0 %sort.17 = (s32[8]{0:T(128)}, s32[8]{0:T(128)S(1)}) sort(s32[8]{0:T(128)S(1)} %bitcast.21, s32[8]{0:T(128)S(1)} %iota.4), dimensions={0}, to_apply=%region_0.0 | sort | flops 24 | bytes 128 | tf_op jit(solution)/shard_map/jit(argsort)/sort | solution.py:15
  43.7 0.1 broadcast_in_dim.16
  43.8 0.1 broadcast_in_dim.17
  43.9 7.8 %all-to-all-done = bf16[4,2,16384]{2,1,0:T(2,128)(2,1)S(1)} async-done(((bf16[4,2,16384]{2,1,0:T(2,128)(2,1)}), bf16[4,2,16384]{2,1,0:T(2,128)(2,1)S(1)}, u32[]{:S(2)}, u32[]{:S(2)}) %all-to-all-start) | async-done | bytes 262176 | tf_op jit(solution)/shard_map/all_to_all | solution.py:9
  51.6 1.0 %reshape.30 = bf16[4096,1,32]{2,1,0:T(2,128)(2,1)S(1)} reshape(bf16[4,2,16384]{2,1,0:T(2,128)(2,1)S(1)} %all-to-all-done) | data formatting | bytes 524288
  52.7 2.1 %copy.11 = bf16[1,32,4096]{2,1,0:T(8,128)(2,1)S(1)} copy(bf16[1,32,4096]{1,0,2:T(2,128)(2,1)S(1)} %bitcast.15) | data formatting | bytes 524288 | tf_op jit(solution)/shard_map/all_to_all | solution.py:9
  54.8 0.2 all_to_all.12
  54.9 0.0 copy-start
  55.0 0.1 copy.12
  55.0 0.0 all-gather.2.cloned.1.call-done
  55.1 1.7 %fusion = f32[128,8,64]{0,2,1:T(8,128)S(1)} fusion(bf16[128,1024,1]{1,0,2:T(8,128)(2,1)S(1)} %bitcast.19, bf16[8,64,1024]{2,1,0:T(8,128)(2,1)} %bitcast.17), kind=kOutput, calls=%fused_computation.5 | convolution fusion | flops 134217728 | bytes 1572864 | tf_op jit(solution)/shard_map/dot_general | solution.py:16
  56.7 0.6 gather_fusion
  57.3 0.8 bitcast_select_fusion
  58.1 0.0 reduce-scatter.2.cloned.1.call-update
  58.2 18.9 %reduce-scatter.2.cloned.1.call-done = f32[128,128]{0,1:T(8,128)} async-done(((f32[128,512]{0,1:T(8,128)}), f32[128,128]{0,1:T(8,128)}) %reduce-scatter.2.cloned.1.call-update) | async-done | bytes 65552 | tf_op jit(solution)/shard_map/reduce_scatter | solution.py:25
  77.0 0.9 %copy.13 = f32[128,128]{1,0:T(8,128)S(1)} copy(f32[128,128]{0,1:T(8,128)} %reduce-scatter.2.cloned.1.call-done) | data formatting | bytes 131072 | tf_op jit(solution)/shard_map/reduce_scatter | solution.py:25
  78.0 0.0 copy-done
  78.0 0.6 add.10
  (4 shorter events, 0.0 us)
Async XLA Ops:
  6.5 48.5 %all-gather.2.cloned.1.call-start = ((), (), s32[]{:S(2)}) async-start(), calls=%async_computation.2 | async-start | bytes 1179648 | tf_op jit(solution)/shard_map/all_gather | solution.py:18
  12.3 30.4 %copy-start.1 = (s32[1,8]{1,0:T(1,128)S(1)}, s32[1,8]{1,0:T(1,128)}, u32[]{:S(2)}) copy-start(s32[1,8]{1,0:T(1,128)} %param.6) | copy-start | bytes 100
  36.4 15.2 %all-to-all-start = ((bf16[4,2,16384]{2,1,0:T(2,128)(2,1)}), bf16[4,2,16384]{2,1,0:T(2,128)(2,1)S(1)}, u32[]{:S(2)}, u32[]{:S(2)}) async-start(bf16[4,2,16384]{2,1,0:T(2,128)(2,1)} %reshape.29), calls=%async_computation | async-start | bytes 524288 | tf_op jit(solution)/shard_map/all_to_all | solution.py:9
  42.7 34.3 %reduce-scatter.2.cloned.1.call-start = ((), (), s32[]{:S(2)}) async-start(), calls=%async_computation.3 | async-start | bytes 327680 | tf_op jit(solution)/shard_map/reduce_scatter | solution.py:25
  54.9 23.0 %copy-start = (f32[4,32,128]{2,1,0:T(8,128)S(1)}, f32[4,32,128]{2,1,0:T(8,128)}, u32[]{:S(2)}) copy-start(f32[4,32,128]{2,1,0:T(8,128)} %param.7) | copy-start | bytes 196612
Sparse Core Ops, SparseCore 0:
  9.2 26.1 all-gather.1
  58.3 18.7 reduce-scatter.1
where the time goes:
time: 86 us; the launch traced here: 85.5 us
  waiting for transfers between devices  27.4 us (32%)
  other arithmetic  24.9 us (29%)
  between operations  13.5 us (16%)
  local copies, waits for them, and re-layouts  11.7 us (14%)
  starting transfers between devices  6.32 us (7%)
  matrix products  1.66 us (2%)
    unnamed x1, other arithmetic  22.4 us
    reduce_scatter x1, waiting for transfers between devices, shards(): summed = lax.psum_scatter(ordered, 'row', scatter_dimension=1, tiled=True)  18.9 us
    all_to_all x1, waiting for transfers between devices, shards(): lax.all_to_all(amplitudes, 'row', split_axis=2, concat_axis=0, tiled=True)  7.76 us
    unnamed x8, local copies, waits for them, and re-layouts  7.75 us
    all_to_all x1, starting transfers between devices, shards(): lax.all_to_all(amplitudes, 'row', split_axis=2, concat_axis=0, tiled=True)  6.32 us
    all_to_all x3, local copies, waits for them, and re-layouts, shards(): lax.all_to_all(amplitudes, 'row', split_axis=2, concat_axis=0, tiled=True)  2.34 us
  transfers between devices with their start and end apart: 3, of which 2 were waited for; matrix products, arithmetic and copies ran while one was open for 39% of the time, Pallas kernels for 0%

commit v1 on v0

v1 whole, which is shorter than its diff:
```python
import functools
import math

import jax
import jax.numpy as jnp
from jax import lax
from jax.experimental import pallas as pl
from jax.experimental.pallas import tpu as pltpu
from jax.sharding import PartitionSpec as P

VMEM = pl.BlockSpec(memory_space=pltpu.VMEM)
ANY = pl.BlockSpec(memory_space=pl.ANY)
SMEM = pl.BlockSpec(memory_space=pltpu.SMEM)


def exchange(value, axis, step):
    n = lax.axis_size(axis)
    return lax.ppermute(value, axis, [(i, i ^ step) for i in range(n)])


def split_kernel(amp_ref, *outs):
    width = outs[0].shape[-1]
    row = lax.axis_index("row")
    for step, out in enumerate(outs):
        at = pl.multiple_of((row ^ step) * width, width)
        out[...] = amp_ref[0, :, pl.ds(at, width)]


def call(kernel, outs, specs, args, scratch=()):
    held = [*outs, *args, *(s for s in scratch if s.dtype in (jnp.float32, jnp.bfloat16))]
    size = sum(math.prod(x.shape) * jnp.dtype(x.dtype).itemsize for x in held)
    return pl.pallas_call(
        kernel, out_shape=outs, in_specs=specs, out_specs=[VMEM] * len(outs), scratch_shapes=scratch,
        compiler_params=pltpu.CompilerParams(vmem_limit_bytes=size + (2 << 20)),
    )(*args)


def split_amplitudes(amplitudes, rows):
    _, pairs, kw = amplitudes.shape
    block = jax.ShapeDtypeStruct((pairs, kw // rows), amplitudes.dtype)
    return call(split_kernel, [block] * rows, [VMEM], [amplitudes])


def assemble_kernel(steps, *refs):
    rows = len(steps)
    amps, panels, (lhs, near) = refs[:rows], refs[rows:-2], refs[-2:]
    pairs, height = amps[0].shape[0], panels[0].shape[0]
    row = lax.axis_index("row")
    for step, amp in zip(steps, amps):
        at = pl.multiple_of((row ^ step) * pairs, pairs)
        lhs[pl.ds(at, pairs), :] = amp[...]
    for index, panel in enumerate(panels):
        near[index * height:(index + 1) * height, :] = panel[...]


def assemble(steps, amps, panels):
    outs = [jax.ShapeDtypeStruct((len(blocks) * blocks[0].shape[0], blocks[0].shape[1]), blocks[0].dtype)
            for blocks in (amps, panels)]
    args = [*amps, *panels]
    return call(functools.partial(assemble_kernel, steps), outs, [VMEM] * len(args), args)


def contract_kernel(steps, owner_ref, residual_ref, lhs, near, far, *refs):
    outs, (weights, residual, sem) = refs[:len(steps)], refs[len(steps):]
    fetch = pltpu.make_async_copy(residual_ref, residual, sem)
    fetch.start()
    width = outs[0].shape[1]
    row, col = lax.axis_index("row"), lax.axis_index("col")
    columns = owner_ref.shape[1]
    height = weights.shape[0] // columns
    per_row = width // height
    for step in range(columns):
        owner = owner_ref[0, col ^ step]
        place = ((owner // per_row) ^ row) * per_row + owner % per_row
        at = pl.multiple_of(place * height, height)
        held, index = (near, far)[step % 2], step // 2
        weights[pl.ds(at, height), :] = held[index * height:(index + 1) * height, :]
    for step, out in zip(steps, outs):
        part = lax.dot_general(
            lhs[...], weights[step * width:(step + 1) * width, :],
            (((1,), (1,)), ((), ())), preferred_element_type=jnp.float32)
        if step == 0:
            fetch.wait()
            part = part + residual[...].reshape(part.shape)
        out[...] = part


def contract(steps, owner, residual, lhs, near, far):
    rows, ab, depth = len(steps), 2 * near.shape[0], near.shape[1]
    part = jax.ShapeDtypeStruct((lhs.shape[0], ab // rows), jnp.float32)
    return call(
        functools.partial(contract_kernel, steps), [part] * rows, [SMEM, ANY, VMEM, VMEM, VMEM],
        [owner, residual, lhs, near, far],
        [pltpu.VMEM((ab, depth), jnp.bfloat16), pltpu.VMEM(residual.shape, jnp.float32), pltpu.SemaphoreType.DMA],
    )


def shards(amplitudes, integrals, panel_owner, residual_in):
    rows, columns = lax.axis_size("row"), lax.axis_size("col")
    steps = tuple(range(rows - 1, -1, -1))
    panels = [exchange(integrals, "col", step) if step else integrals for step in range(0, columns, 2)]
    blocks = split_amplitudes(amplitudes, rows)
    amps = [exchange(blocks[step], "row", step) if step else blocks[0] for step in steps]
    lhs, near = assemble(steps, amps, panels)
    parts = contract(steps, panel_owner, residual_in, lhs, near, exchange(near, "col", 1))
    total = parts[-1]
    for step, part in zip(steps[:-1], parts):
        total = total + exchange(part, "row", step)
    return total.reshape(residual_in.shape)


def solution(mesh):
    placed = (P("row", "col", None), P("col", "row"), P("row", None), P(None, "col", "row"))
    return jax.shard_map(
        shards, mesh=mesh, in_specs=placed, out_specs=P(None, "col", "row"), check_vma=False
    )
```

time: 86 us -> 28.4 us (0.33)
  other arithmetic: 24.9 us -> 0.65 us
  waiting for transfers between devices: 27.4 us -> 10.6 us
  between operations: 13.5 us -> 0.05 us
  local copies, waits for them, and re-layouts: 11.7 us -> 0.96 us
  starting transfers between devices: 6.32 us -> 14.5 us
  matrix products: 1.66 us -> 0 us
  Pallas kernels: 0 us -> 1.53 us
    unnamed x1 -> x0, other arithmetic: 22.4 us -> none
    reduce_scatter x1 -> x0, waiting for transfers between devices: 18.9 us -> none  [shards(): summed = lax.psum_scatter(ordered, 'row', scatter_dimension=1, tiled=True)]
    ppermute x0 -> x10, starting transfers between devices: none -> 14.5 us  [exchange(): return lax.ppermute(value, axis, [(i, i ^ step) for i in range(n)])]
    ppermute x0 -> x10, waiting for transfers between devices: none -> 10.6 us  [exchange(): return lax.ppermute(value, axis, [(i, i ^ step) for i in range(n)])]
    all_to_all x1 -> x0, waiting for transfers between devices: 7.76 us -> none  [shards(): lax.all_to_all(amplitudes, 'row', split_axis=2, concat_axis=0, tiled=True)]
    unnamed x8, local copies, waits for them, and re-layouts: 7.75 us -> 0.96 us
    all_to_all x1 -> x0, starting transfers between devices: 6.32 us -> none  [shards(): lax.all_to_all(amplitudes, 'row', split_axis=2, concat_axis=0, tiled=True)]
    all_to_all x3 -> x0, local copies, waits for them, and re-layouts: 2.34 us -> none  [shards(): lax.all_to_all(amplitudes, 'row', split_axis=2, concat_axis=0, tiled=True)]
  transfers between devices with their start and end apart: 3 -> 10, of which waited for: 2 -> 5; matrix products, arithmetic and copies ran while one was open for 39% -> 0% of each run, Pallas kernels for 0% -> 0%
where the time goes in v1:
time: 28.4 us; the launch traced here: 28.3 us
  starting transfers between devices  14.5 us (51%)
  waiting for transfers between devices  10.6 us (37%)
  Pallas kernels  1.53 us (5%)
  local copies, waits for them, and re-layouts  0.96 us (3%)
  other arithmetic  0.65 us (2%)
    ppermute x10, starting transfers between devices, exchange(): return lax.ppermute(value, axis, [(i, i ^ step) for i in range(n)])  14.5 us
    ppermute x10, waiting for transfers between devices, exchange(): return lax.ppermute(value, axis, [(i, i ^ step) for i in range(n)])  10.6 us
    pallas_call x3, Pallas kernels, call(): pl.pallas_call(kernel, out_shape=outs, in_specs=specs, out_specs=[VMEM] *...  1.53 us
    unnamed x8, local copies, waits for them, and re-layouts  0.96 us
    add x1, other arithmetic, shards(): total = total + exchange(part, 'row', step)  0.65 us
  transfers between devices with their start and end apart: 10, of which 5 were waited for; matrix products, arithmetic and copies ran while one was open for 0% of the time, Pallas kernels for 0%

profile of v1, /device:TPU:0, one launch (start us, length us, event | category | flops | bytes accessed | tf_op | source)
XLA Modules:
  0.0 28.3 jit_solution(11391316451257673397)
XLA Ops:
  0.0 0.0 copy-start
  0.0 0.9 %copy-done = bf16[1,32,4096]{2,1,0:T(8,128)(2,1)S(1)} copy-done((bf16[1,32,4096]{2,1,0:T(8,128)(2,1)S(1)}, bf16[1,32,4096]{2,1,0:T(8,128)(2,1)}, u32[]{:S(2)}) %copy-start) | copy-done | bytes 262168
  1.0 0.0 copy-start.1
  1.0 5.1 %collective-permute-start = (bf16[32,1024]{1,0:T(8,128)(2,1)S(1)}, bf16[32,1024]{1,0:T(8,128)(2,1)S(1)}, u32[]{:S(2)}, u32[]{:S(2)}) collective-permute-start(bf16[32,1024]{1,0:T(8,128)(2,1)S(1)} %get-tuple-element.15), channel_id=1, source_target_pairs={{0,24},{8,16},{16,8},{24,0},{1,25},{9,17},{17,9},{25,1},{2,26},{10... | collective-permute-start | bytes 196616 | tf_op jit(solution)/shard_map/ppermute | solution.py:18
  6.1 0.0 copy-done.1
  6.1 1.5 %collective-permute-start.4 = (bf16[64,1024]{1,0:T(8,128)(2,1)S(1)}, bf16[64,1024]{1,0:T(8,128)(2,1)S(1)}, u32[]{:S(2)}, u32[]{:S(2)}) collective-permute-start(bf16[64,1024]{1,0:T(8,128)(2,1)S(1)} %copy-done.1), channel_id=1, source_target_pairs={{0,4},{1,5},{2,6},{3,7},{4,0},{5,1},{6,2},{7,3},{8,12},{9,13},{10,... | collective-permute-start | bytes 393224 | tf_op jit(solution)/shard_map/ppermute | solution.py:18
  7.6 1.5 %collective-permute-start.3 = (bf16[64,1024]{1,0:T(8,128)(2,1)S(1)}, bf16[64,1024]{1,0:T(8,128)(2,1)S(1)}, u32[]{:S(2)}, u32[]{:S(2)}) collective-permute-start(bf16[64,1024]{1,0:T(8,128)(2,1)S(1)} %copy-done.1), channel_id=1, source_target_pairs={{0,2},{1,3},{2,0},{3,1},{4,6},{5,7},{6,4},{7,5},{8,10},{9,11},{10,... | collective-permute-start | bytes 393224 | tf_op jit(solution)/shard_map/ppermute | solution.py:18
  9.1 0.5 %collective-permute-start.5 = (bf16[64,1024]{1,0:T(8,128)(2,1)S(1)}, bf16[64,1024]{1,0:T(8,128)(2,1)S(1)}, u32[]{:S(2)}, u32[]{:S(2)}) collective-permute-start(bf16[64,1024]{1,0:T(8,128)(2,1)S(1)} %copy-done.1), channel_id=1, source_target_pairs={{0,6},{1,7},{2,4},{3,5},{4,2},{5,3},{6,0},{7,1},{8,14},{9,15},{10,... | collective-permute-start | bytes 393224 | tf_op jit(solution)/shard_map/ppermute | solution.py:18
  9.6 0.0 collective-permute-start.1
  9.6 0.0 collective-permute-done.refs_0_
  9.6 1.4 %collective-permute-start.2 = (bf16[32,1024]{1,0:T(8,128)(2,1)S(1)}, bf16[32,1024]{1,0:T(8,128)(2,1)S(1)}, u32[]{:S(2)}, u32[]{:S(2)}) collective-permute-start(bf16[32,1024]{1,0:T(8,128)(2,1)S(1)} %get-tuple-element.17), channel_id=1, source_target_pairs={{0,8},{8,0},{16,24},{24,16},{1,9},{9,1},{17,25},{25,17},{2,10},{10... | collective-permute-start | bytes 196616 | tf_op jit(solution)/shard_map/ppermute | solution.py:18
  11.0 4.0 %collective-permute-done.1.refs_1_ = bf16[32,1024]{1,0:T(8,128)(2,1)S(1)} collective-permute-done((bf16[32,1024]{1,0:T(8,128)(2,1)S(1)}, bf16[32,1024]{1,0:T(8,128)(2,1)S(1)}, u32[]{:S(2)}, u32[]{:S(2)}) %collective-permute-start.1) | collective-permute-done | bytes 65568 | tf_op jit(solution)/shard_map/ppermute | solution.py:18
  14.9 0.0 collective-permute-done.2.refs_2_
  14.9 0.0 collective-permute-done.4.refs_6_
  14.9 0.0 collective-permute-done.3.refs_5_
  15.0 0.4 %collective-permute-done.5.refs_7_ = bf16[64,1024]{1,0:T(8,128)(2,1)S(1)} collective-permute-done((bf16[64,1024]{1,0:T(8,128)(2,1)S(1)}, bf16[64,1024]{1,0:T(8,128)(2,1)S(1)}, u32[]{:S(2)}, u32[]{:S(2)}) %collective-permute-start.5) | collective-permute-done | bytes 131104 | tf_op jit(solution)/shard_map/ppermute | solution.py:18
  15.3 0.0 copy-start.2
  15.3 0.1 shard_map.47
  15.4 0.0 copy-start.3
  15.4 0.1 collective-permute-start.6
  15.5 1.9 %collective-permute-done.6.far = bf16[256,1024]{1,0:T(8,128)(2,1)S(1)} collective-permute-done((bf16[256,1024]{1,0:T(8,128)(2,1)S(1)}, bf16[256,1024]{1,0:T(8,128)(2,1)S(1)}, u32[]{:S(2)}, u32[]{:S(2)}) %collective-permute-start.6) | collective-permute-done | bytes 524320 | tf_op jit(solution)/shard_map/ppermute | solution.py:18
  17.4 0.0 copy-done.2
  17.4 0.0 copy-done.3
  17.4 1.5 %shard_map.48 = (f32[128,128]{1,0:T(8,128)S(1)}, f32[128,128]{1,0:T(8,128)S(1)}, f32[128,128]{1,0:T(8,128)S(1)}, f32[128,128]{1,0:T(8,128)S(1)}) custom-call(s32[1,8]{1,0:T(1,128)S(1)} %copy-done.3, f32[4,32,128]{2,1,0:T(8,128)S(1)} %copy-done.2, bf16[128,1024]{1,0:T(8,128)(2,1)S(1)} %get-tuple-element.19.lhs, bf16[256,1024]{1,0:T(8,128)(2,1)S(1)} %get-tuple-element.20.near, ...), custom_call_target="tpu_custom_call" | custom-call | tf_op jit(solution)/shard_map/pallas_call | solution.py:32
  18.9 1.7 %collective-permute-start.7 = (f32[128,128]{1,0:T(8,128)S(1)}, f32[128,128]{1,0:T(8,128)S(1)}, u32[]{:S(2)}, u32[]{:S(2)}) collective-permute-start(f32[128,128]{1,0:T(8,128)S(1)} %get-tuple-element.22), channel_id=1, source_target_pairs={{0,24},{8,16},{16,8},{24,0},{1,25},{9,17},{17,9},{25,1},{2,26},{10... | collective-permute-start | bytes 196616 | tf_op jit(solution)/shard_map/ppermute | solution.py:18
  20.5 0.0 collective-permute-start.8
  20.5 2.8 %collective-permute-start.9 = (f32[128,128]{1,0:T(8,128)S(1)}, f32[128,128]{1,0:T(8,128)S(1)}, u32[]{:S(2)}, u32[]{:S(2)}) collective-permute-start(f32[128,128]{1,0:T(8,128)S(1)} %get-tuple-element.24), channel_id=1, source_target_pairs={{0,8},{8,0},{16,24},{24,16},{1,9},{9,1},{17,25},{25,17},{2,10},{10... | collective-permute-start | bytes 196616 | tf_op jit(solution)/shard_map/ppermute | solution.py:18
  23.3 2.4 %collective-permute-done.7 = f32[128,128]{1,0:T(8,128)S(1)} collective-permute-done((f32[128,128]{1,0:T(8,128)S(1)}, f32[128,128]{1,0:T(8,128)S(1)}, u32[]{:S(2)}, u32[]{:S(2)}) %collective-permute-start.7) | collective-permute-done | bytes 65568 | tf_op jit(solution)/shard_map/ppermute | solution.py:18
  25.7 2.0 %collective-permute-done.8 = f32[128,128]{1,0:T(8,128)S(1)} collective-permute-done((f32[128,128]{1,0:T(8,128)S(1)}, f32[128,128]{1,0:T(8,128)S(1)}, u32[]{:S(2)}, u32[]{:S(2)}) %collective-permute-start.8) | collective-permute-done | bytes 65568 | tf_op jit(solution)/shard_map/ppermute | solution.py:18
  27.7 0.0 collective-permute-done.9
  27.7 0.6 %add_add_fusion = f32[128,128]{1,0:T(8,128)} fusion(f32[128,128]{1,0:T(8,128)S(1)} %collective-permute-done.9, f32[128,128]{1,0:T(8,128)S(1)} %collective-permute-done.8, f32[128,128]{1,0:T(8,128)S(1)} %get-tuple-element.21, f32[128,128]{1,0:T(8,128)S(1)} %collective-permute-done.7), kind=kLoop, calls=%fused_computation | loop fusion | flops 49152 | bytes 327680 | tf_op jit(solution)/shard_map/add | solution.py:108
  (1 shorter events, 0.0 us)
Async XLA Ops:
  0.0 0.9 %copy-start = (bf16[1,32,4096]{2,1,0:T(8,128)(2,1)S(1)}, bf16[1,32,4096]{2,1,0:T(8,128)(2,1)}, u32[]{:S(2)}) copy-start(bf16[1,32,4096]{2,1,0:T(8,128)(2,1)} %amp_ref.1) | copy-start | bytes 786436
  1.0 5.1 %copy-start.1 = (bf16[64,1024]{1,0:T(8,128)(2,1)S(1)}, bf16[64,1024]{1,0:T(8,128)(2,1)}, u32[]{:S(2)}) copy-start(bf16[64,1024]{1,0:T(8,128)(2,1)} %refs_4_.1) | copy-start | bytes 393220
  1.0 8.6 %collective-permute-start = (bf16[32,1024]{1,0:T(8,128)(2,1)S(1)}, bf16[32,1024]{1,0:T(8,128)(2,1)S(1)}, u32[]{:S(2)}, u32[]{:S(2)}) collective-permute-start(bf16[32,1024]{1,0:T(8,128)(2,1)S(1)} %get-tuple-element.15), channel_id=1, source_target_pairs={{0,24},{8,16},{16,8},{24,0},{1,25},{9,17},{17,9},{25,1},{2,26},{10... | collective-permute-start | bytes 196616 | tf_op jit(solution)/shard_map/ppermute | solution.py:18
  6.1 8.9 %collective-permute-start.4 = (bf16[64,1024]{1,0:T(8,128)(2,1)S(1)}, bf16[64,1024]{1,0:T(8,128)(2,1)S(1)}, u32[]{:S(2)}, u32[]{:S(2)}) collective-permute-start(bf16[64,1024]{1,0:T(8,128)(2,1)S(1)} %copy-done.1), channel_id=1, source_target_pairs={{0,4},{1,5},{2,6},{3,7},{4,0},{5,1},{6,2},{7,3},{8,12},{9,13},{10,... | collective-permute-start | bytes 393224 | tf_op jit(solution)/shard_map/ppermute | solution.py:18
  7.6 7.3 %collective-permute-start.3 = (bf16[64,1024]{1,0:T(8,128)(2,1)S(1)}, bf16[64,1024]{1,0:T(8,128)(2,1)S(1)}, u32[]{:S(2)}, u32[]{:S(2)}) collective-permute-start(bf16[64,1024]{1,0:T(8,128)(2,1)S(1)} %copy-done.1), channel_id=1, source_target_pairs={{0,2},{1,3},{2,0},{3,1},{4,6},{5,7},{6,4},{7,5},{8,10},{9,11},{10,... | collective-permute-start | bytes 393224 | tf_op jit(solution)/shard_map/ppermute | solution.py:18
  9.1 6.2 %collective-permute-start.5 = (bf16[64,1024]{1,0:T(8,128)(2,1)S(1)}, bf16[64,1024]{1,0:T(8,128)(2,1)S(1)}, u32[]{:S(2)}, u32[]{:S(2)}) collective-permute-start(bf16[64,1024]{1,0:T(8,128)(2,1)S(1)} %copy-done.1), channel_id=1, source_target_pairs={{0,6},{1,7},{2,4},{3,5},{4,2},{5,3},{6,0},{7,1},{8,14},{9,15},{10,... | collective-permute-start | bytes 393224 | tf_op jit(solution)/shard_map/ppermute | solution.py:18
  9.6 5.4 %collective-permute-start.1 = (bf16[32,1024]{1,0:T(8,128)(2,1)S(1)}, bf16[32,1024]{1,0:T(8,128)(2,1)S(1)}, u32[]{:S(2)}, u32[]{:S(2)}) collective-permute-start(bf16[32,1024]{1,0:T(8,128)(2,1)S(1)} %get-tuple-element.16), channel_id=1, source_target_pairs={{0,16},{8,24},{16,0},{24,8},{1,17},{9,25},{17,1},{25,9},{2,18},{10... | collective-permute-start | bytes 196616 | tf_op jit(solution)/shard_map/ppermute | solution.py:18
  9.6 5.4 %collective-permute-start.2 = (bf16[32,1024]{1,0:T(8,128)(2,1)S(1)}, bf16[32,1024]{1,0:T(8,128)(2,1)S(1)}, u32[]{:S(2)}, u32[]{:S(2)}) collective-permute-start(bf16[32,1024]{1,0:T(8,128)(2,1)S(1)} %get-tuple-element.17), channel_id=1, source_target_pairs={{0,8},{8,0},{16,24},{24,16},{1,9},{9,1},{17,25},{25,17},{2,10},{10... | collective-permute-start | bytes 196616 | tf_op jit(solution)/shard_map/ppermute | solution.py:18
  15.3 2.1 %copy-start.2 = (f32[4,32,128]{2,1,0:T(8,128)S(1)}, f32[4,32,128]{2,1,0:T(8,128)}, u32[]{:S(2)}) copy-start(f32[4,32,128]{2,1,0:T(8,128)} %residual_ref.1) | copy-start | bytes 196612
  15.4 2.0 %copy-start.3 = (s32[1,8]{1,0:T(1,128)S(1)}, s32[1,8]{1,0:T(1,128)}, u32[]{:S(2)}) copy-start(s32[1,8]{1,0:T(1,128)} %owner_ref.1) | copy-start | bytes 100
  15.4 2.0 %collective-permute-start.6 = (bf16[256,1024]{1,0:T(8,128)(2,1)S(1)}, bf16[256,1024]{1,0:T(8,128)(2,1)S(1)}, u32[]{:S(2)}, u32[]{:S(2)}) collective-permute-start(bf16[256,1024]{1,0:T(8,128)(2,1)S(1)} %get-tuple-element.20.near), channel_id=1, source_target_pairs={{0,1},{1,0},{2,3},{3,2},{4,5},{5,4},{6,7},{7,6},{8,9},{9,8},{10,11... | collective-permute-start | bytes 1572872 | tf_op jit(solution)/shard_map/ppermute | solution.py:18
  18.9 6.8 %collective-permute-start.7 = (f32[128,128]{1,0:T(8,128)S(1)}, f32[128,128]{1,0:T(8,128)S(1)}, u32[]{:S(2)}, u32[]{:S(2)}) collective-permute-start(f32[128,128]{1,0:T(8,128)S(1)} %get-tuple-element.22), channel_id=1, source_target_pairs={{0,24},{8,16},{16,8},{24,0},{1,25},{9,17},{17,9},{25,1},{2,26},{10... | collective-permute-start | bytes 196616 | tf_op jit(solution)/shard_map/ppermute | solution.py:18
  20.5 7.1 %collective-permute-start.8 = (f32[128,128]{1,0:T(8,128)S(1)}, f32[128,128]{1,0:T(8,128)S(1)}, u32[]{:S(2)}, u32[]{:S(2)}) collective-permute-start(f32[128,128]{1,0:T(8,128)S(1)} %get-tuple-element.23), channel_id=1, source_target_pairs={{0,16},{8,24},{16,0},{24,8},{1,17},{9,25},{17,1},{25,9},{2,18},{10... | collective-permute-start | bytes 196616 | tf_op jit(solution)/shard_map/ppermute | solution.py:18
  20.5 7.1 %collective-permute-start.9 = (f32[128,128]{1,0:T(8,128)S(1)}, f32[128,128]{1,0:T(8,128)S(1)}, u32[]{:S(2)}, u32[]{:S(2)}) collective-permute-start(f32[128,128]{1,0:T(8,128)S(1)} %get-tuple-element.24), channel_id=1, source_target_pairs={{0,8},{8,0},{16,24},{24,16},{1,9},{9,1},{17,25},{25,17},{2,10},{10... | collective-permute-start | bytes 196616 | tf_op jit(solution)/shard_map/ppermute | solution.py:18

commit v2 on v1

--- a/solution.py
+++ b/solution.py
@@ -9,7 +9,6 @@
 from jax.sharding import PartitionSpec as P
 
 VMEM = pl.BlockSpec(memory_space=pltpu.VMEM)
-ANY = pl.BlockSpec(memory_space=pl.ANY)
 SMEM = pl.BlockSpec(memory_space=pltpu.SMEM)
 
 
@@ -27,7 +26,7 @@
 
 
 def call(kernel, outs, specs, args, scratch=()):
-    held = [*outs, *args, *(s for s in scratch if s.dtype in (jnp.float32, jnp.bfloat16))]
+    held = [*outs, *args, *scratch]
     size = sum(math.prod(x.shape) * jnp.dtype(x.dtype).itemsize for x in held)
     return pl.pallas_call(
         kernel, out_shape=outs, in_specs=specs, out_specs=[VMEM] * len(outs), scratch_shapes=scratch,
@@ -41,9 +40,9 @@
     return call(split_kernel, [block] * rows, [VMEM], [amplitudes])
 
 
-def assemble_kernel(steps, *refs):
+def assemble_kernel(steps, residual_ref, *refs):
     rows = len(steps)
-    amps, panels, (lhs, near) = refs[:rows], refs[rows:-2], refs[-2:]
+    panels, amps, (residual, near, lhs) = refs[:-rows - 3], refs[-rows - 3:-3], refs[-3:]
     pairs, height = amps[0].shape[0], panels[0].shape[0]
     row = lax.axis_index("row")
     for step, amp in zip(steps, amps):
@@ -51,19 +50,19 @@
         lhs[pl.ds(at, pairs), :] = amp[...]
     for index, panel in enumerate(panels):
         near[index * height:(index + 1) * height, :] = panel[...]
+    residual[...] = residual_ref[...]
 
 
-def assemble(steps, amps, panels):
+def assemble(steps, residual, panels, amps):
     outs = [jax.ShapeDtypeStruct((len(blocks) * blocks[0].shape[0], blocks[0].shape[1]), blocks[0].dtype)
-            for blocks in (amps, panels)]
-    args = [*amps, *panels]
+            for blocks in (panels, amps)]
+    outs = [jax.ShapeDtypeStruct(residual.shape, residual.dtype)] + outs
+    args = [residual, *panels, *amps]
     return call(functools.partial(assemble_kernel, steps), outs, [VMEM] * len(args), args)
 
 
 def contract_kernel(steps, owner_ref, residual_ref, lhs, near, far, *refs):
-    outs, (weights, residual, sem) = refs[:len(steps)], refs[len(steps):]
-    fetch = pltpu.make_async_copy(residual_ref, residual, sem)
-    fetch.start()
+    outs, weights = refs[:-1], refs[-1]
     width = outs[0].shape[1]
     row, col = lax.axis_index("row"), lax.axis_index("col")
     columns = owner_ref.shape[1]
@@ -80,8 +79,7 @@
             lhs[...], weights[step * width:(step + 1) * width, :],
             (((1,), (1,)), ((), ())), preferred_element_type=jnp.float32)
         if step == 0:
-            fetch.wait()
-            part = part + residual[...].reshape(part.shape)
+            part = part + residual_ref[...].reshape(part.shape)
         out[...] = part
 
 
@@ -89,9 +87,9 @@
     rows, ab, depth = len(steps), 2 * near.shape[0], near.shape[1]
     part = jax.ShapeDtypeStruct((lhs.shape[0], ab // rows), jnp.float32)
     return call(
-        functools.partial(contract_kernel, steps), [part] * rows, [SMEM, ANY, VMEM, VMEM, VMEM],
+        functools.partial(contract_kernel, steps), [part] * rows, [SMEM, VMEM, VMEM, VMEM, VMEM],
         [owner, residual, lhs, near, far],
-        [pltpu.VMEM((ab, depth), jnp.bfloat16), pltpu.VMEM(residual.shape, jnp.float32), pltpu.SemaphoreType.DMA],
+        [pltpu.VMEM((ab, depth), jnp.bfloat16)],
     )
 
 
@@ -101,8 +99,8 @@
     panels = [exchange(integrals, "col", step) if step else integrals for step in range(0, columns, 2)]
     blocks = split_amplitudes(amplitudes, rows)
     amps = [exchange(blocks[step], "row", step) if step else blocks[0] for step in steps]
-    lhs, near = assemble(steps, amps, panels)
-    parts = contract(steps, panel_owner, residual_in, lhs, near, exchange(near, "col", 1))
+    residual, near, lhs = assemble(steps, residual_in, panels, amps)
+    parts = contract(steps, panel_owner, residual, lhs, near, exchange(near, "col", 1))
     total = parts[-1]
     for step, part in zip(steps[:-1], parts):
         total = total + exchange(part, "row", step)

time: 28.4 us -> 28.7 us (1.011)
  local copies, waits for them, and re-layouts: 0.96 us -> 1.61 us
  Pallas kernels: 1.53 us -> 1.15 us
    unnamed x8, local copies, waits for them, and re-layouts: 0.96 us -> 1.61 us
    pallas_call x3, Pallas kernels: 1.53 us -> 1.15 us  [call(): pl.pallas_call(kernel, out_shape=outs, in_specs=specs, out_specs=[VMEM] *...]
where the time goes in v2:
time: 28.7 us; the launch traced here: 28.6 us
  starting transfers between devices  14.5 us (51%)
  waiting for transfers between devices  10.6 us (37%)
  local copies, waits for them, and re-layouts  1.61 us (6%)
  Pallas kernels  1.15 us (4%)
  other arithmetic  0.65 us (2%)
    ppermute x10, starting transfers between devices, exchange(): return lax.ppermute(value, axis, [(i, i ^ step) for i in range(n)])  14.5 us
    ppermute x10, waiting for transfers between devices, exchange(): return lax.ppermute(value, axis, [(i, i ^ step) for i in range(n)])  10.6 us
    unnamed x8, local copies, waits for them, and re-layouts  1.61 us
    pallas_call x3, Pallas kernels, call(): pl.pallas_call(kernel, out_shape=outs, in_specs=specs, out_specs=[VMEM] *...  1.15 us
    add x1, other arithmetic, shards(): total = total + exchange(part, 'row', step)  0.65 us
  transfers between devices with their start and end apart: 10, of which 5 were waited for; matrix products, arithmetic and copies ran while one was open for 0% of the time, Pallas kernels for 0%

profile of v2, /device:TPU:0, one launch (start us, length us, event | category | flops | bytes accessed | tf_op | source)
XLA Modules:
  0.0 28.6 jit_solution(10991924476568805887)
XLA Ops:
  0.0 0.0 copy-start
  0.0 0.9 %copy-done = bf16[1,32,4096]{2,1,0:T(8,128)(2,1)S(1)} copy-done((bf16[1,32,4096]{2,1,0:T(8,128)(2,1)S(1)}, bf16[1,32,4096]{2,1,0:T(8,128)(2,1)}, u32[]{:S(2)}) %copy-start) | copy-done | bytes 262168
  1.0 0.0 copy-start.1
  1.0 0.0 copy-start.2
  1.0 5.1 %collective-permute-start.3 = (bf16[32,1024]{1,0:T(8,128)(2,1)S(1)}, bf16[32,1024]{1,0:T(8,128)(2,1)S(1)}, u32[]{:S(2)}, u32[]{:S(2)}) collective-permute-start(bf16[32,1024]{1,0:T(8,128)(2,1)S(1)} %get-tuple-element.16), channel_id=1, source_target_pairs={{0,24},{8,16},{16,8},{24,0},{1,25},{9,17},{17,9},{25,1},{2,26},{10... | collective-permute-start | bytes 196616 | tf_op jit(solution)/shard_map/ppermute | solution.py:17
  6.1 0.0 copy-done.1
  6.1 1.5 %collective-permute-start.1 = (bf16[64,1024]{1,0:T(8,128)(2,1)S(1)}, bf16[64,1024]{1,0:T(8,128)(2,1)S(1)}, u32[]{:S(2)}, u32[]{:S(2)}) collective-permute-start(bf16[64,1024]{1,0:T(8,128)(2,1)S(1)} %copy-done.1), channel_id=1, source_target_pairs={{0,4},{1,5},{2,6},{3,7},{4,0},{5,1},{6,2},{7,3},{8,12},{9,13},{10,... | collective-permute-start | bytes 393224 | tf_op jit(solution)/shard_map/ppermute | solution.py:17
  7.6 1.5 %collective-permute-start = (bf16[64,1024]{1,0:T(8,128)(2,1)S(1)}, bf16[64,1024]{1,0:T(8,128)(2,1)S(1)}, u32[]{:S(2)}, u32[]{:S(2)}) collective-permute-start(bf16[64,1024]{1,0:T(8,128)(2,1)S(1)} %copy-done.1), channel_id=1, source_target_pairs={{0,2},{1,3},{2,0},{3,1},{4,6},{5,7},{6,4},{7,5},{8,10},{9,11},{10,... | collective-permute-start | bytes 393224 | tf_op jit(solution)/shard_map/ppermute | solution.py:17
  9.1 0.5 %collective-permute-start.2 = (bf16[64,1024]{1,0:T(8,128)(2,1)S(1)}, bf16[64,1024]{1,0:T(8,128)(2,1)S(1)}, u32[]{:S(2)}, u32[]{:S(2)}) collective-permute-start(bf16[64,1024]{1,0:T(8,128)(2,1)S(1)} %copy-done.1), channel_id=1, source_target_pairs={{0,6},{1,7},{2,4},{3,5},{4,2},{5,3},{6,0},{7,1},{8,14},{9,15},{10,... | collective-permute-start | bytes 393224 | tf_op jit(solution)/shard_map/ppermute | solution.py:17
  9.6 0.0 collective-permute-start.4
  9.6 0.0 collective-permute-done.3.refs_4_
  9.6 1.4 %collective-permute-start.5 = (bf16[32,1024]{1,0:T(8,128)(2,1)S(1)}, bf16[32,1024]{1,0:T(8,128)(2,1)S(1)}, u32[]{:S(2)}, u32[]{:S(2)}) collective-permute-start(bf16[32,1024]{1,0:T(8,128)(2,1)S(1)} %get-tuple-element.18), channel_id=1, source_target_pairs={{0,8},{8,0},{16,24},{24,16},{1,9},{9,1},{17,25},{25,17},{2,10},{10... | collective-permute-start | bytes 196616 | tf_op jit(solution)/shard_map/ppermute | solution.py:17
  11.0 4.0 %collective-permute-done.4.refs_5_ = bf16[32,1024]{1,0:T(8,128)(2,1)S(1)} collective-permute-done((bf16[32,1024]{1,0:T(8,128)(2,1)S(1)}, bf16[32,1024]{1,0:T(8,128)(2,1)S(1)}, u32[]{:S(2)}, u32[]{:S(2)}) %collective-permute-start.4) | collective-permute-done | bytes 65568 | tf_op jit(solution)/shard_map/ppermute | solution.py:17
  14.9 0.0 collective-permute-done.5.refs_6_
  14.9 0.0 collective-permute-done.1.refs_2_
  15.0 0.0 collective-permute-done.refs_1_
  15.0 0.4 %collective-permute-done.2.refs_3_ = bf16[64,1024]{1,0:T(8,128)(2,1)S(1)} collective-permute-done((bf16[64,1024]{1,0:T(8,128)(2,1)S(1)}, bf16[64,1024]{1,0:T(8,128)(2,1)S(1)}, u32[]{:S(2)}, u32[]{:S(2)}) %collective-permute-start.2) | collective-permute-done | bytes 131104 | tf_op jit(solution)/shard_map/ppermute | solution.py:17
  15.3 0.0 copy-done.2
  15.3 0.1 shard_map.47
  15.4 0.1 collective-permute-start.6
  15.5 1.9 %collective-permute-done.6.far = bf16[256,1024]{1,0:T(8,128)(2,1)S(1)} collective-permute-done((bf16[256,1024]{1,0:T(8,128)(2,1)S(1)}, bf16[256,1024]{1,0:T(8,128)(2,1)S(1)}, u32[]{:S(2)}, u32[]{:S(2)}) %collective-permute-start.6) | collective-permute-done | bytes 524320 | tf_op jit(solution)/shard_map/ppermute | solution.py:17
  17.4 0.0 copy-start.3
  17.4 0.7 %copy-done.3 = s32[1,8]{1,0:T(1,128)S(1)} copy-done((s32[1,8]{1,0:T(1,128)S(1)}, s32[1,8]{1,0:T(1,128)}, u32[]{:S(2)}) %copy-start.3) | copy-done | bytes 56
  18.0 1.1 %shard_map.48 = (f32[128,128]{1,0:T(8,128)S(1)}, f32[128,128]{1,0:T(8,128)S(1)}, f32[128,128]{1,0:T(8,128)S(1)}, f32[128,128]{1,0:T(8,128)S(1)}) custom-call(s32[1,8]{1,0:T(1,128)S(1)} %copy-done.3, f32[4,32,128]{2,1,0:T(8,128)S(1)} %get-tuple-element.20.residual_ref, bf16[128,1024]{1,0:T(8,128)(2,1)S(1)} %get-tuple-element.21.lhs, ...), custom_call_target="tpu_custom_call" | custom-call | tf_op jit(solution)/shard_map/pallas_call | solution.py:31
  19.1 1.7 %collective-permute-start.7 = (f32[128,128]{1,0:T(8,128)S(1)}, f32[128,128]{1,0:T(8,128)S(1)}, u32[]{:S(2)}, u32[]{:S(2)}) collective-permute-start(f32[128,128]{1,0:T(8,128)S(1)} %get-tuple-element.24), channel_id=1, source_target_pairs={{0,24},{8,16},{16,8},{24,0},{1,25},{9,17},{17,9},{25,1},{2,26},{10... | collective-permute-start | bytes 196616 | tf_op jit(solution)/shard_map/ppermute | solution.py:17
  20.8 0.0 collective-permute-start.8
  20.8 2.8 %collective-permute-start.9 = (f32[128,128]{1,0:T(8,128)S(1)}, f32[128,128]{1,0:T(8,128)S(1)}, u32[]{:S(2)}, u32[]{:S(2)}) collective-permute-start(f32[128,128]{1,0:T(8,128)S(1)} %get-tuple-element.26), channel_id=1, source_target_pairs={{0,8},{8,0},{16,24},{24,16},{1,9},{9,1},{17,25},{25,17},{2,10},{10... | collective-permute-start | bytes 196616 | tf_op jit(solution)/shard_map/ppermute | solution.py:17
  23.6 2.4 %collective-permute-done.7 = f32[128,128]{1,0:T(8,128)S(1)} collective-permute-done((f32[128,128]{1,0:T(8,128)S(1)}, f32[128,128]{1,0:T(8,128)S(1)}, u32[]{:S(2)}, u32[]{:S(2)}) %collective-permute-start.7) | collective-permute-done | bytes 65568 | tf_op jit(solution)/shard_map/ppermute | solution.py:17
  25.9 2.0 %collective-permute-done.8 = f32[128,128]{1,0:T(8,128)S(1)} collective-permute-done((f32[128,128]{1,0:T(8,128)S(1)}, f32[128,128]{1,0:T(8,128)S(1)}, u32[]{:S(2)}, u32[]{:S(2)}) %collective-permute-start.8) | collective-permute-done | bytes 65568 | tf_op jit(solution)/shard_map/ppermute | solution.py:17
  27.9 0.0 collective-permute-done.9
  27.9 0.6 %add_add_fusion = f32[128,128]{1,0:T(8,128)} fusion(f32[128,128]{1,0:T(8,128)S(1)} %collective-permute-done.9, f32[128,128]{1,0:T(8,128)S(1)} %collective-permute-done.8, f32[128,128]{1,0:T(8,128)S(1)} %get-tuple-element.23, f32[128,128]{1,0:T(8,128)S(1)} %collective-permute-done.7), kind=kLoop, calls=%fused_computation | loop fusion | flops 49152 | bytes 327680 | tf_op jit(solution)/shard_map/add | solution.py:106
  (1 shorter events, 0.0 us)
Async XLA Ops:
  0.0 0.9 %copy-start = (bf16[1,32,4096]{2,1,0:T(8,128)(2,1)S(1)}, bf16[1,32,4096]{2,1,0:T(8,128)(2,1)}, u32[]{:S(2)}) copy-start(bf16[1,32,4096]{2,1,0:T(8,128)(2,1)} %amp_ref.1) | copy-start | bytes 786436
  1.0 5.1 %copy-start.1 = (bf16[64,1024]{1,0:T(8,128)(2,1)S(1)}, bf16[64,1024]{1,0:T(8,128)(2,1)}, u32[]{:S(2)}) copy-start(bf16[64,1024]{1,0:T(8,128)(2,1)} %refs_0_.1) | copy-start | bytes 393220
  1.0 14.4 %copy-start.2 = (f32[4,32,128]{2,1,0:T(8,128)S(1)}, f32[4,32,128]{2,1,0:T(8,128)}, u32[]{:S(2)}) copy-start(f32[4,32,128]{2,1,0:T(8,128)} %residual_ref.1) | copy-start | bytes 196612
  1.0 8.6 %collective-permute-start.3 = (bf16[32,1024]{1,0:T(8,128)(2,1)S(1)}, bf16[32,1024]{1,0:T(8,128)(2,1)S(1)}, u32[]{:S(2)}, u32[]{:S(2)}) collective-permute-start(bf16[32,1024]{1,0:T(8,128)(2,1)S(1)} %get-tuple-element.16), channel_id=1, source_target_pairs={{0,24},{8,16},{16,8},{24,0},{1,25},{9,17},{17,9},{25,1},{2,26},{10... | collective-permute-start | bytes 196616 | tf_op jit(solution)/shard_map/ppermute | solution.py:17
  6.1 8.9 %collective-permute-start.1 = (bf16[64,1024]{1,0:T(8,128)(2,1)S(1)}, bf16[64,1024]{1,0:T(8,128)(2,1)S(1)}, u32[]{:S(2)}, u32[]{:S(2)}) collective-permute-start(bf16[64,1024]{1,0:T(8,128)(2,1)S(1)} %copy-done.1), channel_id=1, source_target_pairs={{0,4},{1,5},{2,6},{3,7},{4,0},{5,1},{6,2},{7,3},{8,12},{9,13},{10,... | collective-permute-start | bytes 393224 | tf_op jit(solution)/shard_map/ppermute | solution.py:17
  7.6 7.3 %collective-permute-start = (bf16[64,1024]{1,0:T(8,128)(2,1)S(1)}, bf16[64,1024]{1,0:T(8,128)(2,1)S(1)}, u32[]{:S(2)}, u32[]{:S(2)}) collective-permute-start(bf16[64,1024]{1,0:T(8,128)(2,1)S(1)} %copy-done.1), channel_id=1, source_target_pairs={{0,2},{1,3},{2,0},{3,1},{4,6},{5,7},{6,4},{7,5},{8,10},{9,11},{10,... | collective-permute-start | bytes 393224 | tf_op jit(solution)/shard_map/ppermute | solution.py:17
  9.1 6.2 %collective-permute-start.2 = (bf16[64,1024]{1,0:T(8,128)(2,1)S(1)}, bf16[64,1024]{1,0:T(8,128)(2,1)S(1)}, u32[]{:S(2)}, u32[]{:S(2)}) collective-permute-start(bf16[64,1024]{1,0:T(8,128)(2,1)S(1)} %copy-done.1), channel_id=1, source_target_pairs={{0,6},{1,7},{2,4},{3,5},{4,2},{5,3},{6,0},{7,1},{8,14},{9,15},{10,... | collective-permute-start | bytes 393224 | tf_op jit(solution)/shard_map/ppermute | solution.py:17
  9.6 5.4 %collective-permute-start.4 = (bf16[32,1024]{1,0:T(8,128)(2,1)S(1)}, bf16[32,1024]{1,0:T(8,128)(2,1)S(1)}, u32[]{:S(2)}, u32[]{:S(2)}) collective-permute-start(bf16[32,1024]{1,0:T(8,128)(2,1)S(1)} %get-tuple-element.17), channel_id=1, source_target_pairs={{0,16},{8,24},{16,0},{24,8},{1,17},{9,25},{17,1},{25,9},{2,18},{10... | collective-permute-start | bytes 196616 | tf_op jit(solution)/shard_map/ppermute | solution.py:17
  9.6 5.4 %collective-permute-start.5 = (bf16[32,1024]{1,0:T(8,128)(2,1)S(1)}, bf16[32,1024]{1,0:T(8,128)(2,1)S(1)}, u32[]{:S(2)}, u32[]{:S(2)}) collective-permute-start(bf16[32,1024]{1,0:T(8,128)(2,1)S(1)} %get-tuple-element.18), channel_id=1, source_target_pairs={{0,8},{8,0},{16,24},{24,16},{1,9},{9,1},{17,25},{25,17},{2,10},{10... | collective-permute-start | bytes 196616 | tf_op jit(solution)/shard_map/ppermute | solution.py:17
  15.4 2.0 %collective-permute-start.6 = (bf16[256,1024]{1,0:T(8,128)(2,1)S(1)}, bf16[256,1024]{1,0:T(8,128)(2,1)S(1)}, u32[]{:S(2)}, u32[]{:S(2)}) collective-permute-start(bf16[256,1024]{1,0:T(8,128)(2,1)S(1)} %get-tuple-element.22.near), channel_id=1, source_target_pairs={{0,1},{1,0},{2,3},{3,2},{4,5},{5,4},{6,7},{7,6},{8,9},{9,8},{10,11... | collective-permute-start | bytes 1572872 | tf_op jit(solution)/shard_map/ppermute | solution.py:17
  17.4 0.7 %copy-start.3 = (s32[1,8]{1,0:T(1,128)S(1)}, s32[1,8]{1,0:T(1,128)}, u32[]{:S(2)}) copy-start(s32[1,8]{1,0:T(1,128)} %owner_ref.1) | copy-start | bytes 100
  19.1 6.8 %collective-permute-start.7 = (f32[128,128]{1,0:T(8,128)S(1)}, f32[128,128]{1,0:T(8,128)S(1)}, u32[]{:S(2)}, u32[]{:S(2)}) collective-permute-start(f32[128,128]{1,0:T(8,128)S(1)} %get-tuple-element.24), channel_id=1, source_target_pairs={{0,24},{8,16},{16,8},{24,0},{1,25},{9,17},{17,9},{25,1},{2,26},{10... | collective-permute-start | bytes 196616 | tf_op jit(solution)/shard_map/ppermute | solution.py:17
  20.8 7.1 %collective-permute-start.8 = (f32[128,128]{1,0:T(8,128)S(1)}, f32[128,128]{1,0:T(8,128)S(1)}, u32[]{:S(2)}, u32[]{:S(2)}) collective-permute-start(f32[128,128]{1,0:T(8,128)S(1)} %get-tuple-element.25), channel_id=1, source_target_pairs={{0,16},{8,24},{16,0},{24,8},{1,17},{9,25},{17,1},{25,9},{2,18},{10... | collective-permute-start | bytes 196616 | tf_op jit(solution)/shard_map/ppermute | solution.py:17
  20.8 7.1 %collective-permute-start.9 = (f32[128,128]{1,0:T(8,128)S(1)}, f32[128,128]{1,0:T(8,128)S(1)}, u32[]{:S(2)}, u32[]{:S(2)}) collective-permute-start(f32[128,128]{1,0:T(8,128)S(1)} %get-tuple-element.26), channel_id=1, source_target_pairs={{0,8},{8,0},{16,24},{24,16},{1,9},{9,1},{17,25},{25,17},{2,10},{10... | collective-permute-start | bytes 196616 | tf_op jit(solution)/shard_map/ppermute | solution.py:17

commit v3 on v2

--- a/solution.py
+++ b/solution.py
@@ -9,6 +9,7 @@
 from jax.sharding import PartitionSpec as P
 
 VMEM = pl.BlockSpec(memory_space=pltpu.VMEM)
+SCALE_ROWS = 16
 SMEM = pl.BlockSpec(memory_space=pltpu.SMEM)
 
 
@@ -17,7 +18,8 @@
     return lax.ppermute(value, axis, [(i, i ^ step) for i in range(n)])
 
 
-def split_kernel(amp_ref, *outs):
+def split_kernel(panel_ref, amp_ref, own_ref, *outs):
+    own_ref[...] = panel_ref[...]
     width = outs[0].shape[-1]
     row = lax.axis_index("row")
     for step, out in enumerate(outs):
@@ -34,15 +36,17 @@
     )(*args)
 
 
-def split_amplitudes(amplitudes, rows):
+def split_amplitudes(integrals, amplitudes, rows):
     _, pairs, kw = amplitudes.shape
     block = jax.ShapeDtypeStruct((pairs, kw // rows), amplitudes.dtype)
-    return call(split_kernel, [block] * rows, [VMEM], [amplitudes])
+    outs = [jax.ShapeDtypeStruct(integrals.shape, integrals.dtype)] + [block] * rows
+    own, *blocks = call(split_kernel, outs, [VMEM, VMEM], [integrals, amplitudes])
+    return own, blocks
 
 
-def assemble_kernel(steps, residual_ref, *refs):
+def assemble_kernel(steps, owner_ref, residual_ref, *refs):
     rows = len(steps)
-    panels, amps, (residual, near, lhs) = refs[:-rows - 3], refs[-rows - 3:-3], refs[-3:]
+    panels, amps, (owner, residual, near, lhs) = refs[:-rows - 4], refs[-rows - 4:-4], refs[-4:]
     pairs, height = amps[0].shape[0], panels[0].shape[0]
     row = lax.axis_index("row")
     for step, amp in zip(steps, amps):
@@ -51,13 +55,14 @@
     for index, panel in enumerate(panels):
         near[index * height:(index + 1) * height, :] = panel[...]
     residual[...] = residual_ref[...]
+    owner[...] = owner_ref[...]
 
 
-def assemble(steps, residual, panels, amps):
+def assemble(steps, owner, residual, panels, amps):
     outs = [jax.ShapeDtypeStruct((len(blocks) * blocks[0].shape[0], blocks[0].shape[1]), blocks[0].dtype)
             for blocks in (panels, amps)]
-    outs = [jax.ShapeDtypeStruct(residual.shape, residual.dtype)] + outs
-    args = [residual, *panels, *amps]
+    outs = [jax.ShapeDtypeStruct(x.shape, x.dtype) for x in (owner, residual)] + outs
+    args = [owner, residual, *panels, *amps]
     return call(functools.partial(assemble_kernel, steps), outs, [VMEM] * len(args), args)
 
 
@@ -79,31 +84,41 @@
             lhs[...], weights[step * width:(step + 1) * width, :],
             (((1,), (1,)), ((), ())), preferred_element_type=jnp.float32)
         if step == 0:
-            part = part + residual_ref[...].reshape(part.shape)
-        out[...] = part
+            out[...] = part + residual_ref[...].reshape(part.shape)
+        else:
+            largest = jnp.max(jnp.abs(part), axis=0, keepdims=True)
+            power = jnp.clip(14.0 - jnp.ceil(jnp.log2(jnp.maximum(largest, 1e-36))), -60.0, 120.0)
+            out[:part.shape[0], :] = part * jnp.exp2(power)
+            out[part.shape[0]:, :] = jnp.broadcast_to(power, (SCALE_ROWS, part.shape[1]))
 
 
 def contract(steps, owner, residual, lhs, near, far):
     rows, ab, depth = len(steps), 2 * near.shape[0], near.shape[1]
-    part = jax.ShapeDtypeStruct((lhs.shape[0], ab // rows), jnp.float32)
+    outs = [
+        jax.ShapeDtypeStruct((lhs.shape[0] + (SCALE_ROWS if step else 0), ab // rows), jnp.float32) for step in steps]
     return call(
-        functools.partial(contract_kernel, steps), [part] * rows, [SMEM, VMEM, VMEM, VMEM, VMEM],
+        functools.partial(contract_kernel, steps), outs, [SMEM, VMEM, VMEM, VMEM, VMEM],
         [owner, residual, lhs, near, far],
         [pltpu.VMEM((ab, depth), jnp.bfloat16)],
     )
 
 
+def exchange_partial(part, step):
+    got = exchange(part.astype(jnp.float16), "row", step).astype(jnp.float32)
+    return got[:-SCALE_ROWS] * jnp.exp2(-got[-SCALE_ROWS:1 - SCALE_ROWS])
+
+
 def shards(amplitudes, integrals, panel_owner, residual_in):
     rows, columns = lax.axis_size("row"), lax.axis_size("col")
     steps = tuple(range(rows - 1, -1, -1))
-    panels = [exchange(integrals, "col", step) if step else integrals for step in range(0, columns, 2)]
-    blocks = split_amplitudes(amplitudes, rows)
+    own, blocks = split_amplitudes(integrals, amplitudes, rows)
+    panels = [exchange(own, "col", step) if step else own for step in range(0, columns, 2)]
     amps = [exchange(blocks[step], "row", step) if step else blocks[0] for step in steps]
-    residual, near, lhs = assemble(steps, residual_in, panels, amps)
-    parts = contract(steps, panel_owner, residual, lhs, near, exchange(near, "col", 1))
+    owner, residual, near, lhs = assemble(steps, panel_owner, residual_in, panels, amps)
+    parts = contract(steps, owner, residual, lhs, near, exchange(near, "col", 1))
     total = parts[-1]
     for step, part in zip(steps[:-1], parts):
-        total = total + exchange(part, "row", step)
+        total = total + exchange_partial(part, step)
     return total.reshape(residual_in.shape)
 
 

time: 28.7 us -> 27.8 us (0.969)
  starting transfers between devices: 14.5 us -> 13.8 us
  waiting for transfers between devices: 10.6 us -> 9.99 us
    ppermute x10, starting transfers between devices: 14.5 us -> 13.8 us  [exchange(): return lax.ppermute(value, axis, [(i, i ^ step) for i in range(n)])]
    ppermute x10, waiting for transfers between devices: 10.6 us -> 9.99 us  [exchange(): return lax.ppermute(value, axis, [(i, i ^ step) for i in range(n)])]
  transfers between devices with their start and end apart: 10 -> 10, of which waited for: 5 -> 4; matrix products, arithmetic and copies ran while one was open for 0% -> 0% of each run, Pallas kernels for 0% -> 0%
where the time goes in v3:
time: 27.8 us; the launch traced here: 27.7 us
  starting transfers between devices  13.8 us (50%)
  waiting for transfers between devices  9.99 us (36%)
  local copies, waits for them, and re-layouts  1.86 us (7%)
  Pallas kernels  1.18 us (4%)
  other arithmetic  0.73 us (3%)
    ppermute x10, starting transfers between devices, exchange(): return lax.ppermute(value, axis, [(i, i ^ step) for i in range(n)])  13.8 us
    ppermute x10, waiting for transfers between devices, exchange(): return lax.ppermute(value, axis, [(i, i ^ step) for i in range(n)])  9.99 us
    unnamed x8, local copies, waits for them, and re-layouts  1.86 us
    pallas_call x3, Pallas kernels, call(): pl.pallas_call(kernel, out_shape=outs, in_specs=specs, out_specs=[VMEM] *...  1.18 us
    add x1, other arithmetic, shards(): total = total + exchange_partial(part, step)  0.66 us
  transfers between devices with their start and end apart: 10, of which 4 were waited for; matrix products, arithmetic and copies ran while one was open for 0% of the time, Pallas kernels for 0%

profile of v3, /device:TPU:0, one launch (start us, length us, event | category | flops | bytes accessed | tf_op | source)
XLA Modules:
  0.0 27.7 jit_solution(6037819252463632718)
XLA Ops:
  0.0 0.0 copy-start
  0.0 0.9 %copy-done = bf16[1,32,4096]{2,1,0:T(8,128)(2,1)S(1)} copy-done((bf16[1,32,4096]{2,1,0:T(8,128)(2,1)S(1)}, bf16[1,32,4096]{2,1,0:T(8,128)(2,1)}, u32[]{:S(2)}) %copy-start) | copy-done | bytes 262168
  1.0 0.0 copy-start.1
  1.0 0.9 %copy-done.1 = bf16[64,1024]{1,0:T(8,128)(2,1)S(1)} copy-done((bf16[64,1024]{1,0:T(8,128)(2,1)S(1)}, bf16[64,1024]{1,0:T(8,128)(2,1)}, u32[]{:S(2)}) %copy-start.1) | copy-done | bytes 131096
  1.9 0.0 copy-start.2
  1.9 5.1 %collective-permute-start.3 = (bf16[32,1024]{1,0:T(8,128)(2,1)S(1)}, bf16[32,1024]{1,0:T(8,128)(2,1)S(1)}, u32[]{:S(2)}, u32[]{:S(2)}) collective-permute-start(bf16[32,1024]{1,0:T(8,128)(2,1)S(1)} %get-tuple-element.19), channel_id=1, source_target_pairs={{0,24},{8,16},{16,8},{24,0},{1,25},{9,17},{17,9},{25,1},{2,26},{10... | collective-permute-start | bytes 196616 | tf_op jit(solution)/shard_map/ppermute | solution.py:18
  7.0 2.4 %collective-permute-start.2 = (bf16[64,1024]{1,0:T(8,128)(2,1)S(1)}, bf16[64,1024]{1,0:T(8,128)(2,1)S(1)}, u32[]{:S(2)}, u32[]{:S(2)}) collective-permute-start(bf16[64,1024]{1,0:T(8,128)(2,1)S(1)} %get-tuple-element.18.refs_0_), channel_id=1, source_target_pairs={{0,6},{1,7},{2,4},{3,5},{4,2},{5,3},{6,0},{7,1},{8,14},{9,15},{10,... | collective-permute-start | bytes 393224 | tf_op jit(solution)/shard_map/ppermute | solution.py:18
  9.5 0.5 %collective-permute-start.1 = (bf16[64,1024]{1,0:T(8,128)(2,1)S(1)}, bf16[64,1024]{1,0:T(8,128)(2,1)S(1)}, u32[]{:S(2)}, u32[]{:S(2)}) collective-permute-start(bf16[64,1024]{1,0:T(8,128)(2,1)S(1)} %get-tuple-element.18.refs_0_), channel_id=1, source_target_pairs={{0,4},{1,5},{2,6},{3,7},{4,0},{5,1},{6,2},{7,3},{8,12},{9,13},{10,... | collective-permute-start | bytes 393224 | tf_op jit(solution)/shard_map/ppermute | solution.py:18
  10.0 0.5 %collective-permute-start = (bf16[64,1024]{1,0:T(8,128)(2,1)S(1)}, bf16[64,1024]{1,0:T(8,128)(2,1)S(1)}, u32[]{:S(2)}, u32[]{:S(2)}) collective-permute-start(bf16[64,1024]{1,0:T(8,128)(2,1)S(1)} %get-tuple-element.18.refs_0_), channel_id=1, source_target_pairs={{0,2},{1,3},{2,0},{3,1},{4,6},{5,7},{6,4},{7,5},{8,10},{9,11},{10,... | collective-permute-start | bytes 393224 | tf_op jit(solution)/shard_map/ppermute | solution.py:18
  10.5 0.0 collective-permute-start.4
  10.5 0.0 collective-permute-done.3.refs_4_
  10.5 0.0 copy-start.3
  10.5 0.6 %collective-permute-start.5 = (bf16[32,1024]{1,0:T(8,128)(2,1)S(1)}, bf16[32,1024]{1,0:T(8,128)(2,1)S(1)}, u32[]{:S(2)}, u32[]{:S(2)}) collective-permute-start(bf16[32,1024]{1,0:T(8,128)(2,1)S(1)} %get-tuple-element.21), channel_id=1, source_target_pairs={{0,8},{8,0},{16,24},{24,16},{1,9},{9,1},{17,25},{25,17},{2,10},{10... | collective-permute-start | bytes 196616 | tf_op jit(solution)/shard_map/ppermute | solution.py:18
  11.1 4.7 %collective-permute-done.4.refs_5_ = bf16[32,1024]{1,0:T(8,128)(2,1)S(1)} collective-permute-done((bf16[32,1024]{1,0:T(8,128)(2,1)S(1)}, bf16[32,1024]{1,0:T(8,128)(2,1)S(1)}, u32[]{:S(2)}, u32[]{:S(2)}) %collective-permute-start.4) | collective-permute-done | bytes 65568 | tf_op jit(solution)/shard_map/ppermute | solution.py:18
  15.9 0.0 collective-permute-done.5.refs_6_
  15.9 0.0 collective-permute-done.2.refs_3_
  15.9 0.0 collective-permute-done.1.refs_2_
  15.9 0.0 collective-permute-done.refs_1_
  15.9 0.0 copy-done.2
  15.9 0.0 copy-done.3
  15.9 0.1 shard_map.47
  16.0 0.1 collective-permute-start.6
  16.1 1.9 %collective-permute-done.6.far = bf16[256,1024]{1,0:T(8,128)(2,1)S(1)} collective-permute-done((bf16[256,1024]{1,0:T(8,128)(2,1)S(1)}, bf16[256,1024]{1,0:T(8,128)(2,1)S(1)}, u32[]{:S(2)}, u32[]{:S(2)}) %collective-permute-start.6) | collective-permute-done | bytes 524320 | tf_op jit(solution)/shard_map/ppermute | solution.py:18
  18.0 1.1 %shard_map.48 = (f32[144,128]{1,0:T(8,128)S(1)}, f32[144,128]{1,0:T(8,128)S(1)}, f32[144,128]{1,0:T(8,128)S(1)}, f32[128,128]{1,0:T(8,128)S(1)}) custom-call(s32[1,8]{1,0:T(1,128)S(1)} %get-tuple-element.23.owner_ref, f32[4,32,128]{2,1,0:T(8,128)S(1)} %get-tuple-element.24.residual_ref, bf16[128,1024]{1,0:T(8,128)(2,1)S(1)} %get-tuple-element.25.lhs, ...), custom_call_target="tpu_custom_call" | custom-call | tf_op jit(solution)/shard_map/pallas_call | solution.py:33
  19.1 0.2 collective-permute-start.9
  19.3 2.0 %collective-permute-start.8 = (f16[144,128]{1,0:T(8,128)(2,1)S(1)}, f16[144,128]{1,0:T(8,128)(2,1)S(1)}, u32[]{:S(2)}, u32[]{:S(2)}) collective-permute-start(f16[144,128]{1,0:T(8,128)(2,1)S(1)} %convert_element_type.20), channel_id=1, source_target_pairs={{0,16},{8,24},{16,0},{24,8},{1,17},{9,25},{17,1},{25,9},{2,18},{10... | collective-permute-start | bytes 110600 | tf_op jit(solution)/shard_map/ppermute | solution.py:18
  21.3 2.4 %collective-permute-start.7 = (f16[144,128]{1,0:T(8,128)(2,1)S(1)}, f16[144,128]{1,0:T(8,128)(2,1)S(1)}, u32[]{:S(2)}, u32[]{:S(2)}) collective-permute-start(f16[144,128]{1,0:T(8,128)(2,1)S(1)} %convert_element_type.18), channel_id=1, source_target_pairs={{0,24},{8,16},{16,8},{24,0},{1,25},{9,17},{17,9},{25,1},{2,26},{10... | collective-permute-start | bytes 110600 | tf_op jit(solution)/shard_map/ppermute | solution.py:18
  23.6 0.0 collective-permute-done.9
  23.6 0.7 %collective-permute-done.8 = f16[144,128]{1,0:T(8,128)(2,1)S(1)} collective-permute-done((f16[144,128]{1,0:T(8,128)(2,1)S(1)}, f16[144,128]{1,0:T(8,128)(2,1)S(1)}, u32[]{:S(2)}, u32[]{:S(2)}) %collective-permute-start.8) | collective-permute-done | bytes 36896 | tf_op jit(solution)/shard_map/ppermute | solution.py:18
  24.3 2.7 %collective-permute-done.7 = f16[144,128]{1,0:T(8,128)(2,1)S(1)} collective-permute-done((f16[144,128]{1,0:T(8,128)(2,1)S(1)}, f16[144,128]{1,0:T(8,128)(2,1)S(1)}, u32[]{:S(2)}, u32[]{:S(2)}) %collective-permute-start.7) | collective-permute-done | bytes 36896 | tf_op jit(solution)/shard_map/ppermute | solution.py:18
  27.0 0.7 %fusion = f32[128,128]{1,0:T(8,128)} fusion(f32[144,128]{1,0:T(8,128)S(1)} %convert_element_type.23, f32[144,128]{1,0:T(8,128)S(1)} %convert_element_type.21, f32[128,128]{1,0:T(8,128)S(1)} %get-tuple-element.27, f32[144,128]{1,0:T(8,128)S(1)} %convert_element_type.19, f32[128]{0:T(128)S(1)} %fusion.5, f32[128]{0:T(128)S(1)} %fusion.8, f32[128]{0:T(128)S(1)} %fusion.11), kind=kLoop, calls=%fused_computation.1 | loop fusion | flops 98304 | bytes 329216 | tf_op jit(solution)/shard_map/add | solution.py:121
  (10 shorter events, 0.1 us)
Async XLA Ops:
  0.0 0.9 %copy-start = (bf16[1,32,4096]{2,1,0:T(8,128)(2,1)S(1)}, bf16[1,32,4096]{2,1,0:T(8,128)(2,1)}, u32[]{:S(2)}) copy-start(bf16[1,32,4096]{2,1,0:T(8,128)(2,1)} %amp_ref.1) | copy-start | bytes 786436
  1.0 0.9 %copy-start.1 = (bf16[64,1024]{1,0:T(8,128)(2,1)S(1)}, bf16[64,1024]{1,0:T(8,128)(2,1)}, u32[]{:S(2)}) copy-start(bf16[64,1024]{1,0:T(8,128)(2,1)} %panel_ref.1) | copy-start | bytes 393220
  1.9 14.0 %copy-start.2 = (f32[4,32,128]{2,1,0:T(8,128)S(1)}, f32[4,32,128]{2,1,0:T(8,128)}, u32[]{:S(2)}) copy-start(f32[4,32,128]{2,1,0:T(8,128)} %residual_ref.1) | copy-start | bytes 196612
  1.9 8.6 %collective-permute-start.3 = (bf16[32,1024]{1,0:T(8,128)(2,1)S(1)}, bf16[32,1024]{1,0:T(8,128)(2,1)S(1)}, u32[]{:S(2)}, u32[]{:S(2)}) collective-permute-start(bf16[32,1024]{1,0:T(8,128)(2,1)S(1)} %get-tuple-element.19), channel_id=1, source_target_pairs={{0,24},{8,16},{16,8},{24,0},{1,25},{9,17},{17,9},{25,1},{2,26},{10... | collective-permute-start | bytes 196616 | tf_op jit(solution)/shard_map/ppermute | solution.py:18
  7.0 8.9 %collective-permute-start.2 = (bf16[64,1024]{1,0:T(8,128)(2,1)S(1)}, bf16[64,1024]{1,0:T(8,128)(2,1)S(1)}, u32[]{:S(2)}, u32[]{:S(2)}) collective-permute-start(bf16[64,1024]{1,0:T(8,128)(2,1)S(1)} %get-tuple-element.18.refs_0_), channel_id=1, source_target_pairs={{0,6},{1,7},{2,4},{3,5},{4,2},{5,3},{6,0},{7,1},{8,14},{9,15},{10,... | collective-permute-start | bytes 393224 | tf_op jit(solution)/shard_map/ppermute | solution.py:18
  9.5 6.4 %collective-permute-start.1 = (bf16[64,1024]{1,0:T(8,128)(2,1)S(1)}, bf16[64,1024]{1,0:T(8,128)(2,1)S(1)}, u32[]{:S(2)}, u32[]{:S(2)}) collective-permute-start(bf16[64,1024]{1,0:T(8,128)(2,1)S(1)} %get-tuple-element.18.refs_0_), channel_id=1, source_target_pairs={{0,4},{1,5},{2,6},{3,7},{4,0},{5,1},{6,2},{7,3},{8,12},{9,13},{10,... | collective-permute-start | bytes 393224 | tf_op jit(solution)/shard_map/ppermute | solution.py:18
  10.0 5.9 %collective-permute-start = (bf16[64,1024]{1,0:T(8,128)(2,1)S(1)}, bf16[64,1024]{1,0:T(8,128)(2,1)S(1)}, u32[]{:S(2)}, u32[]{:S(2)}) collective-permute-start(bf16[64,1024]{1,0:T(8,128)(2,1)S(1)} %get-tuple-element.18.refs_0_), channel_id=1, source_target_pairs={{0,2},{1,3},{2,0},{3,1},{4,6},{5,7},{6,4},{7,5},{8,10},{9,11},{10,... | collective-permute-start | bytes 393224 | tf_op jit(solution)/shard_map/ppermute | solution.py:18
  10.5 5.4 %collective-permute-start.4 = (bf16[32,1024]{1,0:T(8,128)(2,1)S(1)}, bf16[32,1024]{1,0:T(8,128)(2,1)S(1)}, u32[]{:S(2)}, u32[]{:S(2)}) collective-permute-start(bf16[32,1024]{1,0:T(8,128)(2,1)S(1)} %get-tuple-element.20), channel_id=1, source_target_pairs={{0,16},{8,24},{16,0},{24,8},{1,17},{9,25},{17,1},{25,9},{2,18},{10... | collective-permute-start | bytes 196616 | tf_op jit(solution)/shard_map/ppermute | solution.py:18
  10.5 5.4 %copy-start.3 = (s32[1,8]{1,0:T(1,128)S(1)}, s32[1,8]{1,0:T(1,128)}, u32[]{:S(2)}) copy-start(s32[1,8]{1,0:T(1,128)} %owner_ref.1) | copy-start | bytes 100
  10.5 5.4 %collective-permute-start.5 = (bf16[32,1024]{1,0:T(8,128)(2,1)S(1)}, bf16[32,1024]{1,0:T(8,128)(2,1)S(1)}, u32[]{:S(2)}, u32[]{:S(2)}) collective-permute-start(bf16[32,1024]{1,0:T(8,128)(2,1)S(1)} %get-tuple-element.21), channel_id=1, source_target_pairs={{0,8},{8,0},{16,24},{24,16},{1,9},{9,1},{17,25},{25,17},{2,10},{10... | collective-permute-start | bytes 196616 | tf_op jit(solution)/shard_map/ppermute | solution.py:18
  16.0 2.0 %collective-permute-start.6 = (bf16[256,1024]{1,0:T(8,128)(2,1)S(1)}, bf16[256,1024]{1,0:T(8,128)(2,1)S(1)}, u32[]{:S(2)}, u32[]{:S(2)}) collective-permute-start(bf16[256,1024]{1,0:T(8,128)(2,1)S(1)} %get-tuple-element.26.near), channel_id=1, source_target_pairs={{0,1},{1,0},{2,3},{3,2},{4,5},{5,4},{6,7},{7,6},{8,9},{9,8},{10,11... | collective-permute-start | bytes 1572872 | tf_op jit(solution)/shard_map/ppermute | solution.py:18
  19.1 4.5 %collective-permute-start.9 = (f16[144,128]{1,0:T(8,128)(2,1)S(1)}, f16[144,128]{1,0:T(8,128)(2,1)S(1)}, u32[]{:S(2)}, u32[]{:S(2)}) collective-permute-start(f16[144,128]{1,0:T(8,128)(2,1)S(1)} %convert_element_type.22), channel_id=1, source_target_pairs={{0,8},{8,0},{16,24},{24,16},{1,9},{9,1},{17,25},{25,17},{2,10},{10... | collective-permute-start | bytes 110600 | tf_op jit(solution)/shard_map/ppermute | solution.py:18
  19.3 5.1 %collective-permute-start.8 = (f16[144,128]{1,0:T(8,128)(2,1)S(1)}, f16[144,128]{1,0:T(8,128)(2,1)S(1)}, u32[]{:S(2)}, u32[]{:S(2)}) collective-permute-start(f16[144,128]{1,0:T(8,128)(2,1)S(1)} %convert_element_type.20), channel_id=1, source_target_pairs={{0,16},{8,24},{16,0},{24,8},{1,17},{9,25},{17,1},{25,9},{2,18},{10... | collective-permute-start | bytes 110600 | tf_op jit(solution)/shard_map/ppermute | solution.py:18
  21.3 5.8 %collective-permute-start.7 = (f16[144,128]{1,0:T(8,128)(2,1)S(1)}, f16[144,128]{1,0:T(8,128)(2,1)S(1)}, u32[]{:S(2)}, u32[]{:S(2)}) collective-permute-start(f16[144,128]{1,0:T(8,128)(2,1)S(1)} %convert_element_type.18), channel_id=1, source_target_pairs={{0,24},{8,16},{16,8},{24,0},{1,25},{9,17},{17,9},{25,1},{2,26},{10... | collective-permute-start | bytes 110600 | tf_op jit(solution)/shard_map/ppermute | solution.py:18

commit v4 on v2

v4 whole, which is shorter than its diff:
```python
import functools
import math

import jax
import jax.numpy as jnp
from jax import lax
from jax.experimental import pallas as pl
from jax.experimental.pallas import tpu as pltpu
from jax.sharding import PartitionSpec as P

VMEM = pl.BlockSpec(memory_space=pltpu.VMEM)
HBM = pl.BlockSpec(memory_space=pltpu.HBM)
SMEM = pl.BlockSpec(memory_space=pltpu.SMEM)


def exchange(value, axis, step):
    n = lax.axis_size(axis)
    return lax.ppermute(value, axis, [(i, i ^ step) for i in range(n)])


def like(array, *shape):
    return jax.ShapeDtypeStruct(shape or array.shape, array.dtype)


def call(kernel, outs, specs, args, scratch=(), semaphores=()):
    size = sum(math.prod(x.shape) * jnp.dtype(x.dtype).itemsize for x in [*outs, *args, *scratch])
    return pl.pallas_call(
        kernel, out_shape=outs, in_specs=specs, out_specs=[VMEM] * len(outs), scratch_shapes=[*scratch, *semaphores],
        compiler_params=pltpu.CompilerParams(vmem_limit_bytes=size + (2 << 20)),
    )(*args)


def fetch_kernel(panel_ref, amp_ref, residual_ref, owner_ref, *refs):
    panel, residual, owner, blocks, sems = refs[0], refs[1], refs[2], refs[3:-1], refs[-1]
    width = blocks[0].shape[-1]
    row = lax.axis_index("row")
    pairs = [(panel_ref, panel), (residual_ref, residual), (owner_ref, owner)]
    for step, block in enumerate(blocks):
        at = pl.multiple_of((row ^ step) * width, width)
        pairs.append((amp_ref.at[0, :, pl.ds(at, width)], block))
    copies = [pltpu.make_async_copy(source, target, sems.at[i]) for i, (source, target) in enumerate(pairs)]
    for copy in copies:
        copy.start()
    for copy in copies:
        copy.wait()


def fetch(integrals, amplitudes, residual, owner, rows):
    _, pairs, kw = amplitudes.shape
    outs = [like(integrals), like(residual), like(owner)] + [like(amplitudes, pairs, kw // rows)] * rows
    args = [integrals, amplitudes, residual, owner]
    panel, residual, owner, *blocks = call(
        fetch_kernel, outs, [HBM] * 4, args, semaphores=[pltpu.SemaphoreType.DMA((len(outs),))])
    return panel, residual, owner, blocks


def assemble_kernel(count, *refs):
    panels, amps, (near, early) = refs[:count], refs[count:-2], refs[-2:]
    for blocks, out in ((panels, near), (amps, early)):
        height = blocks[0].shape[0]
        for index, block in enumerate(blocks):
            out[index * height:(index + 1) * height, :] = block[...]


def assemble(panels, amps):
    outs = [like(blocks[0], len(blocks) * blocks[0].shape[0], blocks[0].shape[1]) for blocks in (panels, amps)]
    args = [*panels, *amps]
    return call(functools.partial(assemble_kernel, len(panels)), outs, [VMEM] * len(args), args)


def contract_kernel(steps, owner_ref, residual_ref, early, late, near, far, *refs):
    outs, (lhs, weights) = refs[:len(steps)], refs[len(steps):]
    width, pairs = outs[0].shape[1], late.shape[0]
    row, col = lax.axis_index("row"), lax.axis_index("col")
    columns = owner_ref.shape[1]
    height = weights.shape[0] // columns
    per_row = width // height
    for index, step in enumerate([step for step in steps if step != 1]):
        at = pl.multiple_of((row ^ step) * pairs, pairs)
        lhs[pl.ds(at, pairs), :] = early[index * pairs:(index + 1) * pairs, :]
    lhs[pl.ds(pl.multiple_of((row ^ 1) * pairs, pairs), pairs), :] = late[...]
    for step in range(columns):
        owner = owner_ref[0, col ^ step]
        place = ((owner // per_row) ^ row) * per_row + owner % per_row
        at = pl.multiple_of(place * height, height)
        held, index = (near, far)[step % 2], step // 2
        weights[pl.ds(at, height), :] = held[index * height:(index + 1) * height, :]
    for step, out in zip(steps, outs):
        part = lax.dot_general(
            lhs[...], weights[step * width:(step + 1) * width, :],
            (((1,), (1,)), ((), ())), preferred_element_type=jnp.float32)
        if step == 0:
            part = part + residual_ref[...].reshape(part.shape)
        out[...] = part


def contract(steps, owner, residual, early, late, near, far):
    rows, ab, depth = len(steps), 2 * near.shape[0], near.shape[1]
    total = early.shape[0] + late.shape[0]
    part = jax.ShapeDtypeStruct((total, ab // rows), jnp.float32)
    return call(
        functools.partial(contract_kernel, steps), [part] * rows, [SMEM] + [VMEM] * 5,
        [owner, residual, early, late, near, far],
        [pltpu.VMEM((total, depth), jnp.bfloat16), pltpu.VMEM((ab, depth), jnp.bfloat16)],
    )


def shards(amplitudes, integrals, panel_owner, residual_in):
    rows, columns = lax.axis_size("row"), lax.axis_size("col")
    steps = tuple(range(rows - 1, -1, -1))
    own, residual, owner, blocks = fetch(integrals, amplitudes, residual_in, panel_owner, rows)
    panels = [exchange(own, "col", step) if step else own for step in range(0, columns, 2)]
    amps = {step: exchange(blocks[step], "row", step) if step else blocks[0] for step in steps}
    near, early = assemble(panels, [amps[step] for step in steps if step != 1])
    parts = contract(steps, owner, residual, early, amps[1], near, exchange(near, "col", 1))
    total = parts[-1]
    for step, part in zip(steps[:-1], parts):
        total = total + exchange(part, "row", step)
    return total.reshape(residual_in.shape)


def solution(mesh):
    placed = (P("row", "col", None), P("col", "row"), P("row", None), P(None, "col", "row"))
    return jax.shard_map(
        shards, mesh=mesh, in_specs=placed, out_specs=P(None, "col", "row"), check_vma=False
    )
```

time: 28.7 us -> 32.5 us (1.13)
  waiting for transfers between devices: 10.6 us -> 13.5 us
  local copies, waits for them, and re-layouts: 1.61 us -> 3.35 us
  starting transfers between devices: 14.5 us -> 13.2 us
  Pallas kernels: 1.15 us -> 1.52 us
    ppermute x10, waiting for transfers between devices: 10.6 us -> 13.5 us  [exchange(): return lax.ppermute(value, axis, [(i, i ^ step) for i in range(n)])]
    unnamed x8, local copies, waits for them, and re-layouts: 1.61 us -> 3.35 us
    ppermute x10, starting transfers between devices: 14.5 us -> 13.2 us  [exchange(): return lax.ppermute(value, axis, [(i, i ^ step) for i in range(n)])]
    pallas_call x3, Pallas kernels: 1.15 us -> 1.52 us  [call(): pl.pallas_call(kernel, out_shape=outs, in_specs=specs, out_specs=[VMEM] *...]
where the time goes in v4:
time: 32.5 us; the launch traced here: 32.3 us
  waiting for transfers between devices  13.5 us (42%)
  starting transfers between devices  13.2 us (41%)
  local copies, waits for them, and re-layouts  3.35 us (10%)
  Pallas kernels  1.52 us (5%)
  other arithmetic  0.65 us (2%)
    ppermute x10, waiting for transfers between devices, exchange(): return lax.ppermute(value, axis, [(i, i ^ step) for i in range(n)])  13.5 us
    ppermute x10, starting transfers between devices, exchange(): return lax.ppermute(value, axis, [(i, i ^ step) for i in range(n)])  13.2 us
    unnamed x8, local copies, waits for them, and re-layouts  3.35 us
    pallas_call x3, Pallas kernels, call(): pl.pallas_call(kernel, out_shape=outs, in_specs=specs, out_specs=[VMEM] *...  1.52 us
  transfers between devices with their start and end apart: 10, of which 5 were waited for; matrix products, arithmetic and copies ran while one was open for 0% of the time, Pallas kernels for 0%

profile of v4, /device:TPU:0, one launch (start us, length us, event | category | flops | bytes accessed | tf_op | source)
XLA Modules:
  0.0 32.3 jit_solution(17115821313065889548)
XLA Ops:
  0.0 0.0 copy-start
  0.0 0.9 %copy-done = bf16[1,32,4096]{2,1,0:T(8,128)(2,1)S(1)} copy-done((bf16[1,32,4096]{2,1,0:T(8,128)(2,1)S(1)}, bf16[1,32,4096]{2,1,0:T(8,128)(2,1)}, u32[]{:S(2)}) %copy-start) | copy-done | bytes 262168
  1.0 0.0 copy-start.1
  1.0 0.9 %copy-done.1 = bf16[64,1024]{1,0:T(8,128)(2,1)S(1)} copy-done((bf16[64,1024]{1,0:T(8,128)(2,1)S(1)}, bf16[64,1024]{1,0:T(8,128)(2,1)}, u32[]{:S(2)}) %copy-start.1) | copy-done | bytes 131096
  1.9 0.0 copy-start.2
  1.9 0.8 %copy-done.2 = f32[4,32,128]{2,1,0:T(8,128)S(1)} copy-done((f32[4,32,128]{2,1,0:T(8,128)S(1)}, f32[4,32,128]{2,1,0:T(8,128)}, u32[]{:S(2)}) %copy-start.2) | copy-done | bytes 65560
  2.7 0.0 copy-start.3
  2.7 0.7 %copy-done.3 = s32[1,8]{1,0:T(1,128)S(1)} copy-done((s32[1,8]{1,0:T(1,128)S(1)}, s32[1,8]{1,0:T(1,128)}, u32[]{:S(2)}) %copy-start.3) | copy-done | bytes 56
  3.4 0.4 %shard_map.46 = (bf16[64,1024]{1,0:T(8,128)(2,1)S(1)}, f32[4,32,128]{2,1,0:T(8,128)S(1)}, s32[1,8]{1,0:T(1,128)S(1)}, bf16[32,1024]{1,0:T(8,128)(2,1)S(1)}, bf16...) custom-call(bf16[64,1024]{1,0:T(8,128)(2,1)S(1)} %copy-done.1, ...), custom_call_target="tpu_custom_call" | custom-call | tf_op jit(solution)/shard_map/pallas_call | solution.py:27
  3.7 4.0 %collective-permute-start.2 = (bf16[64,1024]{1,0:T(8,128)(2,1)S(1)}, bf16[64,1024]{1,0:T(8,128)(2,1)S(1)}, u32[]{:S(2)}, u32[]{:S(2)}) collective-permute-start(bf16[64,1024]{1,0:T(8,128)(2,1)S(1)} %get-tuple-element.20.refs_0_), channel_id=1, source_target_pairs={{0,6},{1,7},{2,4},{3,5},{4,2},{5,3},{6,0},{7,1},{8,14},{9,15},{10,... | collective-permute-start | bytes 393224 | tf_op jit(solution)/shard_map/ppermute | solution.py:18
  7.7 0.5 %collective-permute-start.1 = (bf16[64,1024]{1,0:T(8,128)(2,1)S(1)}, bf16[64,1024]{1,0:T(8,128)(2,1)S(1)}, u32[]{:S(2)}, u32[]{:S(2)}) collective-permute-start(bf16[64,1024]{1,0:T(8,128)(2,1)S(1)} %get-tuple-element.20.refs_0_), channel_id=1, source_target_pairs={{0,4},{1,5},{2,6},{3,7},{4,0},{5,1},{6,2},{7,3},{8,12},{9,13},{10,... | collective-permute-start | bytes 393224 | tf_op jit(solution)/shard_map/ppermute | solution.py:18
  8.2 0.1 collective-permute-start
  8.3 4.0 %collective-permute-start.3 = (bf16[32,1024]{1,0:T(8,128)(2,1)S(1)}, bf16[32,1024]{1,0:T(8,128)(2,1)S(1)}, u32[]{:S(2)}, u32[]{:S(2)}) collective-permute-start(bf16[32,1024]{1,0:T(8,128)(2,1)S(1)} %get-tuple-element.21), channel_id=1, source_target_pairs={{0,24},{8,16},{16,8},{24,0},{1,25},{9,17},{17,9},{25,1},{2,26},{10... | collective-permute-start | bytes 196616 | tf_op jit(solution)/shard_map/ppermute | solution.py:18
  12.3 0.0 collective-permute-start.4
  12.3 2.7 %collective-permute-done.3.refs_4_ = bf16[32,1024]{1,0:T(8,128)(2,1)S(1)} collective-permute-done((bf16[32,1024]{1,0:T(8,128)(2,1)S(1)}, bf16[32,1024]{1,0:T(8,128)(2,1)S(1)}, u32[]{:S(2)}, u32[]{:S(2)}) %collective-permute-start.3) | collective-permute-done | bytes 65568 | tf_op jit(solution)/shard_map/ppermute | solution.py:18
  15.0 2.5 %collective-permute-done.4.refs_5_ = bf16[32,1024]{1,0:T(8,128)(2,1)S(1)} collective-permute-done((bf16[32,1024]{1,0:T(8,128)(2,1)S(1)}, bf16[32,1024]{1,0:T(8,128)(2,1)S(1)}, u32[]{:S(2)}, u32[]{:S(2)}) %collective-permute-start.4) | collective-permute-done | bytes 65568 | tf_op jit(solution)/shard_map/ppermute | solution.py:18
  17.5 0.0 collective-permute-done.2.refs_3_
  17.5 0.0 collective-permute-done.1.refs_2_
  17.5 0.0 collective-permute-done.refs_1_
  17.5 0.1 shard_map.47
  17.6 0.1 collective-permute-start.6
  17.7 0.1 collective-permute-start.5
  17.8 4.4 %collective-permute-done.5.late = bf16[32,1024]{1,0:T(8,128)(2,1)S(1)} collective-permute-done((bf16[32,1024]{1,0:T(8,128)(2,1)S(1)}, bf16[32,1024]{1,0:T(8,128)(2,1)S(1)}, u32[]{:S(2)}, u32[]{:S(2)}) %collective-permute-start.5) | collective-permute-done | bytes 65568 | tf_op jit(solution)/shard_map/ppermute | solution.py:18
  22.2 0.0 collective-permute-done.6.far
  22.2 1.1 %shard_map.48 = (f32[128,128]{1,0:T(8,128)S(1)}, f32[128,128]{1,0:T(8,128)S(1)}, f32[128,128]{1,0:T(8,128)S(1)}, f32[128,128]{1,0:T(8,128)S(1)}) custom-call(s32[1,8]{1,0:T(1,128)S(1)} %get-tuple-element.18.owner_ref, f32[4,32,128]{2,1,0:T(8,128)S(1)} %get-tuple-element.19.residual_ref, bf16[96,1024]{1,0:T(8,128)(2,1)S(1)} %get-tuple-element.24.early, ...), custom_call_target="tpu_custom_call" | custom-call | tf_op jit(solution)/shard_map/pallas_call | solution.py:27
  23.3 2.5 %collective-permute-start.7 = (f32[128,128]{1,0:T(8,128)S(1)}, f32[128,128]{1,0:T(8,128)S(1)}, u32[]{:S(2)}, u32[]{:S(2)}) collective-permute-start(f32[128,128]{1,0:T(8,128)S(1)} %get-tuple-element.28), channel_id=1, source_target_pairs={{0,24},{8,16},{16,8},{24,0},{1,25},{9,17},{17,9},{25,1},{2,26},{10... | collective-permute-start | bytes 196616 | tf_op jit(solution)/shard_map/ppermute | solution.py:18
  25.8 0.0 collective-permute-start.8
  25.8 2.0 %collective-permute-start.9 = (f32[128,128]{1,0:T(8,128)S(1)}, f32[128,128]{1,0:T(8,128)S(1)}, u32[]{:S(2)}, u32[]{:S(2)}) collective-permute-start(f32[128,128]{1,0:T(8,128)S(1)} %get-tuple-element.30), channel_id=1, source_target_pairs={{0,8},{8,0},{16,24},{24,16},{1,9},{9,1},{17,25},{25,17},{2,10},{10... | collective-permute-start | bytes 196616 | tf_op jit(solution)/shard_map/ppermute | solution.py:18
  27.7 1.9 %collective-permute-done.7 = f32[128,128]{1,0:T(8,128)S(1)} collective-permute-done((f32[128,128]{1,0:T(8,128)S(1)}, f32[128,128]{1,0:T(8,128)S(1)}, u32[]{:S(2)}, u32[]{:S(2)}) %collective-permute-start.7) | collective-permute-done | bytes 65568 | tf_op jit(solution)/shard_map/ppermute | solution.py:18
  29.6 2.0 %collective-permute-done.8 = f32[128,128]{1,0:T(8,128)S(1)} collective-permute-done((f32[128,128]{1,0:T(8,128)S(1)}, f32[128,128]{1,0:T(8,128)S(1)}, u32[]{:S(2)}, u32[]{:S(2)}) %collective-permute-start.8) | collective-permute-done | bytes 65568 | tf_op jit(solution)/shard_map/ppermute | solution.py:18
  31.6 0.0 collective-permute-done.9
  31.6 0.6 %add_add_fusion = f32[128,128]{1,0:T(8,128)} fusion(f32[128,128]{1,0:T(8,128)S(1)} %collective-permute-done.9, f32[128,128]{1,0:T(8,128)S(1)} %collective-permute-done.8, f32[128,128]{1,0:T(8,128)S(1)} %get-tuple-element.27, f32[128,128]{1,0:T(8,128)S(1)} %collective-permute-done.7), kind=kLoop, calls=%fused_computation | loop fusion | flops 49152 | bytes 327680 | tf_op jit(solution)/shard_map/add | solution.py:118
Async XLA Ops:
  0.0 0.9 %copy-start = (bf16[1,32,4096]{2,1,0:T(8,128)(2,1)S(1)}, bf16[1,32,4096]{2,1,0:T(8,128)(2,1)}, u32[]{:S(2)}) copy-start(bf16[1,32,4096]{2,1,0:T(8,128)(2,1)} %amp_ref.1) | copy-start | bytes 786436
  1.0 0.9 %copy-start.1 = (bf16[64,1024]{1,0:T(8,128)(2,1)S(1)}, bf16[64,1024]{1,0:T(8,128)(2,1)}, u32[]{:S(2)}) copy-start(bf16[64,1024]{1,0:T(8,128)(2,1)} %panel_ref.1) | copy-start | bytes 393220
  1.9 0.8 %copy-start.2 = (f32[4,32,128]{2,1,0:T(8,128)S(1)}, f32[4,32,128]{2,1,0:T(8,128)}, u32[]{:S(2)}) copy-start(f32[4,32,128]{2,1,0:T(8,128)} %residual_ref.1) | copy-start | bytes 196612
  2.7 0.7 %copy-start.3 = (s32[1,8]{1,0:T(1,128)S(1)}, s32[1,8]{1,0:T(1,128)}, u32[]{:S(2)}) copy-start(s32[1,8]{1,0:T(1,128)} %owner_ref.1) | copy-start | bytes 100
  3.7 13.8 %collective-permute-start.2 = (bf16[64,1024]{1,0:T(8,128)(2,1)S(1)}, bf16[64,1024]{1,0:T(8,128)(2,1)S(1)}, u32[]{:S(2)}, u32[]{:S(2)}) collective-permute-start(bf16[64,1024]{1,0:T(8,128)(2,1)S(1)} %get-tuple-element.20.refs_0_), channel_id=1, source_target_pairs={{0,6},{1,7},{2,4},{3,5},{4,2},{5,3},{6,0},{7,1},{8,14},{9,15},{10,... | collective-permute-start | bytes 393224 | tf_op jit(solution)/shard_map/ppermute | solution.py:18
  7.7 9.8 %collective-permute-start.1 = (bf16[64,1024]{1,0:T(8,128)(2,1)S(1)}, bf16[64,1024]{1,0:T(8,128)(2,1)S(1)}, u32[]{:S(2)}, u32[]{:S(2)}) collective-permute-start(bf16[64,1024]{1,0:T(8,128)(2,1)S(1)} %get-tuple-element.20.refs_0_), channel_id=1, source_target_pairs={{0,4},{1,5},{2,6},{3,7},{4,0},{5,1},{6,2},{7,3},{8,12},{9,13},{10,... | collective-permute-start | bytes 393224 | tf_op jit(solution)/shard_map/ppermute | solution.py:18
  8.2 9.3 %collective-permute-start = (bf16[64,1024]{1,0:T(8,128)(2,1)S(1)}, bf16[64,1024]{1,0:T(8,128)(2,1)S(1)}, u32[]{:S(2)}, u32[]{:S(2)}) collective-permute-start(bf16[64,1024]{1,0:T(8,128)(2,1)S(1)} %get-tuple-element.20.refs_0_), channel_id=1, source_target_pairs={{0,2},{1,3},{2,0},{3,1},{4,6},{5,7},{6,4},{7,5},{8,10},{9,11},{10,... | collective-permute-start | bytes 393224 | tf_op jit(solution)/shard_map/ppermute | solution.py:18
  8.3 6.7 %collective-permute-start.3 = (bf16[32,1024]{1,0:T(8,128)(2,1)S(1)}, bf16[32,1024]{1,0:T(8,128)(2,1)S(1)}, u32[]{:S(2)}, u32[]{:S(2)}) collective-permute-start(bf16[32,1024]{1,0:T(8,128)(2,1)S(1)} %get-tuple-element.21), channel_id=1, source_target_pairs={{0,24},{8,16},{16,8},{24,0},{1,25},{9,17},{17,9},{25,1},{2,26},{10... | collective-permute-start | bytes 196616 | tf_op jit(solution)/shard_map/ppermute | solution.py:18
  12.3 5.2 %collective-permute-start.4 = (bf16[32,1024]{1,0:T(8,128)(2,1)S(1)}, bf16[32,1024]{1,0:T(8,128)(2,1)S(1)}, u32[]{:S(2)}, u32[]{:S(2)}) collective-permute-start(bf16[32,1024]{1,0:T(8,128)(2,1)S(1)} %get-tuple-element.22), channel_id=1, source_target_pairs={{0,16},{8,24},{16,0},{24,8},{1,17},{9,25},{17,1},{25,9},{2,18},{10... | collective-permute-start | bytes 196616 | tf_op jit(solution)/shard_map/ppermute | solution.py:18
  17.6 4.6 %collective-permute-start.6 = (bf16[256,1024]{1,0:T(8,128)(2,1)S(1)}, bf16[256,1024]{1,0:T(8,128)(2,1)S(1)}, u32[]{:S(2)}, u32[]{:S(2)}) collective-permute-start(bf16[256,1024]{1,0:T(8,128)(2,1)S(1)} %get-tuple-element.26.near), channel_id=1, source_target_pairs={{0,1},{1,0},{2,3},{3,2},{4,5},{5,4},{6,7},{7,6},{8,9},{9,8},{10,11... | collective-permute-start | bytes 1572872 | tf_op jit(solution)/shard_map/ppermute | solution.py:18
  17.7 4.5 %collective-permute-start.5 = (bf16[32,1024]{1,0:T(8,128)(2,1)S(1)}, bf16[32,1024]{1,0:T(8,128)(2,1)S(1)}, u32[]{:S(2)}, u32[]{:S(2)}) collective-permute-start(bf16[32,1024]{1,0:T(8,128)(2,1)S(1)} %get-tuple-element.25), channel_id=1, source_target_pairs={{0,8},{8,0},{16,24},{24,16},{1,9},{9,1},{17,25},{25,17},{2,10},{10... | collective-permute-start | bytes 196616 | tf_op jit(solution)/shard_map/ppermute | solution.py:18
  23.3 6.3 %collective-permute-start.7 = (f32[128,128]{1,0:T(8,128)S(1)}, f32[128,128]{1,0:T(8,128)S(1)}, u32[]{:S(2)}, u32[]{:S(2)}) collective-permute-start(f32[128,128]{1,0:T(8,128)S(1)} %get-tuple-element.28), channel_id=1, source_target_pairs={{0,24},{8,16},{16,8},{24,0},{1,25},{9,17},{17,9},{25,1},{2,26},{10... | collective-permute-start | bytes 196616 | tf_op jit(solution)/shard_map/ppermute | solution.py:18
  25.8 5.9 %collective-permute-start.8 = (f32[128,128]{1,0:T(8,128)S(1)}, f32[128,128]{1,0:T(8,128)S(1)}, u32[]{:S(2)}, u32[]{:S(2)}) collective-permute-start(f32[128,128]{1,0:T(8,128)S(1)} %get-tuple-element.29), channel_id=1, source_target_pairs={{0,16},{8,24},{16,0},{24,8},{1,17},{9,25},{17,1},{25,9},{2,18},{10... | collective-permute-start | bytes 196616 | tf_op jit(solution)/shard_map/ppermute | solution.py:18
  25.8 5.9 %collective-permute-start.9 = (f32[128,128]{1,0:T(8,128)S(1)}, f32[128,128]{1,0:T(8,128)S(1)}, u32[]{:S(2)}, u32[]{:S(2)}) collective-permute-start(f32[128,128]{1,0:T(8,128)S(1)} %get-tuple-element.30), channel_id=1, source_target_pairs={{0,8},{8,0},{16,24},{24,16},{1,9},{9,1},{17,25},{25,17},{2,10},{10... | collective-permute-start | bytes 196616 | tf_op jit(solution)/shard_map/ppermute | solution.py:18

commit v5 on v4

v5 whole, which is shorter than its diff:
```python
import functools
import math

import jax
import jax.numpy as jnp
from jax import lax
from jax.experimental import pallas as pl
from jax.experimental.pallas import tpu as pltpu
from jax.sharding import PartitionSpec as P

VMEM = pl.BlockSpec(memory_space=pltpu.VMEM)
HBM = pl.BlockSpec(memory_space=pltpu.HBM)
SMEM = pl.BlockSpec(memory_space=pltpu.SMEM)


def exchange(value, axis, step):
    n = lax.axis_size(axis)
    return lax.ppermute(value, axis, [(i, i ^ step) for i in range(n)])


def like(array, *shape):
    return jax.ShapeDtypeStruct(shape or array.shape, array.dtype)


def call(kernel, outs, specs, args, scratch=(), semaphores=()):
    size = sum(math.prod(x.shape) * jnp.dtype(x.dtype).itemsize for x in [*outs, *args, *scratch])
    return pl.pallas_call(
        kernel, out_shape=outs, in_specs=specs, out_specs=[VMEM] * len(outs), scratch_shapes=[*scratch, *semaphores],
        compiler_params=pltpu.CompilerParams(vmem_limit_bytes=size + (2 << 20)),
    )(*args)


def fetch_kernel(panel_ref, amp_ref, residual_ref, owner_ref, *refs):
    panel, residual, owner, blocks, sems = refs[0], refs[1], refs[2], refs[3:-1], refs[-1]
    width = blocks[0].shape[-1]
    row = lax.axis_index("row")
    pairs = [(panel_ref, panel), (residual_ref, residual), (owner_ref, owner)]
    for step, block in enumerate(blocks):
        at = pl.multiple_of((row ^ step) * width, width)
        pairs.append((amp_ref.at[0, :, pl.ds(at, width)], block))
    copies = [pltpu.make_async_copy(source, target, sems.at[i]) for i, (source, target) in enumerate(pairs)]
    for copy in copies:
        copy.start()
    for copy in copies:
        copy.wait()


def fetch(integrals, amplitudes, residual, owner, rows):
    _, pairs, kw = amplitudes.shape
    outs = [like(integrals), like(residual), like(owner)] + [like(amplitudes, pairs, kw // rows)] * rows
    args = [pltpu.with_memory_space_constraint(x, pltpu.HBM) for x in (integrals, amplitudes, residual, owner)]
    panel, residual, owner, *blocks = call(
        fetch_kernel, outs, [HBM] * 4, args, semaphores=[pltpu.SemaphoreType.DMA((len(outs),))])
    return panel, residual, owner, blocks


def assemble_kernel(steps, *refs):
    rows = len(steps)
    panels, amps, (near, lhs) = refs[:-rows - 2], refs[-rows - 2:-2], refs[-2:]
    height, pairs = panels[0].shape[0], amps[0].shape[0]
    row = lax.axis_index("row")
    for index, panel in enumerate(panels):
        near[index * height:(index + 1) * height, :] = panel[...]
    for step, amp in zip(steps, amps):
        at = pl.multiple_of((row ^ step) * pairs, pairs)
        lhs[pl.ds(at, pairs), :] = amp[...]


def assemble(steps, panels, amps):
    outs = [like(blocks[0], len(blocks) * blocks[0].shape[0], blocks[0].shape[1]) for blocks in (panels, amps)]
    args = [*panels, *amps]
    return call(functools.partial(assemble_kernel, steps), outs, [VMEM] * len(args), args)


def product(panels, lhs):
    return lax.dot_general(panels[...], lhs[...], (((1,), (1,)), ((), ())), preferred_element_type=jnp.float32)


def near_kernel(near, lhs, out):
    out[...] = product(near, lhs)


def contract_near(near, lhs):
    out = jax.ShapeDtypeStruct((near.shape[0], lhs.shape[0]), jnp.float32)
    return call(near_kernel, [out], [VMEM, VMEM], [near, lhs])[0]


def contract_kernel(steps, owner_ref, residual_ref, lhs, near_part, far, *refs):
    outs, ordered = refs[:-1], refs[-1]
    width = outs[0].shape[1]
    row, col = lax.axis_index("row"), lax.axis_index("col")
    columns = owner_ref.shape[1]
    height = ordered.shape[0] // columns
    per_row = width // height
    for half, part in enumerate((near_part[...], product(far, lhs))):
        for index in range(columns // 2):
            owner = owner_ref[0, col ^ (2 * index + half)]
            place = ((owner // per_row) ^ row) * per_row + owner % per_row
            at = pl.multiple_of(place * height, height)
            ordered[pl.ds(at, height), :] = part[index * height:(index + 1) * height, :]
    for step, out in zip(steps, outs):
        part = ordered[step * width:(step + 1) * width, :].T
        if step == 0:
            part = part + residual_ref[...].reshape(part.shape)
        out[...] = part


def contract(steps, owner, residual, lhs, near_part, far):
    rows, ab = len(steps), 2 * far.shape[0]
    part = jax.ShapeDtypeStruct((lhs.shape[0], ab // rows), jnp.float32)
    return call(
        functools.partial(contract_kernel, steps), [part] * rows, [SMEM] + [VMEM] * 4,
        [owner, residual, lhs, near_part, far], [pltpu.VMEM((ab, lhs.shape[0]), jnp.float32)],
    )


def shards(amplitudes, integrals, panel_owner, residual_in):
    rows, columns = lax.axis_size("row"), lax.axis_size("col")
    steps = tuple(range(rows - 1, -1, -1))
    own, residual, owner, blocks = fetch(integrals, amplitudes, residual_in, panel_owner, rows)
    panels = [exchange(own, "col", step) if step else own for step in range(0, columns, 2)]
    amps = [exchange(blocks[step], "row", step) if step else blocks[0] for step in steps]
    near, lhs = assemble(steps, panels, amps)
    far = exchange(near, "col", 1)
    parts = contract(steps, owner, residual, lhs, contract_near(near, lhs), far)
    total = parts[-1]
    for step, part in zip(steps[:-1], parts):
        total = total + exchange(part, "row", step)
    return total.reshape(residual_in.shape)


def solution(mesh):
    placed = (P("row", "col", None), P("col", "row"), P("row", None), P(None, "col", "row"))
    return jax.shard_map(
        shards, mesh=mesh, in_specs=placed, out_specs=P(None, "col", "row"), check_vma=False
    )
```

time: 32.5 us -> 27.7 us (0.85)
  local copies, waits for them, and re-layouts: 3.35 us -> 0 us
  waiting for transfers between devices: 13.5 us -> 10.7 us
  Pallas kernels: 1.52 us -> 2.43 us
  starting transfers between devices: 13.2 us -> 13.8 us
    unnamed x8 -> x0, local copies, waits for them, and re-layouts: 3.35 us -> none
    ppermute x10, waiting for transfers between devices: 13.5 us -> 10.7 us  [exchange(): return lax.ppermute(value, axis, [(i, i ^ step) for i in range(n)])]
    pallas_call x3 -> x4, Pallas kernels: 1.52 us -> 2.43 us  [call(): pl.pallas_call(kernel, out_shape=outs, in_specs=specs, out_specs=[VMEM] *...]
    ppermute x10, starting transfers between devices: 13.2 us -> 13.8 us  [exchange(): return lax.ppermute(value, axis, [(i, i ^ step) for i in range(n)])]
  transfers between devices with their start and end apart: 10 -> 10, of which waited for: 5 -> 4; matrix products, arithmetic and copies ran while one was open for 0% -> 0% of each run, Pallas kernels for 0% -> 1%
where the time goes in v5:
time: 27.7 us; the launch traced here: 27.6 us
  starting transfers between devices  13.8 us (50%)
  waiting for transfers between devices  10.7 us (39%)
  Pallas kernels  2.43 us (9%)
  other arithmetic  0.65 us (2%)
    ppermute x10, starting transfers between devices, exchange(): return lax.ppermute(value, axis, [(i, i ^ step) for i in range(n)])  13.8 us
    ppermute x10, waiting for transfers between devices, exchange(): return lax.ppermute(value, axis, [(i, i ^ step) for i in range(n)])  10.7 us
    pallas_call x4, Pallas kernels, call(): pl.pallas_call(kernel, out_shape=outs, in_specs=specs, out_specs=[VMEM] *...  2.43 us
    add x1, other arithmetic, shards(): total = total + exchange(part, 'row', step)  0.65 us
  transfers between devices with their start and end apart: 10, of which 4 were waited for; matrix products, arithmetic and copies ran while one was open for 0% of the time, Pallas kernels for 1%

profile of v5, /device:TPU:0, one launch (start us, length us, event | category | flops | bytes accessed | tf_op | source)
XLA Modules:
  0.0 27.6 jit_solution(61788179349659116)
XLA Ops:
  0.0 1.1 %shard_map.46 = (bf16[64,1024]{1,0:T(8,128)(2,1)S(1)}, f32[4,32,128]{2,1,0:T(8,128)S(1)}, s32[1,8]{1,0:T(1,128)S(1)}, bf16[32,1024]{1,0:T(8,128)(2,1)S(1)}, bf16...) custom-call(bf16[64,1024]{1,0:T(8,128)(2,1)} %panel_ref.1, ...), custom_call_target="tpu_custom_call" | custom-call | tf_op jit(solution)/shard_map/pallas_call | solution.py:27
  1.1 5.1 %collective-permute-start.3 = (bf16[32,1024]{1,0:T(8,128)(2,1)S(1)}, bf16[32,1024]{1,0:T(8,128)(2,1)S(1)}, u32[]{:S(2)}, u32[]{:S(2)}) collective-permute-start(bf16[32,1024]{1,0:T(8,128)(2,1)S(1)} %get-tuple-element.21), channel_id=1, source_target_pairs={{0,24},{8,16},{16,8},{24,0},{1,25},{9,17},{17,9},{25,1},{2,26},{10... | collective-permute-start | bytes 196616 | tf_op jit(solution)/shard_map/ppermute | solution.py:18
  6.2 2.4 %collective-permute-start.2 = (bf16[64,1024]{1,0:T(8,128)(2,1)S(1)}, bf16[64,1024]{1,0:T(8,128)(2,1)S(1)}, u32[]{:S(2)}, u32[]{:S(2)}) collective-permute-start(bf16[64,1024]{1,0:T(8,128)(2,1)S(1)} %get-tuple-element.20.refs_0_), channel_id=1, source_target_pairs={{0,6},{1,7},{2,4},{3,5},{4,2},{5,3},{6,0},{7,1},{8,14},{9,15},{10,... | collective-permute-start | bytes 393224 | tf_op jit(solution)/shard_map/ppermute | solution.py:18
  8.7 0.5 %collective-permute-start.1 = (bf16[64,1024]{1,0:T(8,128)(2,1)S(1)}, bf16[64,1024]{1,0:T(8,128)(2,1)S(1)}, u32[]{:S(2)}, u32[]{:S(2)}) collective-permute-start(bf16[64,1024]{1,0:T(8,128)(2,1)S(1)} %get-tuple-element.20.refs_0_), channel_id=1, source_target_pairs={{0,4},{1,5},{2,6},{3,7},{4,0},{5,1},{6,2},{7,3},{8,12},{9,13},{10,... | collective-permute-start | bytes 393224 | tf_op jit(solution)/shard_map/ppermute | solution.py:18
  9.2 0.5 %collective-permute-start = (bf16[64,1024]{1,0:T(8,128)(2,1)S(1)}, bf16[64,1024]{1,0:T(8,128)(2,1)S(1)}, u32[]{:S(2)}, u32[]{:S(2)}) collective-permute-start(bf16[64,1024]{1,0:T(8,128)(2,1)S(1)} %get-tuple-element.20.refs_0_), channel_id=1, source_target_pairs={{0,2},{1,3},{2,0},{3,1},{4,6},{5,7},{6,4},{7,5},{8,10},{9,11},{10,... | collective-permute-start | bytes 393224 | tf_op jit(solution)/shard_map/ppermute | solution.py:18
  9.7 0.0 collective-permute-start.4
  9.7 0.0 collective-permute-done.3.refs_4_
  9.7 0.6 %collective-permute-start.5 = (bf16[32,1024]{1,0:T(8,128)(2,1)S(1)}, bf16[32,1024]{1,0:T(8,128)(2,1)S(1)}, u32[]{:S(2)}, u32[]{:S(2)}) collective-permute-start(bf16[32,1024]{1,0:T(8,128)(2,1)S(1)} %get-tuple-element.23), channel_id=1, source_target_pairs={{0,8},{8,0},{16,24},{24,16},{1,9},{9,1},{17,25},{25,17},{2,10},{10... | collective-permute-start | bytes 196616 | tf_op jit(solution)/shard_map/ppermute | solution.py:18
  10.4 4.7 %collective-permute-done.4.refs_5_ = bf16[32,1024]{1,0:T(8,128)(2,1)S(1)} collective-permute-done((bf16[32,1024]{1,0:T(8,128)(2,1)S(1)}, bf16[32,1024]{1,0:T(8,128)(2,1)S(1)}, u32[]{:S(2)}, u32[]{:S(2)}) %collective-permute-start.4) | collective-permute-done | bytes 65568 | tf_op jit(solution)/shard_map/ppermute | solution.py:18
  15.1 0.0 collective-permute-done.5.refs_6_
  15.1 0.0 collective-permute-done.2.refs_3_
  15.1 0.0 collective-permute-done.1.refs_2_
  15.1 0.0 collective-permute-done.refs_1_
  15.1 0.1 shard_map.47
  15.2 0.1 collective-permute-start.6
  15.3 0.3 %shard_map.48.near_part = f32[256,128]{1,0:T(8,128)S(1)} custom-call(bf16[256,1024]{1,0:T(8,128)(2,1)S(1)} %get-tuple-element.26.near, bf16[128,1024]{1,0:T(8,128)(2,1)S(1)} %get-tuple-element.25.lhs), custom_call_target="tpu_custom_call" | custom-call | tf_op jit(solution)/shard_map/pallas_call | solution.py:27
  15.5 1.6 %collective-permute-done.6.far = bf16[256,1024]{1,0:T(8,128)(2,1)S(1)} collective-permute-done((bf16[256,1024]{1,0:T(8,128)(2,1)S(1)}, bf16[256,1024]{1,0:T(8,128)(2,1)S(1)}, u32[]{:S(2)}, u32[]{:S(2)}) %collective-permute-start.6) | collective-permute-done | bytes 524320 | tf_op jit(solution)/shard_map/ppermute | solution.py:18
  17.1 1.0 %shard_map.49 = (f32[128,128]{1,0:T(8,128)S(1)}, f32[128,128]{1,0:T(8,128)S(1)}, f32[128,128]{1,0:T(8,128)S(1)}, f32[128,128]{1,0:T(8,128)S(1)}) custom-call(s32[1,8]{1,0:T(1,128)S(1)} %get-tuple-element.18.owner_ref, f32[4,32,128]{2,1,0:T(8,128)S(1)} %get-tuple-element.19.residual_ref, bf16[128,1024]{1,0:T(8,128)(2,1)S(1)} %get-tuple-element.25.lhs, ...), custom_call_target="tpu_custom_call" | custom-call | tf_op jit(solution)/shard_map/pallas_call | solution.py:27
  18.1 1.5 %collective-permute-start.7 = (f32[128,128]{1,0:T(8,128)S(1)}, f32[128,128]{1,0:T(8,128)S(1)}, u32[]{:S(2)}, u32[]{:S(2)}) collective-permute-start(f32[128,128]{1,0:T(8,128)S(1)} %get-tuple-element.28), channel_id=1, source_target_pairs={{0,24},{8,16},{16,8},{24,0},{1,25},{9,17},{17,9},{25,1},{2,26},{10... | collective-permute-start | bytes 196616 | tf_op jit(solution)/shard_map/ppermute | solution.py:18
  19.7 0.4 %collective-permute-start.8 = (f32[128,128]{1,0:T(8,128)S(1)}, f32[128,128]{1,0:T(8,128)S(1)}, u32[]{:S(2)}, u32[]{:S(2)}) collective-permute-start(f32[128,128]{1,0:T(8,128)S(1)} %get-tuple-element.29), channel_id=1, source_target_pairs={{0,16},{8,24},{16,0},{24,8},{1,17},{9,25},{17,1},{25,9},{2,18},{10... | collective-permute-start | bytes 196616 | tf_op jit(solution)/shard_map/ppermute | solution.py:18
  20.1 2.5 %collective-permute-start.9 = (f32[128,128]{1,0:T(8,128)S(1)}, f32[128,128]{1,0:T(8,128)S(1)}, u32[]{:S(2)}, u32[]{:S(2)}) collective-permute-start(f32[128,128]{1,0:T(8,128)S(1)} %get-tuple-element.30), channel_id=1, source_target_pairs={{0,8},{8,0},{16,24},{24,16},{1,9},{9,1},{17,25},{25,17},{2,10},{10... | collective-permute-start | bytes 196616 | tf_op jit(solution)/shard_map/ppermute | solution.py:18
  22.6 2.4 %collective-permute-done.7 = f32[128,128]{1,0:T(8,128)S(1)} collective-permute-done((f32[128,128]{1,0:T(8,128)S(1)}, f32[128,128]{1,0:T(8,128)S(1)}, u32[]{:S(2)}, u32[]{:S(2)}) %collective-permute-start.7) | collective-permute-done | bytes 65568 | tf_op jit(solution)/shard_map/ppermute | solution.py:18
  25.0 2.0 %collective-permute-done.8 = f32[128,128]{1,0:T(8,128)S(1)} collective-permute-done((f32[128,128]{1,0:T(8,128)S(1)}, f32[128,128]{1,0:T(8,128)S(1)}, u32[]{:S(2)}, u32[]{:S(2)}) %collective-permute-start.8) | collective-permute-done | bytes 65568 | tf_op jit(solution)/shard_map/ppermute | solution.py:18
  26.9 0.0 collective-permute-done.9
  26.9 0.6 %add_add_fusion = f32[128,128]{1,0:T(8,128)} fusion(f32[128,128]{1,0:T(8,128)S(1)} %collective-permute-done.9, f32[128,128]{1,0:T(8,128)S(1)} %collective-permute-done.8, f32[128,128]{1,0:T(8,128)S(1)} %get-tuple-element.27, f32[128,128]{1,0:T(8,128)S(1)} %collective-permute-done.7), kind=kLoop, calls=%fused_computation | loop fusion | flops 49152 | bytes 327680 | tf_op jit(solution)/shard_map/add | solution.py:128
Async XLA Ops:
  1.1 8.6 %collective-permute-start.3 = (bf16[32,1024]{1,0:T(8,128)(2,1)S(1)}, bf16[32,1024]{1,0:T(8,128)(2,1)S(1)}, u32[]{:S(2)}, u32[]{:S(2)}) collective-permute-start(bf16[32,1024]{1,0:T(8,128)(2,1)S(1)} %get-tuple-element.21), channel_id=1, source_target_pairs={{0,24},{8,16},{16,8},{24,0},{1,25},{9,17},{17,9},{25,1},{2,26},{10... | collective-permute-start | bytes 196616 | tf_op jit(solution)/shard_map/ppermute | solution.py:18
  6.2 8.9 %collective-permute-start.2 = (bf16[64,1024]{1,0:T(8,128)(2,1)S(1)}, bf16[64,1024]{1,0:T(8,128)(2,1)S(1)}, u32[]{:S(2)}, u32[]{:S(2)}) collective-permute-start(bf16[64,1024]{1,0:T(8,128)(2,1)S(1)} %get-tuple-element.20.refs_0_), channel_id=1, source_target_pairs={{0,6},{1,7},{2,4},{3,5},{4,2},{5,3},{6,0},{7,1},{8,14},{9,15},{10,... | collective-permute-start | bytes 393224 | tf_op jit(solution)/shard_map/ppermute | solution.py:18
  8.7 6.4 %collective-permute-start.1 = (bf16[64,1024]{1,0:T(8,128)(2,1)S(1)}, bf16[64,1024]{1,0:T(8,128)(2,1)S(1)}, u32[]{:S(2)}, u32[]{:S(2)}) collective-permute-start(bf16[64,1024]{1,0:T(8,128)(2,1)S(1)} %get-tuple-element.20.refs_0_), channel_id=1, source_target_pairs={{0,4},{1,5},{2,6},{3,7},{4,0},{5,1},{6,2},{7,3},{8,12},{9,13},{10,... | collective-permute-start | bytes 393224 | tf_op jit(solution)/shard_map/ppermute | solution.py:18
  9.2 5.9 %collective-permute-start = (bf16[64,1024]{1,0:T(8,128)(2,1)S(1)}, bf16[64,1024]{1,0:T(8,128)(2,1)S(1)}, u32[]{:S(2)}, u32[]{:S(2)}) collective-permute-start(bf16[64,1024]{1,0:T(8,128)(2,1)S(1)} %get-tuple-element.20.refs_0_), channel_id=1, source_target_pairs={{0,2},{1,3},{2,0},{3,1},{4,6},{5,7},{6,4},{7,5},{8,10},{9,11},{10,... | collective-permute-start | bytes 393224 | tf_op jit(solution)/shard_map/ppermute | solution.py:18
  9.7 5.4 %collective-permute-start.4 = (bf16[32,1024]{1,0:T(8,128)(2,1)S(1)}, bf16[32,1024]{1,0:T(8,128)(2,1)S(1)}, u32[]{:S(2)}, u32[]{:S(2)}) collective-permute-start(bf16[32,1024]{1,0:T(8,128)(2,1)S(1)} %get-tuple-element.22), channel_id=1, source_target_pairs={{0,16},{8,24},{16,0},{24,8},{1,17},{9,25},{17,1},{25,9},{2,18},{10... | collective-permute-start | bytes 196616 | tf_op jit(solution)/shard_map/ppermute | solution.py:18
  9.7 5.4 %collective-permute-start.5 = (bf16[32,1024]{1,0:T(8,128)(2,1)S(1)}, bf16[32,1024]{1,0:T(8,128)(2,1)S(1)}, u32[]{:S(2)}, u32[]{:S(2)}) collective-permute-start(bf16[32,1024]{1,0:T(8,128)(2,1)S(1)} %get-tuple-element.23), channel_id=1, source_target_pairs={{0,8},{8,0},{16,24},{24,16},{1,9},{9,1},{17,25},{25,17},{2,10},{10... | collective-permute-start | bytes 196616 | tf_op jit(solution)/shard_map/ppermute | solution.py:18
  15.2 2.0 %collective-permute-start.6 = (bf16[256,1024]{1,0:T(8,128)(2,1)S(1)}, bf16[256,1024]{1,0:T(8,128)(2,1)S(1)}, u32[]{:S(2)}, u32[]{:S(2)}) collective-permute-start(bf16[256,1024]{1,0:T(8,128)(2,1)S(1)} %get-tuple-element.26.near), channel_id=1, source_target_pairs={{0,1},{1,0},{2,3},{3,2},{4,5},{5,4},{6,7},{7,6},{8,9},{9,8},{10,11... | collective-permute-start | bytes 1572872 | tf_op jit(solution)/shard_map/ppermute | solution.py:18
  18.1 6.8 %collective-permute-start.7 = (f32[128,128]{1,0:T(8,128)S(1)}, f32[128,128]{1,0:T(8,128)S(1)}, u32[]{:S(2)}, u32[]{:S(2)}) collective-permute-start(f32[128,128]{1,0:T(8,128)S(1)} %get-tuple-element.28), channel_id=1, source_target_pairs={{0,24},{8,16},{16,8},{24,0},{1,25},{9,17},{17,9},{25,1},{2,26},{10... | collective-permute-start | bytes 196616 | tf_op jit(solution)/shard_map/ppermute | solution.py:18
  19.7 7.3 %collective-permute-start.8 = (f32[128,128]{1,0:T(8,128)S(1)}, f32[128,128]{1,0:T(8,128)S(1)}, u32[]{:S(2)}, u32[]{:S(2)}) collective-permute-start(f32[128,128]{1,0:T(8,128)S(1)} %get-tuple-element.29), channel_id=1, source_target_pairs={{0,16},{8,24},{16,0},{24,8},{1,17},{9,25},{17,1},{25,9},{2,18},{10... | collective-permute-start | bytes 196616 | tf_op jit(solution)/shard_map/ppermute | solution.py:18
  20.1 6.8 %collective-permute-start.9 = (f32[128,128]{1,0:T(8,128)S(1)}, f32[128,128]{1,0:T(8,128)S(1)}, u32[]{:S(2)}, u32[]{:S(2)}) collective-permute-start(f32[128,128]{1,0:T(8,128)S(1)} %get-tuple-element.30), channel_id=1, source_target_pairs={{0,8},{8,0},{16,24},{24,16},{1,9},{9,1},{17,25},{25,17},{2,10},{10... | collective-permute-start | bytes 196616 | tf_op jit(solution)/shard_map/ppermute | solution.py:18

commit v6 on v5

--- a/solution.py
+++ b/solution.py
@@ -10,6 +10,7 @@
 
 VMEM = pl.BlockSpec(memory_space=pltpu.VMEM)
 HBM = pl.BlockSpec(memory_space=pltpu.HBM)
+SCALE_ROWS = 16
 SMEM = pl.BlockSpec(memory_space=pltpu.SMEM)
 
 
@@ -101,17 +102,27 @@
     for step, out in zip(steps, outs):
         part = ordered[step * width:(step + 1) * width, :].T
         if step == 0:
-            part = part + residual_ref[...].reshape(part.shape)
-        out[...] = part
+            out[...] = part + residual_ref[...].reshape(part.shape)
+        else:
+            largest = jnp.max(jnp.abs(part), axis=0, keepdims=True)
+            power = jnp.clip(14.0 - jnp.ceil(jnp.log2(jnp.maximum(largest, 1e-36))), -60.0, 120.0)
+            out[:part.shape[0], :] = part * jnp.exp2(power)
+            out[part.shape[0]:, :] = jnp.broadcast_to(power, (SCALE_ROWS, part.shape[1]))
 
 
 def contract(steps, owner, residual, lhs, near_part, far):
     rows, ab = len(steps), 2 * far.shape[0]
-    part = jax.ShapeDtypeStruct((lhs.shape[0], ab // rows), jnp.float32)
+    outs = [
+        jax.ShapeDtypeStruct((lhs.shape[0] + (SCALE_ROWS if step else 0), ab // rows), jnp.float32) for step in steps]
     return call(
-        functools.partial(contract_kernel, steps), [part] * rows, [SMEM] + [VMEM] * 4,
+        functools.partial(contract_kernel, steps), outs, [SMEM] + [VMEM] * 4,
         [owner, residual, lhs, near_part, far], [pltpu.VMEM((ab, lhs.shape[0]), jnp.float32)],
     )
+
+
+def exchange_partial(part, step):
+    got = exchange(part.astype(jnp.float16), "row", step).astype(jnp.float32)
+    return got[:-SCALE_ROWS] * jnp.exp2(-got[-SCALE_ROWS:1 - SCALE_ROWS])
 
 
 def shards(amplitudes, integrals, panel_owner, residual_in):
@@ -124,8 +135,8 @@
     far = exchange(near, "col", 1)
     parts = contract(steps, owner, residual, lhs, contract_near(near, lhs), far)
     total = parts[-1]
-    for step, part in zip(steps[:-1], parts):
-        total = total + exchange(part, "row", step)
+    for step, part in zip(steps[-2::-1], parts[-2::-1]):
+        total = total + exchange_partial(part, step)
     return total.reshape(residual_in.shape)
 
 

time: 27.7 us -> 26 us (0.939)
  waiting for transfers between devices: 10.7 us -> 8.73 us
    ppermute x10, waiting for transfers between devices: 10.7 us -> 8.73 us  [exchange(): return lax.ppermute(value, axis, [(i, i ^ step) for i in range(n)])]
where the time goes in v6:
time: 26 us; the launch traced here: 25.8 us
  starting transfers between devices  13.8 us (53%)
  waiting for transfers between devices  8.73 us (34%)
  Pallas kernels  2.45 us (9%)
  other arithmetic  0.73 us (3%)
    ppermute x10, starting transfers between devices, exchange(): return lax.ppermute(value, axis, [(i, i ^ step) for i in range(n)])  13.8 us
    ppermute x10, waiting for transfers between devices, exchange(): return lax.ppermute(value, axis, [(i, i ^ step) for i in range(n)])  8.73 us
    pallas_call x4, Pallas kernels, call(): pl.pallas_call(kernel, out_shape=outs, in_specs=specs, out_specs=[VMEM] *...  2.45 us
    add x1, other arithmetic, shards(): total = total + exchange_partial(part, step)  0.65 us
  transfers between devices with their start and end apart: 10, of which 4 were waited for; matrix products, arithmetic and copies ran while one was open for 0% of the time, Pallas kernels for 1%

profile of v6, /device:TPU:0, one launch (start us, length us, event | category | flops | bytes accessed | tf_op | source)
XLA Modules:
  0.0 25.8 jit_solution(9189061010542723444)
XLA Ops:
  0.0 1.1 %shard_map.46 = (bf16[64,1024]{1,0:T(8,128)(2,1)S(1)}, f32[4,32,128]{2,1,0:T(8,128)S(1)}, s32[1,8]{1,0:T(1,128)S(1)}, bf16[32,1024]{1,0:T(8,128)(2,1)S(1)}, bf16...) custom-call(bf16[64,1024]{1,0:T(8,128)(2,1)} %panel_ref.1, ...), custom_call_target="tpu_custom_call" | custom-call | tf_op jit(solution)/shard_map/pallas_call | solution.py:28
  1.1 5.1 %collective-permute-start.3 = (bf16[32,1024]{1,0:T(8,128)(2,1)S(1)}, bf16[32,1024]{1,0:T(8,128)(2,1)S(1)}, u32[]{:S(2)}, u32[]{:S(2)}) collective-permute-start(bf16[32,1024]{1,0:T(8,128)(2,1)S(1)} %get-tuple-element.21), channel_id=1, source_target_pairs={{0,24},{8,16},{16,8},{24,0},{1,25},{9,17},{17,9},{25,1},{2,26},{10... | collective-permute-start | bytes 196616 | tf_op jit(solution)/shard_map/ppermute | solution.py:19
  6.2 2.4 %collective-permute-start.2 = (bf16[64,1024]{1,0:T(8,128)(2,1)S(1)}, bf16[64,1024]{1,0:T(8,128)(2,1)S(1)}, u32[]{:S(2)}, u32[]{:S(2)}) collective-permute-start(bf16[64,1024]{1,0:T(8,128)(2,1)S(1)} %get-tuple-element.20.refs_0_), channel_id=1, source_target_pairs={{0,6},{1,7},{2,4},{3,5},{4,2},{5,3},{6,0},{7,1},{8,14},{9,15},{10,... | collective-permute-start | bytes 393224 | tf_op jit(solution)/shard_map/ppermute | solution.py:19
  8.7 0.5 %collective-permute-start.1 = (bf16[64,1024]{1,0:T(8,128)(2,1)S(1)}, bf16[64,1024]{1,0:T(8,128)(2,1)S(1)}, u32[]{:S(2)}, u32[]{:S(2)}) collective-permute-start(bf16[64,1024]{1,0:T(8,128)(2,1)S(1)} %get-tuple-element.20.refs_0_), channel_id=1, source_target_pairs={{0,4},{1,5},{2,6},{3,7},{4,0},{5,1},{6,2},{7,3},{8,12},{9,13},{10,... | collective-permute-start | bytes 393224 | tf_op jit(solution)/shard_map/ppermute | solution.py:19
  9.2 0.5 %collective-permute-start = (bf16[64,1024]{1,0:T(8,128)(2,1)S(1)}, bf16[64,1024]{1,0:T(8,128)(2,1)S(1)}, u32[]{:S(2)}, u32[]{:S(2)}) collective-permute-start(bf16[64,1024]{1,0:T(8,128)(2,1)S(1)} %get-tuple-element.20.refs_0_), channel_id=1, source_target_pairs={{0,2},{1,3},{2,0},{3,1},{4,6},{5,7},{6,4},{7,5},{8,10},{9,11},{10,... | collective-permute-start | bytes 393224 | tf_op jit(solution)/shard_map/ppermute | solution.py:19
  9.7 0.0 collective-permute-start.4
  9.7 0.0 collective-permute-done.3.refs_4_
  9.7 0.6 %collective-permute-start.5 = (bf16[32,1024]{1,0:T(8,128)(2,1)S(1)}, bf16[32,1024]{1,0:T(8,128)(2,1)S(1)}, u32[]{:S(2)}, u32[]{:S(2)}) collective-permute-start(bf16[32,1024]{1,0:T(8,128)(2,1)S(1)} %get-tuple-element.23), channel_id=1, source_target_pairs={{0,8},{8,0},{16,24},{24,16},{1,9},{9,1},{17,25},{25,17},{2,10},{10... | collective-permute-start | bytes 196616 | tf_op jit(solution)/shard_map/ppermute | solution.py:19
  10.4 4.7 %collective-permute-done.4.refs_5_ = bf16[32,1024]{1,0:T(8,128)(2,1)S(1)} collective-permute-done((bf16[32,1024]{1,0:T(8,128)(2,1)S(1)}, bf16[32,1024]{1,0:T(8,128)(2,1)S(1)}, u32[]{:S(2)}, u32[]{:S(2)}) %collective-permute-start.4) | collective-permute-done | bytes 65568 | tf_op jit(solution)/shard_map/ppermute | solution.py:19
  15.1 0.0 collective-permute-done.5.refs_6_
  15.1 0.0 collective-permute-done.2.refs_3_
  15.1 0.0 collective-permute-done.1.refs_2_
  15.1 0.0 collective-permute-done.refs_1_
  15.1 0.1 shard_map.47
  15.2 0.1 collective-permute-start.6
  15.3 0.3 %shard_map.48.near_part = f32[256,128]{1,0:T(8,128)S(1)} custom-call(bf16[256,1024]{1,0:T(8,128)(2,1)S(1)} %get-tuple-element.26.near, bf16[128,1024]{1,0:T(8,128)(2,1)S(1)} %get-tuple-element.25.lhs), custom_call_target="tpu_custom_call" | custom-call | tf_op jit(solution)/shard_map/pallas_call | solution.py:28
  15.5 1.6 %collective-permute-done.6.far = bf16[256,1024]{1,0:T(8,128)(2,1)S(1)} collective-permute-done((bf16[256,1024]{1,0:T(8,128)(2,1)S(1)}, bf16[256,1024]{1,0:T(8,128)(2,1)S(1)}, u32[]{:S(2)}, u32[]{:S(2)}) %collective-permute-start.6) | collective-permute-done | bytes 524320 | tf_op jit(solution)/shard_map/ppermute | solution.py:19
  17.1 1.0 %shard_map.49 = (f32[144,128]{1,0:T(8,128)S(1)}, f32[144,128]{1,0:T(8,128)S(1)}, f32[144,128]{1,0:T(8,128)S(1)}, f32[128,128]{1,0:T(8,128)S(1)}) custom-call(s32[1,8]{1,0:T(1,128)S(1)} %get-tuple-element.18.owner_ref, f32[4,32,128]{2,1,0:T(8,128)S(1)} %get-tuple-element.19.residual_ref, bf16[128,1024]{1,0:T(8,128)(2,1)S(1)} %get-tuple-element.25.lhs, ...), custom_call_target="tpu_custom_call" | custom-call | tf_op jit(solution)/shard_map/pallas_call | solution.py:28
  18.2 1.5 %collective-permute-start.9 = (f16[144,128]{1,0:T(8,128)(2,1)S(1)}, f16[144,128]{1,0:T(8,128)(2,1)S(1)}, u32[]{:S(2)}, u32[]{:S(2)}) collective-permute-start(f16[144,128]{1,0:T(8,128)(2,1)S(1)} %convert_element_type.22), channel_id=1, source_target_pairs={{0,24},{8,16},{16,8},{24,0},{1,25},{9,17},{17,9},{25,1},{2,26},{10... | collective-permute-start | bytes 110600 | tf_op jit(solution)/shard_map/ppermute | solution.py:19
  19.7 0.4 %collective-permute-start.8 = (f16[144,128]{1,0:T(8,128)(2,1)S(1)}, f16[144,128]{1,0:T(8,128)(2,1)S(1)}, u32[]{:S(2)}, u32[]{:S(2)}) collective-permute-start(f16[144,128]{1,0:T(8,128)(2,1)S(1)} %convert_element_type.20), channel_id=1, source_target_pairs={{0,16},{8,24},{16,0},{24,8},{1,17},{9,25},{17,1},{25,9},{2,18},{10... | collective-permute-start | bytes 110600 | tf_op jit(solution)/shard_map/ppermute | solution.py:19
  20.2 2.6 %collective-permute-start.7 = (f16[144,128]{1,0:T(8,128)(2,1)S(1)}, f16[144,128]{1,0:T(8,128)(2,1)S(1)}, u32[]{:S(2)}, u32[]{:S(2)}) collective-permute-start(f16[144,128]{1,0:T(8,128)(2,1)S(1)} %convert_element_type.18), channel_id=1, source_target_pairs={{0,8},{8,0},{16,24},{24,16},{1,9},{9,1},{17,25},{25,17},{2,10},{10... | collective-permute-start | bytes 110600 | tf_op jit(solution)/shard_map/ppermute | solution.py:19
  22.7 1.6 %collective-permute-done.9 = f16[144,128]{1,0:T(8,128)(2,1)S(1)} collective-permute-done((f16[144,128]{1,0:T(8,128)(2,1)S(1)}, f16[144,128]{1,0:T(8,128)(2,1)S(1)}, u32[]{:S(2)}, u32[]{:S(2)}) %collective-permute-start.9) | collective-permute-done | bytes 36896 | tf_op jit(solution)/shard_map/ppermute | solution.py:19
  24.3 0.8 %collective-permute-done.8 = f16[144,128]{1,0:T(8,128)(2,1)S(1)} collective-permute-done((f16[144,128]{1,0:T(8,128)(2,1)S(1)}, f16[144,128]{1,0:T(8,128)(2,1)S(1)}, u32[]{:S(2)}, u32[]{:S(2)}) %collective-permute-start.8) | collective-permute-done | bytes 36896 | tf_op jit(solution)/shard_map/ppermute | solution.py:19
  25.1 0.0 collective-permute-done.7
  25.2 0.7 %fusion = f32[128,128]{1,0:T(8,128)} fusion(f32[144,128]{1,0:T(8,128)S(1)} %convert_element_type.23, f32[144,128]{1,0:T(8,128)S(1)} %convert_element_type.21, f32[128,128]{1,0:T(8,128)S(1)} %get-tuple-element.27, f32[144,128]{1,0:T(8,128)S(1)} %convert_element_type.19, f32[128]{0:T(128)S(1)} %fusion.5, f32[128]{0:T(128)S(1)} %fusion.8, f32[128]{0:T(128)S(1)} %fusion.11), kind=kLoop, calls=%fused_computation.1 | loop fusion | flops 98304 | bytes 329216 | tf_op jit(solution)/shard_map/add | solution.py:139
  (9 shorter events, 0.1 us)
Async XLA Ops:
  1.1 8.6 %collective-permute-start.3 = (bf16[32,1024]{1,0:T(8,128)(2,1)S(1)}, bf16[32,1024]{1,0:T(8,128)(2,1)S(1)}, u32[]{:S(2)}, u32[]{:S(2)}) collective-permute-start(bf16[32,1024]{1,0:T(8,128)(2,1)S(1)} %get-tuple-element.21), channel_id=1, source_target_pairs={{0,24},{8,16},{16,8},{24,0},{1,25},{9,17},{17,9},{25,1},{2,26},{10... | collective-permute-start | bytes 196616 | tf_op jit(solution)/shard_map/ppermute | solution.py:19
  6.2 8.9 %collective-permute-start.2 = (bf16[64,1024]{1,0:T(8,128)(2,1)S(1)}, bf16[64,1024]{1,0:T(8,128)(2,1)S(1)}, u32[]{:S(2)}, u32[]{:S(2)}) collective-permute-start(bf16[64,1024]{1,0:T(8,128)(2,1)S(1)} %get-tuple-element.20.refs_0_), channel_id=1, source_target_pairs={{0,6},{1,7},{2,4},{3,5},{4,2},{5,3},{6,0},{7,1},{8,14},{9,15},{10,... | collective-permute-start | bytes 393224 | tf_op jit(solution)/shard_map/ppermute | solution.py:19
  8.7 6.4 %collective-permute-start.1 = (bf16[64,1024]{1,0:T(8,128)(2,1)S(1)}, bf16[64,1024]{1,0:T(8,128)(2,1)S(1)}, u32[]{:S(2)}, u32[]{:S(2)}) collective-permute-start(bf16[64,1024]{1,0:T(8,128)(2,1)S(1)} %get-tuple-element.20.refs_0_), channel_id=1, source_target_pairs={{0,4},{1,5},{2,6},{3,7},{4,0},{5,1},{6,2},{7,3},{8,12},{9,13},{10,... | collective-permute-start | bytes 393224 | tf_op jit(solution)/shard_map/ppermute | solution.py:19
  9.2 5.9 %collective-permute-start = (bf16[64,1024]{1,0:T(8,128)(2,1)S(1)}, bf16[64,1024]{1,0:T(8,128)(2,1)S(1)}, u32[]{:S(2)}, u32[]{:S(2)}) collective-permute-start(bf16[64,1024]{1,0:T(8,128)(2,1)S(1)} %get-tuple-element.20.refs_0_), channel_id=1, source_target_pairs={{0,2},{1,3},{2,0},{3,1},{4,6},{5,7},{6,4},{7,5},{8,10},{9,11},{10,... | collective-permute-start | bytes 393224 | tf_op jit(solution)/shard_map/ppermute | solution.py:19
  9.7 5.4 %collective-permute-start.4 = (bf16[32,1024]{1,0:T(8,128)(2,1)S(1)}, bf16[32,1024]{1,0:T(8,128)(2,1)S(1)}, u32[]{:S(2)}, u32[]{:S(2)}) collective-permute-start(bf16[32,1024]{1,0:T(8,128)(2,1)S(1)} %get-tuple-element.22), channel_id=1, source_target_pairs={{0,16},{8,24},{16,0},{24,8},{1,17},{9,25},{17,1},{25,9},{2,18},{10... | collective-permute-start | bytes 196616 | tf_op jit(solution)/shard_map/ppermute | solution.py:19
  9.7 5.4 %collective-permute-start.5 = (bf16[32,1024]{1,0:T(8,128)(2,1)S(1)}, bf16[32,1024]{1,0:T(8,128)(2,1)S(1)}, u32[]{:S(2)}, u32[]{:S(2)}) collective-permute-start(bf16[32,1024]{1,0:T(8,128)(2,1)S(1)} %get-tuple-element.23), channel_id=1, source_target_pairs={{0,8},{8,0},{16,24},{24,16},{1,9},{9,1},{17,25},{25,17},{2,10},{10... | collective-permute-start | bytes 196616 | tf_op jit(solution)/shard_map/ppermute | solution.py:19
  15.2 2.0 %collective-permute-start.6 = (bf16[256,1024]{1,0:T(8,128)(2,1)S(1)}, bf16[256,1024]{1,0:T(8,128)(2,1)S(1)}, u32[]{:S(2)}, u32[]{:S(2)}) collective-permute-start(bf16[256,1024]{1,0:T(8,128)(2,1)S(1)} %get-tuple-element.26.near), channel_id=1, source_target_pairs={{0,1},{1,0},{2,3},{3,2},{4,5},{5,4},{6,7},{7,6},{8,9},{9,8},{10,11... | collective-permute-start | bytes 1572872 | tf_op jit(solution)/shard_map/ppermute | solution.py:19
  18.2 6.1 %collective-permute-start.9 = (f16[144,128]{1,0:T(8,128)(2,1)S(1)}, f16[144,128]{1,0:T(8,128)(2,1)S(1)}, u32[]{:S(2)}, u32[]{:S(2)}) collective-permute-start(f16[144,128]{1,0:T(8,128)(2,1)S(1)} %convert_element_type.22), channel_id=1, source_target_pairs={{0,24},{8,16},{16,8},{24,0},{1,25},{9,17},{17,9},{25,1},{2,26},{10... | collective-permute-start | bytes 110600 | tf_op jit(solution)/shard_map/ppermute | solution.py:19
  19.7 5.4 %collective-permute-start.8 = (f16[144,128]{1,0:T(8,128)(2,1)S(1)}, f16[144,128]{1,0:T(8,128)(2,1)S(1)}, u32[]{:S(2)}, u32[]{:S(2)}) collective-permute-start(f16[144,128]{1,0:T(8,128)(2,1)S(1)} %convert_element_type.20), channel_id=1, source_target_pairs={{0,16},{8,24},{16,0},{24,8},{1,17},{9,25},{17,1},{25,9},{2,18},{10... | collective-permute-start | bytes 110600 | tf_op jit(solution)/shard_map/ppermute | solution.py:19
  20.2 5.0 %collective-permute-start.7 = (f16[144,128]{1,0:T(8,128)(2,1)S(1)}, f16[144,128]{1,0:T(8,128)(2,1)S(1)}, u32[]{:S(2)}, u32[]{:S(2)}) collective-permute-start(f16[144,128]{1,0:T(8,128)(2,1)S(1)} %convert_element_type.18), channel_id=1, source_target_pairs={{0,8},{8,0},{16,24},{24,16},{1,9},{9,1},{17,25},{25,17},{2,10},{10... | collective-permute-start | bytes 110600 | tf_op jit(solution)/shard_map/ppermute | solution.py:19

commit v7 on v6

--- a/solution.py
+++ b/solution.py
@@ -11,7 +11,7 @@
 VMEM = pl.BlockSpec(memory_space=pltpu.VMEM)
 HBM = pl.BlockSpec(memory_space=pltpu.HBM)
 SCALE_ROWS = 16
-SMEM = pl.BlockSpec(memory_space=pltpu.SMEM)
+SWAPS = 2
 
 
 def exchange(value, axis, step):
@@ -57,48 +57,62 @@
 
 def assemble_kernel(steps, *refs):
     rows = len(steps)
-    panels, amps, (near, lhs) = refs[:-rows - 2], refs[-rows - 2:-2], refs[-2:]
+    count = len(refs) - rows - SWAPS - 1
+    panels, amps, nears, lhs = refs[:count], refs[count:count + rows], refs[count + rows:-1], refs[-1]
     height, pairs = panels[0].shape[0], amps[0].shape[0]
     row = lax.axis_index("row")
     for index, panel in enumerate(panels):
-        near[index * height:(index + 1) * height, :] = panel[...]
+        near, place = nears[index * SWAPS // count], index % (count // SWAPS)
+        near[place * height:(place + 1) * height, :] = panel[...]
     for step, amp in zip(steps, amps):
         at = pl.multiple_of((row ^ step) * pairs, pairs)
         lhs[pl.ds(at, pairs), :] = amp[...]
 
 
 def assemble(steps, panels, amps):
-    outs = [like(blocks[0], len(blocks) * blocks[0].shape[0], blocks[0].shape[1]) for blocks in (panels, amps)]
+    height, depth = panels[0].shape
+    outs = [like(panels[0], len(panels) // SWAPS * height, depth)] * SWAPS
+    outs.append(like(amps[0], len(amps) * amps[0].shape[0], depth))
     args = [*panels, *amps]
-    return call(functools.partial(assemble_kernel, steps), outs, [VMEM] * len(args), args)
+    *nears, lhs = call(functools.partial(assemble_kernel, steps), outs, [VMEM] * len(args), args)
+    return nears, lhs
 
 
 def product(panels, lhs):
     return lax.dot_general(panels[...], lhs[...], (((1,), (1,)), ((), ())), preferred_element_type=jnp.float32)
 
 
-def near_kernel(near, lhs, out):
-    out[...] = product(near, lhs)
+def product_kernel(lhs, *refs):
+    panels, out = refs[:-1], refs[-1]
+    height = panels[0].shape[0]
+    for index, panel in enumerate(panels):
+        out[index * height:(index + 1) * height, :] = product(panel, lhs)
 
 
-def contract_near(near, lhs):
-    out = jax.ShapeDtypeStruct((near.shape[0], lhs.shape[0]), jnp.float32)
-    return call(near_kernel, [out], [VMEM, VMEM], [near, lhs])[0]
+def products(lhs, panels):
+    out = jax.ShapeDtypeStruct((sum(panel.shape[0] for panel in panels), lhs.shape[0]), jnp.float32)
+    return call(product_kernel, [out], [VMEM] * (1 + len(panels)), [lhs, *panels])[0]
 
 
-def contract_kernel(steps, owner_ref, residual_ref, lhs, near_part, far, *refs):
+def contract_kernel(steps, owner_ref, residual_ref, lhs, near_part, far_part, last, *refs):
     outs, ordered = refs[:-1], refs[-1]
     width = outs[0].shape[1]
     row, col = lax.axis_index("row"), lax.axis_index("col")
-    columns = owner_ref.shape[1]
+    owner = owner_ref[...]
+    columns = owner.shape[1]
     height = ordered.shape[0] // columns
     per_row = width // height
-    for half, part in enumerate((near_part[...], product(far, lhs))):
-        for index in range(columns // 2):
-            owner = owner_ref[0, col ^ (2 * index + half)]
-            place = ((owner // per_row) ^ row) * per_row + owner % per_row
-            at = pl.multiple_of(place * height, height)
-            ordered[pl.ds(at, height), :] = part[index * height:(index + 1) * height, :]
+    places = (((owner // per_row) ^ row) * per_row + owner % per_row).astype(jnp.float32)
+    slots = lax.broadcasted_iota(jnp.int32, owner.shape, 1)
+    blocks = [(near_part, 2 * index, index) for index in range(columns // 2)]
+    blocks += [(far_part, 2 * index + 1, index) for index in range(far_part.shape[0] // height)]
+    done = len(blocks) - columns // 2
+    tail = product(last, lhs)
+    blocks += [(tail, 2 * index + 1, index - done) for index in range(done, columns // 2)]
+    for part, step, index in blocks:
+        place = jnp.sum(jnp.where(slots == (col ^ step), places, 0.0)).astype(jnp.int32)
+        at = pl.multiple_of(place * height, height)
+        ordered[pl.ds(at, height), :] = part[index * height:(index + 1) * height, :]
     for step, out in zip(steps, outs):
         part = ordered[step * width:(step + 1) * width, :].T
         if step == 0:
@@ -110,13 +124,14 @@
             out[part.shape[0]:, :] = jnp.broadcast_to(power, (SCALE_ROWS, part.shape[1]))
 
 
-def contract(steps, owner, residual, lhs, near_part, far):
-    rows, ab = len(steps), 2 * far.shape[0]
+def contract(steps, owner, residual, lhs, near_part, far_part, last):
+    rows, ab = len(steps), 2 * near_part.shape[0]
     outs = [
         jax.ShapeDtypeStruct((lhs.shape[0] + (SCALE_ROWS if step else 0), ab // rows), jnp.float32) for step in steps]
+    args = [owner, residual, lhs, near_part, far_part, last]
     return call(
-        functools.partial(contract_kernel, steps), outs, [SMEM] + [VMEM] * 4,
-        [owner, residual, lhs, near_part, far], [pltpu.VMEM((ab, lhs.shape[0]), jnp.float32)],
+        functools.partial(contract_kernel, steps), outs, [VMEM] * len(args), args,
+        [pltpu.VMEM((ab, lhs.shape[0]), jnp.float32)],
     )
 
 
@@ -131,9 +146,9 @@
     own, residual, owner, blocks = fetch(integrals, amplitudes, residual_in, panel_owner, rows)
     panels = [exchange(own, "col", step) if step else own for step in range(0, columns, 2)]
     amps = [exchange(blocks[step], "row", step) if step else blocks[0] for step in steps]
-    near, lhs = assemble(steps, panels, amps)
-    far = exchange(near, "col", 1)
-    parts = contract(steps, owner, residual, lhs, contract_near(near, lhs), far)
+    nears, lhs = assemble(steps, panels, amps)
+    *fars, last = [exchange(near, "col", 1) for near in nears]
+    parts = contract(steps, owner, residual, lhs, products(lhs, nears), products(lhs, fars), last)
     total = parts[-1]
     for step, part in zip(steps[-2::-1], parts[-2::-1]):
         total = total + exchange_partial(part, step)

time: 26 us -> 25.4 us (0.977)
  waiting for transfers between devices: 8.73 us -> 8 us
  starting transfers between devices: 13.8 us -> 14.3 us
  Pallas kernels: 2.45 us -> 2.07 us
    ppermute x10 -> x11, waiting for transfers between devices: 8.73 us -> 8 us  [exchange(): return lax.ppermute(value, axis, [(i, i ^ step) for i in range(n)])]
    ppermute x10 -> x11, starting transfers between devices: 13.8 us -> 14.3 us  [exchange(): return lax.ppermute(value, axis, [(i, i ^ step) for i in range(n)])]
    pallas_call x4 -> x5, Pallas kernels: 2.45 us -> 2.07 us  [call(): pl.pallas_call(kernel, out_shape=outs, in_specs=specs, out_specs=[VMEM] *...]
  transfers between devices with their start and end apart: 10 -> 11, of which waited for: 4 -> 5; matrix products, arithmetic and copies ran while one was open for 0% -> 0% of each run, Pallas kernels for 1% -> 2%
where the time goes in v7:
time: 25.4 us; the launch traced here: 25.2 us
  starting transfers between devices  14.3 us (56%)
  waiting for transfers between devices  8 us (31%)
  Pallas kernels  2.07 us (8%)
  other arithmetic  0.73 us (3%)
    ppermute x11, starting transfers between devices, exchange(): return lax.ppermute(value, axis, [(i, i ^ step) for i in range(n)])  14.3 us
    ppermute x11, waiting for transfers between devices, exchange(): return lax.ppermute(value, axis, [(i, i ^ step) for i in range(n)])  8 us
    pallas_call x5, Pallas kernels, call(): pl.pallas_call(kernel, out_shape=outs, in_specs=specs, out_specs=[VMEM] *...  2.07 us
    add x1, other arithmetic, shards(): total = total + exchange_partial(part, step)  0.65 us
  transfers between devices with their start and end apart: 11, of which 5 were waited for; matrix products, arithmetic and copies ran while one was open for 0% of the time, Pallas kernels for 2%

profile of v7, /device:TPU:0, one launch (start us, length us, event | category | flops | bytes accessed | tf_op | source)
XLA Modules:
  0.0 25.2 jit_solution(15278700502235486967)
XLA Ops:
  0.0 1.1 %shard_map.46 = (bf16[64,1024]{1,0:T(8,128)(2,1)S(1)}, f32[4,32,128]{2,1,0:T(8,128)S(1)}, s32[1,8]{1,0:T(1,128)S(1)}, bf16[32,1024]{1,0:T(8,128)(2,1)S(1)}, bf16...) custom-call(bf16[64,1024]{1,0:T(8,128)(2,1)} %panel_ref.1, ...), custom_call_target="tpu_custom_call" | custom-call | tf_op jit(solution)/shard_map/pallas_call | solution.py:28
  1.1 5.1 %collective-permute-start.3 = (bf16[32,1024]{1,0:T(8,128)(2,1)S(1)}, bf16[32,1024]{1,0:T(8,128)(2,1)S(1)}, u32[]{:S(2)}, u32[]{:S(2)}) collective-permute-start(bf16[32,1024]{1,0:T(8,128)(2,1)S(1)} %get-tuple-element.22), channel_id=1, source_target_pairs={{0,24},{8,16},{16,8},{24,0},{1,25},{9,17},{17,9},{25,1},{2,26},{10... | collective-permute-start | bytes 196616 | tf_op jit(solution)/shard_map/ppermute | solution.py:19
  6.2 2.4 %collective-permute-start.2 = (bf16[64,1024]{1,0:T(8,128)(2,1)S(1)}, bf16[64,1024]{1,0:T(8,128)(2,1)S(1)}, u32[]{:S(2)}, u32[]{:S(2)}) collective-permute-start(bf16[64,1024]{1,0:T(8,128)(2,1)S(1)} %get-tuple-element.21.refs_0_), channel_id=1, source_target_pairs={{0,6},{1,7},{2,4},{3,5},{4,2},{5,3},{6,0},{7,1},{8,14},{9,15},{10,... | collective-permute-start | bytes 393224 | tf_op jit(solution)/shard_map/ppermute | solution.py:19
  8.7 0.5 %collective-permute-start.1 = (bf16[64,1024]{1,0:T(8,128)(2,1)S(1)}, bf16[64,1024]{1,0:T(8,128)(2,1)S(1)}, u32[]{:S(2)}, u32[]{:S(2)}) collective-permute-start(bf16[64,1024]{1,0:T(8,128)(2,1)S(1)} %get-tuple-element.21.refs_0_), channel_id=1, source_target_pairs={{0,4},{1,5},{2,6},{3,7},{4,0},{5,1},{6,2},{7,3},{8,12},{9,13},{10,... | collective-permute-start | bytes 393224 | tf_op jit(solution)/shard_map/ppermute | solution.py:19
  9.2 0.5 %collective-permute-start = (bf16[64,1024]{1,0:T(8,128)(2,1)S(1)}, bf16[64,1024]{1,0:T(8,128)(2,1)S(1)}, u32[]{:S(2)}, u32[]{:S(2)}) collective-permute-start(bf16[64,1024]{1,0:T(8,128)(2,1)S(1)} %get-tuple-element.21.refs_0_), channel_id=1, source_target_pairs={{0,2},{1,3},{2,0},{3,1},{4,6},{5,7},{6,4},{7,5},{8,10},{9,11},{10,... | collective-permute-start | bytes 393224 | tf_op jit(solution)/shard_map/ppermute | solution.py:19
  9.7 0.0 collective-permute-start.4
  9.7 0.0 collective-permute-done.3.refs_4_
  9.7 0.6 %collective-permute-start.5 = (bf16[32,1024]{1,0:T(8,128)(2,1)S(1)}, bf16[32,1024]{1,0:T(8,128)(2,1)S(1)}, u32[]{:S(2)}, u32[]{:S(2)}) collective-permute-start(bf16[32,1024]{1,0:T(8,128)(2,1)S(1)} %get-tuple-element.24), channel_id=1, source_target_pairs={{0,8},{8,0},{16,24},{24,16},{1,9},{9,1},{17,25},{25,17},{2,10},{10... | collective-permute-start | bytes 196616 | tf_op jit(solution)/shard_map/ppermute | solution.py:19
  10.4 4.7 %collective-permute-done.4.refs_5_ = bf16[32,1024]{1,0:T(8,128)(2,1)S(1)} collective-permute-done((bf16[32,1024]{1,0:T(8,128)(2,1)S(1)}, bf16[32,1024]{1,0:T(8,128)(2,1)S(1)}, u32[]{:S(2)}, u32[]{:S(2)}) %collective-permute-start.4) | collective-permute-done | bytes 65568 | tf_op jit(solution)/shard_map/ppermute | solution.py:19
  15.1 0.0 collective-permute-done.5.refs_6_
  15.1 0.0 collective-permute-done.2.refs_3_
  15.1 0.0 collective-permute-done.1.refs_2_
  15.1 0.0 collective-permute-done.refs_1_
  15.1 0.1 shard_map.47
  15.2 0.1 collective-permute-start.6
  15.3 0.5 %collective-permute-start.7 = (bf16[128,1024]{1,0:T(8,128)(2,1)S(1)}, bf16[128,1024]{1,0:T(8,128)(2,1)S(1)}, u32[]{:S(2)}, u32[]{:S(2)}) collective-permute-start(bf16[128,1024]{1,0:T(8,128)(2,1)S(1)} %get-tuple-element.28.refs_1_), channel_id=1, source_target_pairs={{0,1},{1,0},{2,3},{3,2},{4,5},{5,4},{6,7},{7,6},{8,9},{9,8},{10,11... | collective-permute-start | bytes 786440 | tf_op jit(solution)/shard_map/ppermute | solution.py:19
  15.7 0.3 %shard_map.48.near_part = f32[256,128]{1,0:T(8,128)S(1)} custom-call(bf16[128,1024]{1,0:T(8,128)(2,1)S(1)} %get-tuple-element.26.lhs, bf16[128,1024]{1,0:T(8,128)(2,1)S(1)} %get-tuple-element.27.refs_0_, bf16[128,1024]{1,0:T(8,128)(2,1)S(1)} %get-tuple-element.28.refs_1_), custom_call_target="tpu_custom_call" | custom-call | tf_op jit(solution)/shard_map/pallas_call | solution.py:28
  16.1 0.7 %collective-permute-done.6.refs_0_ = bf16[128,1024]{1,0:T(8,128)(2,1)S(1)} collective-permute-done((bf16[128,1024]{1,0:T(8,128)(2,1)S(1)}, bf16[128,1024]{1,0:T(8,128)(2,1)S(1)}, u32[]{:S(2)}, u32[]{:S(2)}) %collective-permute-start.6) | collective-permute-done | bytes 262176 | tf_op jit(solution)/shard_map/ppermute | solution.py:19
  16.8 0.2 shard_map.49.far_part
  17.0 0.1 collective-permute-done.7.last
  17.1 0.4 %shard_map.50 = (f32[144,128]{1,0:T(8,128)S(1)}, f32[144,128]{1,0:T(8,128)S(1)}, f32[144,128]{1,0:T(8,128)S(1)}, f32[128,128]{1,0:T(8,128)S(1)}) custom-call(s32[1,8]{1,0:T(1,128)S(1)} %get-tuple-element.19.owner_ref, f32[4,32,128]{2,1,0:T(8,128)S(1)} %get-tuple-element.20.residual_ref, bf16[128,1024]{1,0:T(8,128)(2,1)S(1)} %get-tuple-element.26.lhs, ...), custom_call_target="tpu_custom_call" | custom-call | tf_op jit(solution)/shard_map/pallas_call | solution.py:28
  17.6 1.5 %collective-permute-start.10 = (f16[144,128]{1,0:T(8,128)(2,1)S(1)}, f16[144,128]{1,0:T(8,128)(2,1)S(1)}, u32[]{:S(2)}, u32[]{:S(2)}) collective-permute-start(f16[144,128]{1,0:T(8,128)(2,1)S(1)} %convert_element_type.22), channel_id=1, source_target_pairs={{0,24},{8,16},{16,8},{24,0},{1,25},{9,17},{17,9},{25,1},{2,26},{10... | collective-permute-start | bytes 110600 | tf_op jit(solution)/shard_map/ppermute | solution.py:19
  19.1 0.5 %collective-permute-start.9 = (f16[144,128]{1,0:T(8,128)(2,1)S(1)}, f16[144,128]{1,0:T(8,128)(2,1)S(1)}, u32[]{:S(2)}, u32[]{:S(2)}) collective-permute-start(f16[144,128]{1,0:T(8,128)(2,1)S(1)} %convert_element_type.20), channel_id=1, source_target_pairs={{0,16},{8,24},{16,0},{24,8},{1,17},{9,25},{17,1},{25,9},{2,18},{10... | collective-permute-start | bytes 110600 | tf_op jit(solution)/shard_map/ppermute | solution.py:19
  19.6 2.5 %collective-permute-start.8 = (f16[144,128]{1,0:T(8,128)(2,1)S(1)}, f16[144,128]{1,0:T(8,128)(2,1)S(1)}, u32[]{:S(2)}, u32[]{:S(2)}) collective-permute-start(f16[144,128]{1,0:T(8,128)(2,1)S(1)} %convert_element_type.18), channel_id=1, source_target_pairs={{0,8},{8,0},{16,24},{24,16},{1,9},{9,1},{17,25},{25,17},{2,10},{10... | collective-permute-start | bytes 110600 | tf_op jit(solution)/shard_map/ppermute | solution.py:19
  22.1 1.6 %collective-permute-done.10 = f16[144,128]{1,0:T(8,128)(2,1)S(1)} collective-permute-done((f16[144,128]{1,0:T(8,128)(2,1)S(1)}, f16[144,128]{1,0:T(8,128)(2,1)S(1)}, u32[]{:S(2)}, u32[]{:S(2)}) %collective-permute-start.10) | collective-permute-done | bytes 36896 | tf_op jit(solution)/shard_map/ppermute | solution.py:19
  23.7 0.8 %collective-permute-done.9 = f16[144,128]{1,0:T(8,128)(2,1)S(1)} collective-permute-done((f16[144,128]{1,0:T(8,128)(2,1)S(1)}, f16[144,128]{1,0:T(8,128)(2,1)S(1)}, u32[]{:S(2)}, u32[]{:S(2)}) %collective-permute-start.9) | collective-permute-done | bytes 36896 | tf_op jit(solution)/shard_map/ppermute | solution.py:19
  24.5 0.0 collective-permute-done.8
  24.6 0.7 %fusion = f32[128,128]{1,0:T(8,128)} fusion(f32[144,128]{1,0:T(8,128)S(1)} %convert_element_type.23, f32[144,128]{1,0:T(8,128)S(1)} %convert_element_type.21, f32[128,128]{1,0:T(8,128)S(1)} %get-tuple-element.29, f32[144,128]{1,0:T(8,128)S(1)} %convert_element_type.19, f32[128]{0:T(128)S(1)} %fusion.5, f32[128]{0:T(128)S(1)} %fusion.8, f32[128]{0:T(128)S(1)} %fusion.11), kind=kLoop, calls=%fused_computation.1 | loop fusion | flops 98304 | bytes 329216 | tf_op jit(solution)/shard_map/add | solution.py:154
  (9 shorter events, 0.1 us)
Async XLA Ops:
  1.1 8.6 %collective-permute-start.3 = (bf16[32,1024]{1,0:T(8,128)(2,1)S(1)}, bf16[32,1024]{1,0:T(8,128)(2,1)S(1)}, u32[]{:S(2)}, u32[]{:S(2)}) collective-permute-start(bf16[32,1024]{1,0:T(8,128)(2,1)S(1)} %get-tuple-element.22), channel_id=1, source_target_pairs={{0,24},{8,16},{16,8},{24,0},{1,25},{9,17},{17,9},{25,1},{2,26},{10... | collective-permute-start | bytes 196616 | tf_op jit(solution)/shard_map/ppermute | solution.py:19
  6.2 8.9 %collective-permute-start.2 = (bf16[64,1024]{1,0:T(8,128)(2,1)S(1)}, bf16[64,1024]{1,0:T(8,128)(2,1)S(1)}, u32[]{:S(2)}, u32[]{:S(2)}) collective-permute-start(bf16[64,1024]{1,0:T(8,128)(2,1)S(1)} %get-tuple-element.21.refs_0_), channel_id=1, source_target_pairs={{0,6},{1,7},{2,4},{3,5},{4,2},{5,3},{6,0},{7,1},{8,14},{9,15},{10,... | collective-permute-start | bytes 393224 | tf_op jit(solution)/shard_map/ppermute | solution.py:19
  8.7 6.4 %collective-permute-start.1 = (bf16[64,1024]{1,0:T(8,128)(2,1)S(1)}, bf16[64,1024]{1,0:T(8,128)(2,1)S(1)}, u32[]{:S(2)}, u32[]{:S(2)}) collective-permute-start(bf16[64,1024]{1,0:T(8,128)(2,1)S(1)} %get-tuple-element.21.refs_0_), channel_id=1, source_target_pairs={{0,4},{1,5},{2,6},{3,7},{4,0},{5,1},{6,2},{7,3},{8,12},{9,13},{10,... | collective-permute-start | bytes 393224 | tf_op jit(solution)/shard_map/ppermute | solution.py:19
  9.2 5.9 %collective-permute-start = (bf16[64,1024]{1,0:T(8,128)(2,1)S(1)}, bf16[64,1024]{1,0:T(8,128)(2,1)S(1)}, u32[]{:S(2)}, u32[]{:S(2)}) collective-permute-start(bf16[64,1024]{1,0:T(8,128)(2,1)S(1)} %get-tuple-element.21.refs_0_), channel_id=1, source_target_pairs={{0,2},{1,3},{2,0},{3,1},{4,6},{5,7},{6,4},{7,5},{8,10},{9,11},{10,... | collective-permute-start | bytes 393224 | tf_op jit(solution)/shard_map/ppermute | solution.py:19
  9.7 5.4 %collective-permute-start.4 = (bf16[32,1024]{1,0:T(8,128)(2,1)S(1)}, bf16[32,1024]{1,0:T(8,128)(2,1)S(1)}, u32[]{:S(2)}, u32[]{:S(2)}) collective-permute-start(bf16[32,1024]{1,0:T(8,128)(2,1)S(1)} %get-tuple-element.23), channel_id=1, source_target_pairs={{0,16},{8,24},{16,0},{24,8},{1,17},{9,25},{17,1},{25,9},{2,18},{10... | collective-permute-start | bytes 196616 | tf_op jit(solution)/shard_map/ppermute | solution.py:19
  9.7 5.4 %collective-permute-start.5 = (bf16[32,1024]{1,0:T(8,128)(2,1)S(1)}, bf16[32,1024]{1,0:T(8,128)(2,1)S(1)}, u32[]{:S(2)}, u32[]{:S(2)}) collective-permute-start(bf16[32,1024]{1,0:T(8,128)(2,1)S(1)} %get-tuple-element.24), channel_id=1, source_target_pairs={{0,8},{8,0},{16,24},{24,16},{1,9},{9,1},{17,25},{25,17},{2,10},{10... | collective-permute-start | bytes 196616 | tf_op jit(solution)/shard_map/ppermute | solution.py:19
  15.2 1.6 %collective-permute-start.6 = (bf16[128,1024]{1,0:T(8,128)(2,1)S(1)}, bf16[128,1024]{1,0:T(8,128)(2,1)S(1)}, u32[]{:S(2)}, u32[]{:S(2)}) collective-permute-start(bf16[128,1024]{1,0:T(8,128)(2,1)S(1)} %get-tuple-element.27.refs_0_), channel_id=1, source_target_pairs={{0,1},{1,0},{2,3},{3,2},{4,5},{5,4},{6,7},{7,6},{8,9},{9,8},{10,11... | collective-permute-start | bytes 786440 | tf_op jit(solution)/shard_map/ppermute | solution.py:19
  15.3 1.9 %collective-permute-start.7 = (bf16[128,1024]{1,0:T(8,128)(2,1)S(1)}, bf16[128,1024]{1,0:T(8,128)(2,1)S(1)}, u32[]{:S(2)}, u32[]{:S(2)}) collective-permute-start(bf16[128,1024]{1,0:T(8,128)(2,1)S(1)} %get-tuple-element.28.refs_1_), channel_id=1, source_target_pairs={{0,1},{1,0},{2,3},{3,2},{4,5},{5,4},{6,7},{7,6},{8,9},{9,8},{10,11... | collective-permute-start | bytes 786440 | tf_op jit(solution)/shard_map/ppermute | solution.py:19
  17.6 6.1 %collective-permute-start.10 = (f16[144,128]{1,0:T(8,128)(2,1)S(1)}, f16[144,128]{1,0:T(8,128)(2,1)S(1)}, u32[]{:S(2)}, u32[]{:S(2)}) collective-permute-start(f16[144,128]{1,0:T(8,128)(2,1)S(1)} %convert_element_type.22), channel_id=1, source_target_pairs={{0,24},{8,16},{16,8},{24,0},{1,25},{9,17},{17,9},{25,1},{2,26},{10... | collective-permute-start | bytes 110600 | tf_op jit(solution)/shard_map/ppermute | solution.py:19
  19.1 5.4 %collective-permute-start.9 = (f16[144,128]{1,0:T(8,128)(2,1)S(1)}, f16[144,128]{1,0:T(8,128)(2,1)S(1)}, u32[]{:S(2)}, u32[]{:S(2)}) collective-permute-start(f16[144,128]{1,0:T(8,128)(2,1)S(1)} %convert_element_type.20), channel_id=1, source_target_pairs={{0,16},{8,24},{16,0},{24,8},{1,17},{9,25},{17,1},{25,9},{2,18},{10... | collective-permute-start | bytes 110600 | tf_op jit(solution)/shard_map/ppermute | solution.py:19
  19.6 5.0 %collective-permute-start.8 = (f16[144,128]{1,0:T(8,128)(2,1)S(1)}, f16[144,128]{1,0:T(8,128)(2,1)S(1)}, u32[]{:S(2)}, u32[]{:S(2)}) collective-permute-start(f16[144,128]{1,0:T(8,128)(2,1)S(1)} %convert_element_type.18), channel_id=1, source_target_pairs={{0,8},{8,0},{16,24},{24,16},{1,9},{9,1},{17,25},{25,17},{2,10},{10... | collective-permute-start | bytes 110600 | tf_op jit(solution)/shard_map/ppermute | solution.py:19

commit v8 on v7

--- a/solution.py
+++ b/solution.py
@@ -23,22 +23,15 @@
     return jax.ShapeDtypeStruct(shape or array.shape, array.dtype)
 
 
-def call(kernel, outs, specs, args, scratch=(), semaphores=()):
+def call(kernel, outs, specs, args, scratch=(), semaphores=(), cost=None):
     size = sum(math.prod(x.shape) * jnp.dtype(x.dtype).itemsize for x in [*outs, *args, *scratch])
     return pl.pallas_call(
         kernel, out_shape=outs, in_specs=specs, out_specs=[VMEM] * len(outs), scratch_shapes=[*scratch, *semaphores],
-        compiler_params=pltpu.CompilerParams(vmem_limit_bytes=size + (2 << 20)),
+        compiler_params=pltpu.CompilerParams(vmem_limit_bytes=size + (2 << 20)), cost_estimate=cost,
     )(*args)
 
 
-def fetch_kernel(panel_ref, amp_ref, residual_ref, owner_ref, *refs):
-    panel, residual, owner, blocks, sems = refs[0], refs[1], refs[2], refs[3:-1], refs[-1]
-    width = blocks[0].shape[-1]
-    row = lax.axis_index("row")
-    pairs = [(panel_ref, panel), (residual_ref, residual), (owner_ref, owner)]
-    for step, block in enumerate(blocks):
-        at = pl.multiple_of((row ^ step) * width, width)
-        pairs.append((amp_ref.at[0, :, pl.ds(at, width)], block))
+def copy_all(pairs, sems):
     copies = [pltpu.make_async_copy(source, target, sems.at[i]) for i, (source, target) in enumerate(pairs)]
     for copy in copies:
         copy.start()
@@ -46,17 +39,44 @@
         copy.wait()
 
 
-def fetch(integrals, amplitudes, residual, owner, rows):
-    _, pairs, kw = amplitudes.shape
-    outs = [like(integrals), like(residual), like(owner)] + [like(amplitudes, pairs, kw // rows)] * rows
-    args = [pltpu.with_memory_space_constraint(x, pltpu.HBM) for x in (integrals, amplitudes, residual, owner)]
-    panel, residual, owner, *blocks = call(
-        fetch_kernel, outs, [HBM] * 4, args, semaphores=[pltpu.SemaphoreType.DMA((len(outs),))])
-    return panel, residual, owner, blocks
+def fetch_kernel(panel_ref, amp_ref, panel, *refs):
+    blocks, sems = refs[:-1], refs[-1]
+    width = blocks[0].shape[-1]
+    row = lax.axis_index("row")
+    pairs = [(panel_ref, panel)]
+    for step, block in enumerate(blocks):
+        at = pl.multiple_of((row ^ step) * width, width)
+        pairs.append((amp_ref.at[0, :, pl.ds(at, width)], block))
+    copy_all(pairs, sems)
 
 
-def assemble_kernel(steps, *refs):
-    rows = len(steps)
+def in_hbm(*arrays):
+    return [pltpu.with_memory_space_constraint(x, pltpu.HBM) for x in arrays]
+
+
+def fetch(integrals, amplitudes, rows):
+    _, pairs, kw = amplitudes.shape
+    outs = [like(integrals)] + [like(amplitudes, pairs, kw // rows)] * rows
+    panel, *blocks = call(
+        fetch_kernel, outs, [HBM] * 2, in_hbm(integrals, amplitudes), semaphores=[pltpu.SemaphoreType.DMA((len(outs),))])
+    return panel, blocks
+
+
+def fetch_late_kernel(residual_ref, owner_ref, residual, owner, sems):
+    copy_all([(residual_ref, residual), (owner_ref, owner)], sems)
+
+
+def fetch_late(residual, owner):
+    cost = pl.CostEstimate(flops=0, bytes_accessed=16 << 20, transcendentals=0)
+    return call(
+        fetch_late_kernel, [like(residual), like(owner)], [HBM] * 2, in_hbm(residual, owner),
+        semaphores=[pltpu.SemaphoreType.DMA((2,))], cost=cost)
+
+
+def assemble_kernel(steps, residual_ref, owner_ref, *refs):
+    rows, (residual, owner), refs = len(steps), refs[-2:], refs[:-2]
+    residual[...] = residual_ref[...]
+    owner[...] = owner_ref[...]
     count = len(refs) - rows - SWAPS - 1
     panels, amps, nears, lhs = refs[:count], refs[count:count + rows], refs[count + rows:-1], refs[-1]
     height, pairs = panels[0].shape[0], amps[0].shape[0]
@@ -69,13 +89,13 @@
         lhs[pl.ds(at, pairs), :] = amp[...]
 
 
-def assemble(steps, panels, amps):
+def assemble(steps, residual, owner, panels, amps):
     height, depth = panels[0].shape
     outs = [like(panels[0], len(panels) // SWAPS * height, depth)] * SWAPS
-    outs.append(like(amps[0], len(amps) * amps[0].shape[0], depth))
-    args = [*panels, *amps]
-    *nears, lhs = call(functools.partial(assemble_kernel, steps), outs, [VMEM] * len(args), args)
-    return nears, lhs
+    outs += [like(amps[0], len(amps) * amps[0].shape[0], depth), like(residual), like(owner)]
+    args = [residual, owner, *panels, *amps]
+    *nears, lhs, residual, owner = call(functools.partial(assemble_kernel, steps), outs, [VMEM] * len(args), args)
+    return nears, lhs, residual, owner
 
 
 def product(panels, lhs):
@@ -143,10 +163,11 @@
 def shards(amplitudes, integrals, panel_owner, residual_in):
     rows, columns = lax.axis_size("row"), lax.axis_size("col")
     steps = tuple(range(rows - 1, -1, -1))
-    own, residual, owner, blocks = fetch(integrals, amplitudes, residual_in, panel_owner, rows)
+    own, blocks = fetch(integrals, amplitudes, rows)
+    residual, owner = fetch_late(residual_in, panel_owner)
     panels = [exchange(own, "col", step) if step else own for step in range(0, columns, 2)]
     amps = [exchange(blocks[step], "row", step) if step else blocks[0] for step in steps]
-    nears, lhs = assemble(steps, panels, amps)
+    nears, lhs, residual, owner = assemble(steps, residual, owner, panels, amps)
     *fars, last = [exchange(near, "col", 1) for near in nears]
     parts = contract(steps, owner, residual, lhs, products(lhs, nears), products(lhs, fars), last)
     total = parts[-1]

time: 25.4 us -> 25.4 us (level)
  waiting for transfers between devices: 8 us -> 7.14 us
  Pallas kernels: 2.07 us -> 2.87 us
    ppermute x11, waiting for transfers between devices: 8 us -> 7.14 us  [exchange(): return lax.ppermute(value, axis, [(i, i ^ step) for i in range(n)])]
    pallas_call x5 -> x6, Pallas kernels: 2.07 us -> 2.87 us  [call(): pl.pallas_call(kernel, out_shape=outs, in_specs=specs, out_specs=[VMEM] *...]
  transfers between devices with their start and end apart: 11 -> 11, of which waited for: 5 -> 5; matrix products, arithmetic and copies ran while one was open for 0% -> 0% of each run, Pallas kernels for 2% -> 5%
where the time goes in v8:
time: 25.4 us; the launch traced here: 25.2 us
  starting transfers between devices  14.3 us (56%)
  waiting for transfers between devices  7.14 us (28%)
  Pallas kernels  2.87 us (11%)
  other arithmetic  0.73 us (3%)
    ppermute x11, starting transfers between devices, exchange(): return lax.ppermute(value, axis, [(i, i ^ step) for i in range(n)])  14.3 us
    ppermute x11, waiting for transfers between devices, exchange(): return lax.ppermute(value, axis, [(i, i ^ step) for i in range(n)])  7.14 us
    pallas_call x6, Pallas kernels, call(): pl.pallas_call(kernel, out_shape=outs, in_specs=specs, out_specs=[VMEM] *...  2.87 us
    add x1, other arithmetic, shards(): total = total + exchange_partial(part, step)  0.65 us
  transfers between devices with their start and end apart: 11, of which 5 were waited for; matrix products, arithmetic and copies ran while one was open for 0% of the time, Pallas kernels for 5%

profile of v8, /device:TPU:0, one launch (start us, length us, event | category | flops | bytes accessed | tf_op | source)
XLA Modules:
  0.0 25.2 jit_solution(3256002843875224700)
XLA Ops:
  0.0 1.0 %shard_map.47 = (bf16[64,1024]{1,0:T(8,128)(2,1)S(1)}, bf16[32,1024]{1,0:T(8,128)(2,1)S(1)}, bf16[32,1024]{1,0:T(8,128)(2,1)S(1)}, bf16[32,1024]{1,0:T(8,128)(2,1)S(1)}, bf16[32,1024]{1,0:T(8,128)(2,1)S(1)}) custom-call(bf16[64,1024]{1,0:T(8,128)(2,1)} %panel_ref.1, bf16[1,32,4096]{2,1,0:T(8,128)(2,1)} %amp_ref.1), custom_call_target="tpu_custom_call" | custom-call | tf_op jit(solution)/shard_map/pallas_call | solution.py:28
  1.0 5.1 %collective-permute-start.3 = (bf16[32,1024]{1,0:T(8,128)(2,1)S(1)}, bf16[32,1024]{1,0:T(8,128)(2,1)S(1)}, u32[]{:S(2)}, u32[]{:S(2)}) collective-permute-start(bf16[32,1024]{1,0:T(8,128)(2,1)S(1)} %get-tuple-element.24), channel_id=1, source_target_pairs={{0,24},{8,16},{16,8},{24,0},{1,25},{9,17},{17,9},{25,1},{2,26},{10... | collective-permute-start | bytes 196616 | tf_op jit(solution)/shard_map/ppermute | solution.py:19
  6.2 2.4 %collective-permute-start.2 = (bf16[64,1024]{1,0:T(8,128)(2,1)S(1)}, bf16[64,1024]{1,0:T(8,128)(2,1)S(1)}, u32[]{:S(2)}, u32[]{:S(2)}) collective-permute-start(bf16[64,1024]{1,0:T(8,128)(2,1)S(1)} %get-tuple-element.23.refs_0_), channel_id=1, source_target_pairs={{0,6},{1,7},{2,4},{3,5},{4,2},{5,3},{6,0},{7,1},{8,14},{9,15},{10,... | collective-permute-start | bytes 393224 | tf_op jit(solution)/shard_map/ppermute | solution.py:19
  8.6 0.5 %collective-permute-start.1 = (bf16[64,1024]{1,0:T(8,128)(2,1)S(1)}, bf16[64,1024]{1,0:T(8,128)(2,1)S(1)}, u32[]{:S(2)}, u32[]{:S(2)}) collective-permute-start(bf16[64,1024]{1,0:T(8,128)(2,1)S(1)} %get-tuple-element.23.refs_0_), channel_id=1, source_target_pairs={{0,4},{1,5},{2,6},{3,7},{4,0},{5,1},{6,2},{7,3},{8,12},{9,13},{10,... | collective-permute-start | bytes 393224 | tf_op jit(solution)/shard_map/ppermute | solution.py:19
  9.1 0.5 %collective-permute-start = (bf16[64,1024]{1,0:T(8,128)(2,1)S(1)}, bf16[64,1024]{1,0:T(8,128)(2,1)S(1)}, u32[]{:S(2)}, u32[]{:S(2)}) collective-permute-start(bf16[64,1024]{1,0:T(8,128)(2,1)S(1)} %get-tuple-element.23.refs_0_), channel_id=1, source_target_pairs={{0,2},{1,3},{2,0},{3,1},{4,6},{5,7},{6,4},{7,5},{8,10},{9,11},{10,... | collective-permute-start | bytes 393224 | tf_op jit(solution)/shard_map/ppermute | solution.py:19
  9.7 0.0 collective-permute-start.4
  9.7 0.0 collective-permute-done.3.refs_4_
  9.7 0.6 %collective-permute-start.5 = (bf16[32,1024]{1,0:T(8,128)(2,1)S(1)}, bf16[32,1024]{1,0:T(8,128)(2,1)S(1)}, u32[]{:S(2)}, u32[]{:S(2)}) collective-permute-start(bf16[32,1024]{1,0:T(8,128)(2,1)S(1)} %get-tuple-element.26), channel_id=1, source_target_pairs={{0,8},{8,0},{16,24},{24,16},{1,9},{9,1},{17,25},{25,17},{2,10},{10... | collective-permute-start | bytes 196616 | tf_op jit(solution)/shard_map/ppermute | solution.py:19
  10.3 0.9 %shard_map.46 = (f32[4,32,128]{2,1,0:T(8,128)S(1)}, s32[1,8]{1,0:T(1,128)S(1)}) custom-call(f32[4,32,128]{2,1,0:T(8,128)} %residual_ref.1, s32[1,8]{1,0:T(1,128)} %owner_ref.1), custom_call_target="tpu_custom_call" | custom-call | bytes 16777216 | tf_op jit(solution)/shard_map/pallas_call | solution.py:28
  11.2 3.9 %collective-permute-done.4.refs_5_ = bf16[32,1024]{1,0:T(8,128)(2,1)S(1)} collective-permute-done((bf16[32,1024]{1,0:T(8,128)(2,1)S(1)}, bf16[32,1024]{1,0:T(8,128)(2,1)S(1)}, u32[]{:S(2)}, u32[]{:S(2)}) %collective-permute-start.4) | collective-permute-done | bytes 65568 | tf_op jit(solution)/shard_map/ppermute | solution.py:19
  15.0 0.0 collective-permute-done.5.refs_6_
  15.0 0.0 collective-permute-done.2.refs_3_
  15.0 0.0 collective-permute-done.1.refs_2_
  15.0 0.0 collective-permute-done.refs_1_
  15.0 0.1 shard_map.48
  15.1 0.1 collective-permute-start.6
  15.2 0.5 %collective-permute-start.7 = (bf16[128,1024]{1,0:T(8,128)(2,1)S(1)}, bf16[128,1024]{1,0:T(8,128)(2,1)S(1)}, u32[]{:S(2)}, u32[]{:S(2)}) collective-permute-start(bf16[128,1024]{1,0:T(8,128)(2,1)S(1)} %get-tuple-element.32.refs_1_), channel_id=1, source_target_pairs={{0,1},{1,0},{2,3},{3,2},{4,5},{5,4},{6,7},{7,6},{8,9},{9,8},{10,11... | collective-permute-start | bytes 786440 | tf_op jit(solution)/shard_map/ppermute | solution.py:19
  15.7 0.3 %shard_map.49.near_part = f32[256,128]{1,0:T(8,128)S(1)} custom-call(bf16[128,1024]{1,0:T(8,128)(2,1)S(1)} %get-tuple-element.30.lhs, bf16[128,1024]{1,0:T(8,128)(2,1)S(1)} %get-tuple-element.31.refs_0_, bf16[128,1024]{1,0:T(8,128)(2,1)S(1)} %get-tuple-element.32.refs_1_), custom_call_target="tpu_custom_call" | custom-call | tf_op jit(solution)/shard_map/pallas_call | solution.py:28
  16.0 0.7 %collective-permute-done.6.refs_0_ = bf16[128,1024]{1,0:T(8,128)(2,1)S(1)} collective-permute-done((bf16[128,1024]{1,0:T(8,128)(2,1)S(1)}, bf16[128,1024]{1,0:T(8,128)(2,1)S(1)}, u32[]{:S(2)}, u32[]{:S(2)}) %collective-permute-start.6) | collective-permute-done | bytes 262176 | tf_op jit(solution)/shard_map/ppermute | solution.py:19
  16.7 0.2 shard_map.50.far_part
  16.9 0.1 collective-permute-done.7.last
  17.1 0.4 %shard_map.51 = (f32[144,128]{1,0:T(8,128)S(1)}, f32[144,128]{1,0:T(8,128)S(1)}, f32[144,128]{1,0:T(8,128)S(1)}, f32[128,128]{1,0:T(8,128)S(1)}) custom-call(s32[1,8]{1,0:T(1,128)S(1)} %get-tuple-element.28.owner_ref, f32[4,32,128]{2,1,0:T(8,128)S(1)} %get-tuple-element.29.residual_ref, bf16[128,1024]{1,0:T(8,128)(2,1)S(1)} %get-tuple-element.30.lhs, ...), custom_call_target="tpu_custom_call" | custom-call | tf_op jit(solution)/shard_map/pallas_call | solution.py:28
  17.5 1.5 %collective-permute-start.10 = (f16[144,128]{1,0:T(8,128)(2,1)S(1)}, f16[144,128]{1,0:T(8,128)(2,1)S(1)}, u32[]{:S(2)}, u32[]{:S(2)}) collective-permute-start(f16[144,128]{1,0:T(8,128)(2,1)S(1)} %convert_element_type.22), channel_id=1, source_target_pairs={{0,24},{8,16},{16,8},{24,0},{1,25},{9,17},{17,9},{25,1},{2,26},{10... | collective-permute-start | bytes 110600 | tf_op jit(solution)/shard_map/ppermute | solution.py:19
  19.1 0.5 %collective-permute-start.9 = (f16[144,128]{1,0:T(8,128)(2,1)S(1)}, f16[144,128]{1,0:T(8,128)(2,1)S(1)}, u32[]{:S(2)}, u32[]{:S(2)}) collective-permute-start(f16[144,128]{1,0:T(8,128)(2,1)S(1)} %convert_element_type.20), channel_id=1, source_target_pairs={{0,16},{8,24},{16,0},{24,8},{1,17},{9,25},{17,1},{25,9},{2,18},{10... | collective-permute-start | bytes 110600 | tf_op jit(solution)/shard_map/ppermute | solution.py:19
  19.5 2.5 %collective-permute-start.8 = (f16[144,128]{1,0:T(8,128)(2,1)S(1)}, f16[144,128]{1,0:T(8,128)(2,1)S(1)}, u32[]{:S(2)}, u32[]{:S(2)}) collective-permute-start(f16[144,128]{1,0:T(8,128)(2,1)S(1)} %convert_element_type.18), channel_id=1, source_target_pairs={{0,8},{8,0},{16,24},{24,16},{1,9},{9,1},{17,25},{25,17},{2,10},{10... | collective-permute-start | bytes 110600 | tf_op jit(solution)/shard_map/ppermute | solution.py:19
  22.0 1.6 %collective-permute-done.10 = f16[144,128]{1,0:T(8,128)(2,1)S(1)} collective-permute-done((f16[144,128]{1,0:T(8,128)(2,1)S(1)}, f16[144,128]{1,0:T(8,128)(2,1)S(1)}, u32[]{:S(2)}, u32[]{:S(2)}) %collective-permute-start.10) | collective-permute-done | bytes 36896 | tf_op jit(solution)/shard_map/ppermute | solution.py:19
  23.6 0.8 %collective-permute-done.9 = f16[144,128]{1,0:T(8,128)(2,1)S(1)} collective-permute-done((f16[144,128]{1,0:T(8,128)(2,1)S(1)}, f16[144,128]{1,0:T(8,128)(2,1)S(1)}, u32[]{:S(2)}, u32[]{:S(2)}) %collective-permute-start.9) | collective-permute-done | bytes 36896 | tf_op jit(solution)/shard_map/ppermute | solution.py:19
  24.5 0.0 collective-permute-done.8
  24.5 0.7 %fusion = f32[128,128]{1,0:T(8,128)} fusion(f32[144,128]{1,0:T(8,128)S(1)} %convert_element_type.23, f32[144,128]{1,0:T(8,128)S(1)} %convert_element_type.21, f32[128,128]{1,0:T(8,128)S(1)} %get-tuple-element.33, f32[144,128]{1,0:T(8,128)S(1)} %convert_element_type.19, f32[128]{0:T(128)S(1)} %fusion.5, f32[128]{0:T(128)S(1)} %fusion.8, f32[128]{0:T(128)S(1)} %fusion.11), kind=kLoop, calls=%fused_computation.1 | loop fusion | flops 98304 | bytes 329216 | tf_op jit(solution)/shard_map/add | solution.py:175
  (9 shorter events, 0.1 us)
Async XLA Ops:
  1.0 8.6 %collective-permute-start.3 = (bf16[32,1024]{1,0:T(8,128)(2,1)S(1)}, bf16[32,1024]{1,0:T(8,128)(2,1)S(1)}, u32[]{:S(2)}, u32[]{:S(2)}) collective-permute-start(bf16[32,1024]{1,0:T(8,128)(2,1)S(1)} %get-tuple-element.24), channel_id=1, source_target_pairs={{0,24},{8,16},{16,8},{24,0},{1,25},{9,17},{17,9},{25,1},{2,26},{10... | collective-permute-start | bytes 196616 | tf_op jit(solution)/shard_map/ppermute | solution.py:19
  6.2 8.9 %collective-permute-start.2 = (bf16[64,1024]{1,0:T(8,128)(2,1)S(1)}, bf16[64,1024]{1,0:T(8,128)(2,1)S(1)}, u32[]{:S(2)}, u32[]{:S(2)}) collective-permute-start(bf16[64,1024]{1,0:T(8,128)(2,1)S(1)} %get-tuple-element.23.refs_0_), channel_id=1, source_target_pairs={{0,6},{1,7},{2,4},{3,5},{4,2},{5,3},{6,0},{7,1},{8,14},{9,15},{10,... | collective-permute-start | bytes 393224 | tf_op jit(solution)/shard_map/ppermute | solution.py:19
  8.6 6.4 %collective-permute-start.1 = (bf16[64,1024]{1,0:T(8,128)(2,1)S(1)}, bf16[64,1024]{1,0:T(8,128)(2,1)S(1)}, u32[]{:S(2)}, u32[]{:S(2)}) collective-permute-start(bf16[64,1024]{1,0:T(8,128)(2,1)S(1)} %get-tuple-element.23.refs_0_), channel_id=1, source_target_pairs={{0,4},{1,5},{2,6},{3,7},{4,0},{5,1},{6,2},{7,3},{8,12},{9,13},{10,... | collective-permute-start | bytes 393224 | tf_op jit(solution)/shard_map/ppermute | solution.py:19
  9.1 5.9 %collective-permute-start = (bf16[64,1024]{1,0:T(8,128)(2,1)S(1)}, bf16[64,1024]{1,0:T(8,128)(2,1)S(1)}, u32[]{:S(2)}, u32[]{:S(2)}) collective-permute-start(bf16[64,1024]{1,0:T(8,128)(2,1)S(1)} %get-tuple-element.23.refs_0_), channel_id=1, source_target_pairs={{0,2},{1,3},{2,0},{3,1},{4,6},{5,7},{6,4},{7,5},{8,10},{9,11},{10,... | collective-permute-start | bytes 393224 | tf_op jit(solution)/shard_map/ppermute | solution.py:19
  9.7 5.4 %collective-permute-start.4 = (bf16[32,1024]{1,0:T(8,128)(2,1)S(1)}, bf16[32,1024]{1,0:T(8,128)(2,1)S(1)}, u32[]{:S(2)}, u32[]{:S(2)}) collective-permute-start(bf16[32,1024]{1,0:T(8,128)(2,1)S(1)} %get-tuple-element.25), channel_id=1, source_target_pairs={{0,16},{8,24},{16,0},{24,8},{1,17},{9,25},{17,1},{25,9},{2,18},{10... | collective-permute-start | bytes 196616 | tf_op jit(solution)/shard_map/ppermute | solution.py:19
  9.7 5.4 %collective-permute-start.5 = (bf16[32,1024]{1,0:T(8,128)(2,1)S(1)}, bf16[32,1024]{1,0:T(8,128)(2,1)S(1)}, u32[]{:S(2)}, u32[]{:S(2)}) collective-permute-start(bf16[32,1024]{1,0:T(8,128)(2,1)S(1)} %get-tuple-element.26), channel_id=1, source_target_pairs={{0,8},{8,0},{16,24},{24,16},{1,9},{9,1},{17,25},{25,17},{2,10},{10... | collective-permute-start | bytes 196616 | tf_op jit(solution)/shard_map/ppermute | solution.py:19
  15.1 1.6 %collective-permute-start.6 = (bf16[128,1024]{1,0:T(8,128)(2,1)S(1)}, bf16[128,1024]{1,0:T(8,128)(2,1)S(1)}, u32[]{:S(2)}, u32[]{:S(2)}) collective-permute-start(bf16[128,1024]{1,0:T(8,128)(2,1)S(1)} %get-tuple-element.31.refs_0_), channel_id=1, source_target_pairs={{0,1},{1,0},{2,3},{3,2},{4,5},{5,4},{6,7},{7,6},{8,9},{9,8},{10,11... | collective-permute-start | bytes 786440 | tf_op jit(solution)/shard_map/ppermute | solution.py:19
  15.2 1.9 %collective-permute-start.7 = (bf16[128,1024]{1,0:T(8,128)(2,1)S(1)}, bf16[128,1024]{1,0:T(8,128)(2,1)S(1)}, u32[]{:S(2)}, u32[]{:S(2)}) collective-permute-start(bf16[128,1024]{1,0:T(8,128)(2,1)S(1)} %get-tuple-element.32.refs_1_), channel_id=1, source_target_pairs={{0,1},{1,0},{2,3},{3,2},{4,5},{5,4},{6,7},{7,6},{8,9},{9,8},{10,11... | collective-permute-start | bytes 786440 | tf_op jit(solution)/shard_map/ppermute | solution.py:19
  17.5 6.1 %collective-permute-start.10 = (f16[144,128]{1,0:T(8,128)(2,1)S(1)}, f16[144,128]{1,0:T(8,128)(2,1)S(1)}, u32[]{:S(2)}, u32[]{:S(2)}) collective-permute-start(f16[144,128]{1,0:T(8,128)(2,1)S(1)} %convert_element_type.22), channel_id=1, source_target_pairs={{0,24},{8,16},{16,8},{24,0},{1,25},{9,17},{17,9},{25,1},{2,26},{10... | collective-permute-start | bytes 110600 | tf_op jit(solution)/shard_map/ppermute | solution.py:19
  19.1 5.4 %collective-permute-start.9 = (f16[144,128]{1,0:T(8,128)(2,1)S(1)}, f16[144,128]{1,0:T(8,128)(2,1)S(1)}, u32[]{:S(2)}, u32[]{:S(2)}) collective-permute-start(f16[144,128]{1,0:T(8,128)(2,1)S(1)} %convert_element_type.20), channel_id=1, source_target_pairs={{0,16},{8,24},{16,0},{24,8},{1,17},{9,25},{17,1},{25,9},{2,18},{10... | collective-permute-start | bytes 110600 | tf_op jit(solution)/shard_map/ppermute | solution.py:19
  19.5 5.0 %collective-permute-start.8 = (f16[144,128]{1,0:T(8,128)(2,1)S(1)}, f16[144,128]{1,0:T(8,128)(2,1)S(1)}, u32[]{:S(2)}, u32[]{:S(2)}) collective-permute-start(f16[144,128]{1,0:T(8,128)(2,1)S(1)} %convert_element_type.18), channel_id=1, source_target_pairs={{0,8},{8,0},{16,24},{24,16},{1,9},{9,1},{17,25},{25,17},{2,10},{10... | collective-permute-start | bytes 110600 | tf_op jit(solution)/shard_map/ppermute | solution.py:19

commit v9 on v8

--- a/solution.py
+++ b/solution.py
@@ -156,8 +156,9 @@
 
 
 def exchange_partial(part, step):
-    got = exchange(part.astype(jnp.float16), "row", step).astype(jnp.float32)
-    return got[:-SCALE_ROWS] * jnp.exp2(-got[-SCALE_ROWS:1 - SCALE_ROWS])
+    got = exchange(part.astype(jnp.float16), "row", step)
+    power = got[-SCALE_ROWS:1 - SCALE_ROWS].astype(jnp.float32)
+    return got[:-SCALE_ROWS].astype(jnp.float32) * jnp.exp2(-power)
 
 
 def shards(amplitudes, integrals, panel_owner, residual_in):

time: 25.4 us -> 25.3 us (level)
  no operation moved by 1% of the time
where the time goes in v9:
time: 25.3 us; the launch traced here: 25.2 us
  starting transfers between devices  14.3 us (57%)
  waiting for transfers between devices  7.14 us (28%)
  Pallas kernels  2.87 us (11%)
  other arithmetic  0.71 us (3%)
    ppermute x11, starting transfers between devices, exchange(): return lax.ppermute(value, axis, [(i, i ^ step) for i in range(n)])  14.3 us
    ppermute x11, waiting for transfers between devices, exchange(): return lax.ppermute(value, axis, [(i, i ^ step) for i in range(n)])  7.14 us
    pallas_call x6, Pallas kernels, call(): pl.pallas_call(kernel, out_shape=outs, in_specs=specs, out_specs=[VMEM] *...  2.87 us
    add x1, other arithmetic, shards(): total = total + exchange_partial(part, step)  0.66 us
  transfers between devices with their start and end apart: 11, of which 5 were waited for; matrix products, arithmetic and copies ran while one was open for 0% of the time, Pallas kernels for 5%

profile of v9, /device:TPU:0, one launch (start us, length us, event | category | flops | bytes accessed | tf_op | source)
XLA Modules:
  0.0 25.2 jit_solution(1846634122952491206)
XLA Ops:
  0.0 1.0 %shard_map.47 = (bf16[64,1024]{1,0:T(8,128)(2,1)S(1)}, bf16[32,1024]{1,0:T(8,128)(2,1)S(1)}, bf16[32,1024]{1,0:T(8,128)(2,1)S(1)}, bf16[32,1024]{1,0:T(8,128)(2,1)S(1)}, bf16[32,1024]{1,0:T(8,128)(2,1)S(1)}) custom-call(bf16[64,1024]{1,0:T(8,128)(2,1)} %panel_ref.1, bf16[1,32,4096]{2,1,0:T(8,128)(2,1)} %amp_ref.1), custom_call_target="tpu_custom_call" | custom-call | tf_op jit(solution)/shard_map/pallas_call | solution.py:28
  1.0 5.1 %collective-permute-start.3 = (bf16[32,1024]{1,0:T(8,128)(2,1)S(1)}, bf16[32,1024]{1,0:T(8,128)(2,1)S(1)}, u32[]{:S(2)}, u32[]{:S(2)}) collective-permute-start(bf16[32,1024]{1,0:T(8,128)(2,1)S(1)} %get-tuple-element.24), channel_id=1, source_target_pairs={{0,24},{8,16},{16,8},{24,0},{1,25},{9,17},{17,9},{25,1},{2,26},{10... | collective-permute-start | bytes 196616 | tf_op jit(solution)/shard_map/ppermute | solution.py:19
  6.2 2.4 %collective-permute-start.2 = (bf16[64,1024]{1,0:T(8,128)(2,1)S(1)}, bf16[64,1024]{1,0:T(8,128)(2,1)S(1)}, u32[]{:S(2)}, u32[]{:S(2)}) collective-permute-start(bf16[64,1024]{1,0:T(8,128)(2,1)S(1)} %get-tuple-element.23.refs_0_), channel_id=1, source_target_pairs={{0,6},{1,7},{2,4},{3,5},{4,2},{5,3},{6,0},{7,1},{8,14},{9,15},{10,... | collective-permute-start | bytes 393224 | tf_op jit(solution)/shard_map/ppermute | solution.py:19
  8.6 0.5 %collective-permute-start.1 = (bf16[64,1024]{1,0:T(8,128)(2,1)S(1)}, bf16[64,1024]{1,0:T(8,128)(2,1)S(1)}, u32[]{:S(2)}, u32[]{:S(2)}) collective-permute-start(bf16[64,1024]{1,0:T(8,128)(2,1)S(1)} %get-tuple-element.23.refs_0_), channel_id=1, source_target_pairs={{0,4},{1,5},{2,6},{3,7},{4,0},{5,1},{6,2},{7,3},{8,12},{9,13},{10,... | collective-permute-start | bytes 393224 | tf_op jit(solution)/shard_map/ppermute | solution.py:19
  9.1 0.5 %collective-permute-start = (bf16[64,1024]{1,0:T(8,128)(2,1)S(1)}, bf16[64,1024]{1,0:T(8,128)(2,1)S(1)}, u32[]{:S(2)}, u32[]{:S(2)}) collective-permute-start(bf16[64,1024]{1,0:T(8,128)(2,1)S(1)} %get-tuple-element.23.refs_0_), channel_id=1, source_target_pairs={{0,2},{1,3},{2,0},{3,1},{4,6},{5,7},{6,4},{7,5},{8,10},{9,11},{10,... | collective-permute-start | bytes 393224 | tf_op jit(solution)/shard_map/ppermute | solution.py:19
  9.7 0.0 collective-permute-start.4
  9.7 0.0 collective-permute-done.3.refs_4_
  9.7 0.6 %collective-permute-start.5 = (bf16[32,1024]{1,0:T(8,128)(2,1)S(1)}, bf16[32,1024]{1,0:T(8,128)(2,1)S(1)}, u32[]{:S(2)}, u32[]{:S(2)}) collective-permute-start(bf16[32,1024]{1,0:T(8,128)(2,1)S(1)} %get-tuple-element.26), channel_id=1, source_target_pairs={{0,8},{8,0},{16,24},{24,16},{1,9},{9,1},{17,25},{25,17},{2,10},{10... | collective-permute-start | bytes 196616 | tf_op jit(solution)/shard_map/ppermute | solution.py:19
  10.3 0.9 %shard_map.46 = (f32[4,32,128]{2,1,0:T(8,128)S(1)}, s32[1,8]{1,0:T(1,128)S(1)}) custom-call(f32[4,32,128]{2,1,0:T(8,128)} %residual_ref.1, s32[1,8]{1,0:T(1,128)} %owner_ref.1), custom_call_target="tpu_custom_call" | custom-call | bytes 16777216 | tf_op jit(solution)/shard_map/pallas_call | solution.py:28
  11.2 3.9 %collective-permute-done.4.refs_5_ = bf16[32,1024]{1,0:T(8,128)(2,1)S(1)} collective-permute-done((bf16[32,1024]{1,0:T(8,128)(2,1)S(1)}, bf16[32,1024]{1,0:T(8,128)(2,1)S(1)}, u32[]{:S(2)}, u32[]{:S(2)}) %collective-permute-start.4) | collective-permute-done | bytes 65568 | tf_op jit(solution)/shard_map/ppermute | solution.py:19
  15.0 0.0 collective-permute-done.5.refs_6_
  15.0 0.0 collective-permute-done.2.refs_3_
  15.0 0.0 collective-permute-done.1.refs_2_
  15.0 0.0 collective-permute-done.refs_1_
  15.0 0.1 shard_map.48
  15.1 0.1 collective-permute-start.6
  15.2 0.5 %collective-permute-start.7 = (bf16[128,1024]{1,0:T(8,128)(2,1)S(1)}, bf16[128,1024]{1,0:T(8,128)(2,1)S(1)}, u32[]{:S(2)}, u32[]{:S(2)}) collective-permute-start(bf16[128,1024]{1,0:T(8,128)(2,1)S(1)} %get-tuple-element.32.refs_1_), channel_id=1, source_target_pairs={{0,1},{1,0},{2,3},{3,2},{4,5},{5,4},{6,7},{7,6},{8,9},{9,8},{10,11... | collective-permute-start | bytes 786440 | tf_op jit(solution)/shard_map/ppermute | solution.py:19
  15.7 0.3 %shard_map.49.near_part = f32[256,128]{1,0:T(8,128)S(1)} custom-call(bf16[128,1024]{1,0:T(8,128)(2,1)S(1)} %get-tuple-element.30.lhs, bf16[128,1024]{1,0:T(8,128)(2,1)S(1)} %get-tuple-element.31.refs_0_, bf16[128,1024]{1,0:T(8,128)(2,1)S(1)} %get-tuple-element.32.refs_1_), custom_call_target="tpu_custom_call" | custom-call | tf_op jit(solution)/shard_map/pallas_call | solution.py:28
  16.0 0.7 %collective-permute-done.6.refs_0_ = bf16[128,1024]{1,0:T(8,128)(2,1)S(1)} collective-permute-done((bf16[128,1024]{1,0:T(8,128)(2,1)S(1)}, bf16[128,1024]{1,0:T(8,128)(2,1)S(1)}, u32[]{:S(2)}, u32[]{:S(2)}) %collective-permute-start.6) | collective-permute-done | bytes 262176 | tf_op jit(solution)/shard_map/ppermute | solution.py:19
  16.7 0.2 shard_map.50.far_part
  16.9 0.1 collective-permute-done.7.last
  17.1 0.4 %shard_map.51 = (f32[144,128]{1,0:T(8,128)S(1)}, f32[144,128]{1,0:T(8,128)S(1)}, f32[144,128]{1,0:T(8,128)S(1)}, f32[128,128]{1,0:T(8,128)S(1)}) custom-call(s32[1,8]{1,0:T(1,128)S(1)} %get-tuple-element.28.owner_ref, f32[4,32,128]{2,1,0:T(8,128)S(1)} %get-tuple-element.29.residual_ref, bf16[128,1024]{1,0:T(8,128)(2,1)S(1)} %get-tuple-element.30.lhs, ...), custom_call_target="tpu_custom_call" | custom-call | tf_op jit(solution)/shard_map/pallas_call | solution.py:28
  17.5 1.5 %collective-permute-start.10 = (f16[144,128]{1,0:T(8,128)(2,1)S(1)}, f16[144,128]{1,0:T(8,128)(2,1)S(1)}, u32[]{:S(2)}, u32[]{:S(2)}) collective-permute-start(f16[144,128]{1,0:T(8,128)(2,1)S(1)} %convert_element_type.33), channel_id=1, source_target_pairs={{0,24},{8,16},{16,8},{24,0},{1,25},{9,17},{17,9},{25,1},{2,26},{10... | collective-permute-start | bytes 110600 | tf_op jit(solution)/shard_map/ppermute | solution.py:19
  19.1 0.5 %collective-permute-start.9 = (f16[144,128]{1,0:T(8,128)(2,1)S(1)}, f16[144,128]{1,0:T(8,128)(2,1)S(1)}, u32[]{:S(2)}, u32[]{:S(2)}) collective-permute-start(f16[144,128]{1,0:T(8,128)(2,1)S(1)} %convert_element_type.30), channel_id=1, source_target_pairs={{0,16},{8,24},{16,0},{24,8},{1,17},{9,25},{17,1},{25,9},{2,18},{10... | collective-permute-start | bytes 110600 | tf_op jit(solution)/shard_map/ppermute | solution.py:19
  19.5 2.5 %collective-permute-start.8 = (f16[144,128]{1,0:T(8,128)(2,1)S(1)}, f16[144,128]{1,0:T(8,128)(2,1)S(1)}, u32[]{:S(2)}, u32[]{:S(2)}) collective-permute-start(f16[144,128]{1,0:T(8,128)(2,1)S(1)} %convert_element_type.27), channel_id=1, source_target_pairs={{0,8},{8,0},{16,24},{24,16},{1,9},{9,1},{17,25},{25,17},{2,10},{10... | collective-permute-start | bytes 110600 | tf_op jit(solution)/shard_map/ppermute | solution.py:19
  22.0 1.6 %collective-permute-done.10 = f16[144,128]{1,0:T(8,128)(2,1)S(1)} collective-permute-done((f16[144,128]{1,0:T(8,128)(2,1)S(1)}, f16[144,128]{1,0:T(8,128)(2,1)S(1)}, u32[]{:S(2)}, u32[]{:S(2)}) %collective-permute-start.10) | collective-permute-done | bytes 36896 | tf_op jit(solution)/shard_map/ppermute | solution.py:19
  23.6 0.8 %collective-permute-done.9 = f16[144,128]{1,0:T(8,128)(2,1)S(1)} collective-permute-done((f16[144,128]{1,0:T(8,128)(2,1)S(1)}, f16[144,128]{1,0:T(8,128)(2,1)S(1)}, u32[]{:S(2)}, u32[]{:S(2)}) %collective-permute-start.9) | collective-permute-done | bytes 36896 | tf_op jit(solution)/shard_map/ppermute | solution.py:19
  24.5 0.0 collective-permute-done.8
  24.5 0.7 %multiply_add_fusion = f32[128,128]{1,0:T(8,128)} fusion(f32[128,128]{1,0:T(8,128)S(1)} %get-tuple-element.33, f16[144,128]{1,0:T(8,128)(2,1)S(1)} %collective-permute-done.10, f16[144,128]{1,0:T(8,128)(2,1)S(1)} %collective-permute-done.9, f16[144,128]{1,0:T(8,128)(2,1)S(1)} %collective-permute-done.8, f32[128]{0:T(128)S(1)} %fusion.3, f32[128]{0:T(128)S(1)} %fusion.7, ...), kind=kLoop, calls=%fused_computation | loop fusion | flops 147456 | bytes 230912 | tf_op jit(solution)/shard_map/add | solution.py:176
  (6 shorter events, 0.0 us)
Async XLA Ops:
  1.0 8.6 %collective-permute-start.3 = (bf16[32,1024]{1,0:T(8,128)(2,1)S(1)}, bf16[32,1024]{1,0:T(8,128)(2,1)S(1)}, u32[]{:S(2)}, u32[]{:S(2)}) collective-permute-start(bf16[32,1024]{1,0:T(8,128)(2,1)S(1)} %get-tuple-element.24), channel_id=1, source_target_pairs={{0,24},{8,16},{16,8},{24,0},{1,25},{9,17},{17,9},{25,1},{2,26},{10... | collective-permute-start | bytes 196616 | tf_op jit(solution)/shard_map/ppermute | solution.py:19
  6.2 8.9 %collective-permute-start.2 = (bf16[64,1024]{1,0:T(8,128)(2,1)S(1)}, bf16[64,1024]{1,0:T(8,128)(2,1)S(1)}, u32[]{:S(2)}, u32[]{:S(2)}) collective-permute-start(bf16[64,1024]{1,0:T(8,128)(2,1)S(1)} %get-tuple-element.23.refs_0_), channel_id=1, source_target_pairs={{0,6},{1,7},{2,4},{3,5},{4,2},{5,3},{6,0},{7,1},{8,14},{9,15},{10,... | collective-permute-start | bytes 393224 | tf_op jit(solution)/shard_map/ppermute | solution.py:19
  8.6 6.4 %collective-permute-start.1 = (bf16[64,1024]{1,0:T(8,128)(2,1)S(1)}, bf16[64,1024]{1,0:T(8,128)(2,1)S(1)}, u32[]{:S(2)}, u32[]{:S(2)}) collective-permute-start(bf16[64,1024]{1,0:T(8,128)(2,1)S(1)} %get-tuple-element.23.refs_0_), channel_id=1, source_target_pairs={{0,4},{1,5},{2,6},{3,7},{4,0},{5,1},{6,2},{7,3},{8,12},{9,13},{10,... | collective-permute-start | bytes 393224 | tf_op jit(solution)/shard_map/ppermute | solution.py:19
  9.1 5.9 %collective-permute-start = (bf16[64,1024]{1,0:T(8,128)(2,1)S(1)}, bf16[64,1024]{1,0:T(8,128)(2,1)S(1)}, u32[]{:S(2)}, u32[]{:S(2)}) collective-permute-start(bf16[64,1024]{1,0:T(8,128)(2,1)S(1)} %get-tuple-element.23.refs_0_), channel_id=1, source_target_pairs={{0,2},{1,3},{2,0},{3,1},{4,6},{5,7},{6,4},{7,5},{8,10},{9,11},{10,... | collective-permute-start | bytes 393224 | tf_op jit(solution)/shard_map/ppermute | solution.py:19
  9.7 5.4 %collective-permute-start.4 = (bf16[32,1024]{1,0:T(8,128)(2,1)S(1)}, bf16[32,1024]{1,0:T(8,128)(2,1)S(1)}, u32[]{:S(2)}, u32[]{:S(2)}) collective-permute-start(bf16[32,1024]{1,0:T(8,128)(2,1)S(1)} %get-tuple-element.25), channel_id=1, source_target_pairs={{0,16},{8,24},{16,0},{24,8},{1,17},{9,25},{17,1},{25,9},{2,18},{10... | collective-permute-start | bytes 196616 | tf_op jit(solution)/shard_map/ppermute | solution.py:19
  9.7 5.4 %collective-permute-start.5 = (bf16[32,1024]{1,0:T(8,128)(2,1)S(1)}, bf16[32,1024]{1,0:T(8,128)(2,1)S(1)}, u32[]{:S(2)}, u32[]{:S(2)}) collective-permute-start(bf16[32,1024]{1,0:T(8,128)(2,1)S(1)} %get-tuple-element.26), channel_id=1, source_target_pairs={{0,8},{8,0},{16,24},{24,16},{1,9},{9,1},{17,25},{25,17},{2,10},{10... | collective-permute-start | bytes 196616 | tf_op jit(solution)/shard_map/ppermute | solution.py:19
  15.1 1.6 %collective-permute-start.6 = (bf16[128,1024]{1,0:T(8,128)(2,1)S(1)}, bf16[128,1024]{1,0:T(8,128)(2,1)S(1)}, u32[]{:S(2)}, u32[]{:S(2)}) collective-permute-start(bf16[128,1024]{1,0:T(8,128)(2,1)S(1)} %get-tuple-element.31.refs_0_), channel_id=1, source_target_pairs={{0,1},{1,0},{2,3},{3,2},{4,5},{5,4},{6,7},{7,6},{8,9},{9,8},{10,11... | collective-permute-start | bytes 786440 | tf_op jit(solution)/shard_map/ppermute | solution.py:19
  15.2 1.9 %collective-permute-start.7 = (bf16[128,1024]{1,0:T(8,128)(2,1)S(1)}, bf16[128,1024]{1,0:T(8,128)(2,1)S(1)}, u32[]{:S(2)}, u32[]{:S(2)}) collective-permute-start(bf16[128,1024]{1,0:T(8,128)(2,1)S(1)} %get-tuple-element.32.refs_1_), channel_id=1, source_target_pairs={{0,1},{1,0},{2,3},{3,2},{4,5},{5,4},{6,7},{7,6},{8,9},{9,8},{10,11... | collective-permute-start | bytes 786440 | tf_op jit(solution)/shard_map/ppermute | solution.py:19
  17.5 6.1 %collective-permute-start.10 = (f16[144,128]{1,0:T(8,128)(2,1)S(1)}, f16[144,128]{1,0:T(8,128)(2,1)S(1)}, u32[]{:S(2)}, u32[]{:S(2)}) collective-permute-start(f16[144,128]{1,0:T(8,128)(2,1)S(1)} %convert_element_type.33), channel_id=1, source_target_pairs={{0,24},{8,16},{16,8},{24,0},{1,25},{9,17},{17,9},{25,1},{2,26},{10... | collective-permute-start | bytes 110600 | tf_op jit(solution)/shard_map/ppermute | solution.py:19
  19.1 5.4 %collective-permute-start.9 = (f16[144,128]{1,0:T(8,128)(2,1)S(1)}, f16[144,128]{1,0:T(8,128)(2,1)S(1)}, u32[]{:S(2)}, u32[]{:S(2)}) collective-permute-start(f16[144,128]{1,0:T(8,128)(2,1)S(1)} %convert_element_type.30), channel_id=1, source_target_pairs={{0,16},{8,24},{16,0},{24,8},{1,17},{9,25},{17,1},{25,9},{2,18},{10... | collective-permute-start | bytes 110600 | tf_op jit(solution)/shard_map/ppermute | solution.py:19
  19.5 5.0 %collective-permute-start.8 = (f16[144,128]{1,0:T(8,128)(2,1)S(1)}, f16[144,128]{1,0:T(8,128)(2,1)S(1)}, u32[]{:S(2)}, u32[]{:S(2)}) collective-permute-start(f16[144,128]{1,0:T(8,128)(2,1)S(1)} %convert_element_type.27), channel_id=1, source_target_pairs={{0,8},{8,0},{16,24},{24,16},{1,9},{9,1},{17,25},{25,17},{2,10},{10... | collective-permute-start | bytes 110600 | tf_op jit(solution)/shard_map/ppermute | solution.py:19

commit v10 on v8

--- a/solution.py
+++ b/solution.py
@@ -67,7 +67,7 @@
 
 
 def fetch_late(residual, owner):
-    cost = pl.CostEstimate(flops=0, bytes_accessed=16 << 20, transcendentals=0)
+    cost = pl.CostEstimate(flops=0, bytes_accessed=256 << 20, transcendentals=0)
     return call(
         fetch_late_kernel, [like(residual), like(owner)], [HBM] * 2, in_hbm(residual, owner),
         semaphores=[pltpu.SemaphoreType.DMA((2,))], cost=cost)

time: 25.4 us -> 25.4 us (level)
  no operation moved by 1% of the time
where the time goes in v10:
time: 25.4 us; the launch traced here: 25.2 us
  starting transfers between devices  14.3 us (56%)
  waiting for transfers between devices  7.14 us (28%)
  Pallas kernels  2.87 us (11%)
  other arithmetic  0.73 us (3%)
    ppermute x11, starting transfers between devices, exchange(): return lax.ppermute(value, axis, [(i, i ^ step) for i in range(n)])  14.3 us
    ppermute x11, waiting for transfers between devices, exchange(): return lax.ppermute(value, axis, [(i, i ^ step) for i in range(n)])  7.14 us
    pallas_call x6, Pallas kernels, call(): pl.pallas_call(kernel, out_shape=outs, in_specs=specs, out_specs=[VMEM] *...  2.87 us
    add x1, other arithmetic, shards(): total = total + exchange_partial(part, step)  0.65 us
  transfers between devices with their start and end apart: 11, of which 5 were waited for; matrix products, arithmetic and copies ran while one was open for 0% of the time, Pallas kernels for 5%

profile of v10, /device:TPU:0, one launch (start us, length us, event | category | flops | bytes accessed | tf_op | source)
XLA Modules:
  0.0 25.2 jit_solution(3256002843875224700)
XLA Ops:
  0.0 1.0 %shard_map.47 = (bf16[64,1024]{1,0:T(8,128)(2,1)S(1)}, bf16[32,1024]{1,0:T(8,128)(2,1)S(1)}, bf16[32,1024]{1,0:T(8,128)(2,1)S(1)}, bf16[32,1024]{1,0:T(8,128)(2,1)S(1)}, bf16[32,1024]{1,0:T(8,128)(2,1)S(1)}) custom-call(bf16[64,1024]{1,0:T(8,128)(2,1)} %panel_ref.1, bf16[1,32,4096]{2,1,0:T(8,128)(2,1)} %amp_ref.1), custom_call_target="tpu_custom_call" | custom-call | tf_op jit(solution)/shard_map/pallas_call | solution.py:28
  1.0 5.1 %collective-permute-start.3 = (bf16[32,1024]{1,0:T(8,128)(2,1)S(1)}, bf16[32,1024]{1,0:T(8,128)(2,1)S(1)}, u32[]{:S(2)}, u32[]{:S(2)}) collective-permute-start(bf16[32,1024]{1,0:T(8,128)(2,1)S(1)} %get-tuple-element.24), channel_id=1, source_target_pairs={{0,24},{8,16},{16,8},{24,0},{1,25},{9,17},{17,9},{25,1},{2,26},{10... | collective-permute-start | bytes 196616 | tf_op jit(solution)/shard_map/ppermute | solution.py:19
  6.2 2.4 %collective-permute-start.2 = (bf16[64,1024]{1,0:T(8,128)(2,1)S(1)}, bf16[64,1024]{1,0:T(8,128)(2,1)S(1)}, u32[]{:S(2)}, u32[]{:S(2)}) collective-permute-start(bf16[64,1024]{1,0:T(8,128)(2,1)S(1)} %get-tuple-element.23.refs_0_), channel_id=1, source_target_pairs={{0,6},{1,7},{2,4},{3,5},{4,2},{5,3},{6,0},{7,1},{8,14},{9,15},{10,... | collective-permute-start | bytes 393224 | tf_op jit(solution)/shard_map/ppermute | solution.py:19
  8.6 0.5 %collective-permute-start.1 = (bf16[64,1024]{1,0:T(8,128)(2,1)S(1)}, bf16[64,1024]{1,0:T(8,128)(2,1)S(1)}, u32[]{:S(2)}, u32[]{:S(2)}) collective-permute-start(bf16[64,1024]{1,0:T(8,128)(2,1)S(1)} %get-tuple-element.23.refs_0_), channel_id=1, source_target_pairs={{0,4},{1,5},{2,6},{3,7},{4,0},{5,1},{6,2},{7,3},{8,12},{9,13},{10,... | collective-permute-start | bytes 393224 | tf_op jit(solution)/shard_map/ppermute | solution.py:19
  9.1 0.5 %collective-permute-start = (bf16[64,1024]{1,0:T(8,128)(2,1)S(1)}, bf16[64,1024]{1,0:T(8,128)(2,1)S(1)}, u32[]{:S(2)}, u32[]{:S(2)}) collective-permute-start(bf16[64,1024]{1,0:T(8,128)(2,1)S(1)} %get-tuple-element.23.refs_0_), channel_id=1, source_target_pairs={{0,2},{1,3},{2,0},{3,1},{4,6},{5,7},{6,4},{7,5},{8,10},{9,11},{10,... | collective-permute-start | bytes 393224 | tf_op jit(solution)/shard_map/ppermute | solution.py:19
  9.7 0.0 collective-permute-start.4
  9.7 0.0 collective-permute-done.3.refs_4_
  9.7 0.6 %collective-permute-start.5 = (bf16[32,1024]{1,0:T(8,128)(2,1)S(1)}, bf16[32,1024]{1,0:T(8,128)(2,1)S(1)}, u32[]{:S(2)}, u32[]{:S(2)}) collective-permute-start(bf16[32,1024]{1,0:T(8,128)(2,1)S(1)} %get-tuple-element.26), channel_id=1, source_target_pairs={{0,8},{8,0},{16,24},{24,16},{1,9},{9,1},{17,25},{25,17},{2,10},{10... | collective-permute-start | bytes 196616 | tf_op jit(solution)/shard_map/ppermute | solution.py:19
  10.3 0.9 %shard_map.46 = (f32[4,32,128]{2,1,0:T(8,128)S(1)}, s32[1,8]{1,0:T(1,128)S(1)}) custom-call(f32[4,32,128]{2,1,0:T(8,128)} %residual_ref.1, s32[1,8]{1,0:T(1,128)} %owner_ref.1), custom_call_target="tpu_custom_call" | custom-call | bytes 268435456 | tf_op jit(solution)/shard_map/pallas_call | solution.py:28
  11.2 3.9 %collective-permute-done.4.refs_5_ = bf16[32,1024]{1,0:T(8,128)(2,1)S(1)} collective-permute-done((bf16[32,1024]{1,0:T(8,128)(2,1)S(1)}, bf16[32,1024]{1,0:T(8,128)(2,1)S(1)}, u32[]{:S(2)}, u32[]{:S(2)}) %collective-permute-start.4) | collective-permute-done | bytes 65568 | tf_op jit(solution)/shard_map/ppermute | solution.py:19
  15.0 0.0 collective-permute-done.5.refs_6_
  15.0 0.0 collective-permute-done.2.refs_3_
  15.0 0.0 collective-permute-done.1.refs_2_
  15.0 0.0 collective-permute-done.refs_1_
  15.0 0.1 shard_map.48
  15.1 0.1 collective-permute-start.6
  15.2 0.5 %collective-permute-start.7 = (bf16[128,1024]{1,0:T(8,128)(2,1)S(1)}, bf16[128,1024]{1,0:T(8,128)(2,1)S(1)}, u32[]{:S(2)}, u32[]{:S(2)}) collective-permute-start(bf16[128,1024]{1,0:T(8,128)(2,1)S(1)} %get-tuple-element.32.refs_1_), channel_id=1, source_target_pairs={{0,1},{1,0},{2,3},{3,2},{4,5},{5,4},{6,7},{7,6},{8,9},{9,8},{10,11... | collective-permute-start | bytes 786440 | tf_op jit(solution)/shard_map/ppermute | solution.py:19
  15.7 0.3 %shard_map.49.near_part = f32[256,128]{1,0:T(8,128)S(1)} custom-call(bf16[128,1024]{1,0:T(8,128)(2,1)S(1)} %get-tuple-element.30.lhs, bf16[128,1024]{1,0:T(8,128)(2,1)S(1)} %get-tuple-element.31.refs_0_, bf16[128,1024]{1,0:T(8,128)(2,1)S(1)} %get-tuple-element.32.refs_1_), custom_call_target="tpu_custom_call" | custom-call | tf_op jit(solution)/shard_map/pallas_call | solution.py:28
  16.0 0.7 %collective-permute-done.6.refs_0_ = bf16[128,1024]{1,0:T(8,128)(2,1)S(1)} collective-permute-done((bf16[128,1024]{1,0:T(8,128)(2,1)S(1)}, bf16[128,1024]{1,0:T(8,128)(2,1)S(1)}, u32[]{:S(2)}, u32[]{:S(2)}) %collective-permute-start.6) | collective-permute-done | bytes 262176 | tf_op jit(solution)/shard_map/ppermute | solution.py:19
  16.7 0.2 shard_map.50.far_part
  16.9 0.1 collective-permute-done.7.last
  17.1 0.4 %shard_map.51 = (f32[144,128]{1,0:T(8,128)S(1)}, f32[144,128]{1,0:T(8,128)S(1)}, f32[144,128]{1,0:T(8,128)S(1)}, f32[128,128]{1,0:T(8,128)S(1)}) custom-call(s32[1,8]{1,0:T(1,128)S(1)} %get-tuple-element.28.owner_ref, f32[4,32,128]{2,1,0:T(8,128)S(1)} %get-tuple-element.29.residual_ref, bf16[128,1024]{1,0:T(8,128)(2,1)S(1)} %get-tuple-element.30.lhs, ...), custom_call_target="tpu_custom_call" | custom-call | tf_op jit(solution)/shard_map/pallas_call | solution.py:28
  17.5 1.5 %collective-permute-start.10 = (f16[144,128]{1,0:T(8,128)(2,1)S(1)}, f16[144,128]{1,0:T(8,128)(2,1)S(1)}, u32[]{:S(2)}, u32[]{:S(2)}) collective-permute-start(f16[144,128]{1,0:T(8,128)(2,1)S(1)} %convert_element_type.22), channel_id=1, source_target_pairs={{0,24},{8,16},{16,8},{24,0},{1,25},{9,17},{17,9},{25,1},{2,26},{10... | collective-permute-start | bytes 110600 | tf_op jit(solution)/shard_map/ppermute | solution.py:19
  19.1 0.5 %collective-permute-start.9 = (f16[144,128]{1,0:T(8,128)(2,1)S(1)}, f16[144,128]{1,0:T(8,128)(2,1)S(1)}, u32[]{:S(2)}, u32[]{:S(2)}) collective-permute-start(f16[144,128]{1,0:T(8,128)(2,1)S(1)} %convert_element_type.20), channel_id=1, source_target_pairs={{0,16},{8,24},{16,0},{24,8},{1,17},{9,25},{17,1},{25,9},{2,18},{10... | collective-permute-start | bytes 110600 | tf_op jit(solution)/shard_map/ppermute | solution.py:19
  19.5 2.5 %collective-permute-start.8 = (f16[144,128]{1,0:T(8,128)(2,1)S(1)}, f16[144,128]{1,0:T(8,128)(2,1)S(1)}, u32[]{:S(2)}, u32[]{:S(2)}) collective-permute-start(f16[144,128]{1,0:T(8,128)(2,1)S(1)} %convert_element_type.18), channel_id=1, source_target_pairs={{0,8},{8,0},{16,24},{24,16},{1,9},{9,1},{17,25},{25,17},{2,10},{10... | collective-permute-start | bytes 110600 | tf_op jit(solution)/shard_map/ppermute | solution.py:19
  22.0 1.6 %collective-permute-done.10 = f16[144,128]{1,0:T(8,128)(2,1)S(1)} collective-permute-done((f16[144,128]{1,0:T(8,128)(2,1)S(1)}, f16[144,128]{1,0:T(8,128)(2,1)S(1)}, u32[]{:S(2)}, u32[]{:S(2)}) %collective-permute-start.10) | collective-permute-done | bytes 36896 | tf_op jit(solution)/shard_map/ppermute | solution.py:19
  23.6 0.8 %collective-permute-done.9 = f16[144,128]{1,0:T(8,128)(2,1)S(1)} collective-permute-done((f16[144,128]{1,0:T(8,128)(2,1)S(1)}, f16[144,128]{1,0:T(8,128)(2,1)S(1)}, u32[]{:S(2)}, u32[]{:S(2)}) %collective-permute-start.9) | collective-permute-done | bytes 36896 | tf_op jit(solution)/shard_map/ppermute | solution.py:19
  24.5 0.0 collective-permute-done.8
  24.5 0.7 %fusion = f32[128,128]{1,0:T(8,128)} fusion(f32[144,128]{1,0:T(8,128)S(1)} %convert_element_type.23, f32[144,128]{1,0:T(8,128)S(1)} %convert_element_type.21, f32[128,128]{1,0:T(8,128)S(1)} %get-tuple-element.33, f32[144,128]{1,0:T(8,128)S(1)} %convert_element_type.19, f32[128]{0:T(128)S(1)} %fusion.5, f32[128]{0:T(128)S(1)} %fusion.8, f32[128]{0:T(128)S(1)} %fusion.11), kind=kLoop, calls=%fused_computation.1 | loop fusion | flops 98304 | bytes 329216 | tf_op jit(solution)/shard_map/add | solution.py:175
  (9 shorter events, 0.1 us)
Async XLA Ops:
  1.0 8.6 %collective-permute-start.3 = (bf16[32,1024]{1,0:T(8,128)(2,1)S(1)}, bf16[32,1024]{1,0:T(8,128)(2,1)S(1)}, u32[]{:S(2)}, u32[]{:S(2)}) collective-permute-start(bf16[32,1024]{1,0:T(8,128)(2,1)S(1)} %get-tuple-element.24), channel_id=1, source_target_pairs={{0,24},{8,16},{16,8},{24,0},{1,25},{9,17},{17,9},{25,1},{2,26},{10... | collective-permute-start | bytes 196616 | tf_op jit(solution)/shard_map/ppermute | solution.py:19
  6.2 8.9 %collective-permute-start.2 = (bf16[64,1024]{1,0:T(8,128)(2,1)S(1)}, bf16[64,1024]{1,0:T(8,128)(2,1)S(1)}, u32[]{:S(2)}, u32[]{:S(2)}) collective-permute-start(bf16[64,1024]{1,0:T(8,128)(2,1)S(1)} %get-tuple-element.23.refs_0_), channel_id=1, source_target_pairs={{0,6},{1,7},{2,4},{3,5},{4,2},{5,3},{6,0},{7,1},{8,14},{9,15},{10,... | collective-permute-start | bytes 393224 | tf_op jit(solution)/shard_map/ppermute | solution.py:19
  8.6 6.4 %collective-permute-start.1 = (bf16[64,1024]{1,0:T(8,128)(2,1)S(1)}, bf16[64,1024]{1,0:T(8,128)(2,1)S(1)}, u32[]{:S(2)}, u32[]{:S(2)}) collective-permute-start(bf16[64,1024]{1,0:T(8,128)(2,1)S(1)} %get-tuple-element.23.refs_0_), channel_id=1, source_target_pairs={{0,4},{1,5},{2,6},{3,7},{4,0},{5,1},{6,2},{7,3},{8,12},{9,13},{10,... | collective-permute-start | bytes 393224 | tf_op jit(solution)/shard_map/ppermute | solution.py:19
  9.1 5.9 %collective-permute-start = (bf16[64,1024]{1,0:T(8,128)(2,1)S(1)}, bf16[64,1024]{1,0:T(8,128)(2,1)S(1)}, u32[]{:S(2)}, u32[]{:S(2)}) collective-permute-start(bf16[64,1024]{1,0:T(8,128)(2,1)S(1)} %get-tuple-element.23.refs_0_), channel_id=1, source_target_pairs={{0,2},{1,3},{2,0},{3,1},{4,6},{5,7},{6,4},{7,5},{8,10},{9,11},{10,... | collective-permute-start | bytes 393224 | tf_op jit(solution)/shard_map/ppermute | solution.py:19
  9.7 5.4 %collective-permute-start.4 = (bf16[32,1024]{1,0:T(8,128)(2,1)S(1)}, bf16[32,1024]{1,0:T(8,128)(2,1)S(1)}, u32[]{:S(2)}, u32[]{:S(2)}) collective-permute-start(bf16[32,1024]{1,0:T(8,128)(2,1)S(1)} %get-tuple-element.25), channel_id=1, source_target_pairs={{0,16},{8,24},{16,0},{24,8},{1,17},{9,25},{17,1},{25,9},{2,18},{10... | collective-permute-start | bytes 196616 | tf_op jit(solution)/shard_map/ppermute | solution.py:19
  9.7 5.4 %collective-permute-start.5 = (bf16[32,1024]{1,0:T(8,128)(2,1)S(1)}, bf16[32,1024]{1,0:T(8,128)(2,1)S(1)}, u32[]{:S(2)}, u32[]{:S(2)}) collective-permute-start(bf16[32,1024]{1,0:T(8,128)(2,1)S(1)} %get-tuple-element.26), channel_id=1, source_target_pairs={{0,8},{8,0},{16,24},{24,16},{1,9},{9,1},{17,25},{25,17},{2,10},{10... | collective-permute-start | bytes 196616 | tf_op jit(solution)/shard_map/ppermute | solution.py:19
  15.1 1.6 %collective-permute-start.6 = (bf16[128,1024]{1,0:T(8,128)(2,1)S(1)}, bf16[128,1024]{1,0:T(8,128)(2,1)S(1)}, u32[]{:S(2)}, u32[]{:S(2)}) collective-permute-start(bf16[128,1024]{1,0:T(8,128)(2,1)S(1)} %get-tuple-element.31.refs_0_), channel_id=1, source_target_pairs={{0,1},{1,0},{2,3},{3,2},{4,5},{5,4},{6,7},{7,6},{8,9},{9,8},{10,11... | collective-permute-start | bytes 786440 | tf_op jit(solution)/shard_map/ppermute | solution.py:19
  15.2 1.9 %collective-permute-start.7 = (bf16[128,1024]{1,0:T(8,128)(2,1)S(1)}, bf16[128,1024]{1,0:T(8,128)(2,1)S(1)}, u32[]{:S(2)}, u32[]{:S(2)}) collective-permute-start(bf16[128,1024]{1,0:T(8,128)(2,1)S(1)} %get-tuple-element.32.refs_1_), channel_id=1, source_target_pairs={{0,1},{1,0},{2,3},{3,2},{4,5},{5,4},{6,7},{7,6},{8,9},{9,8},{10,11... | collective-permute-start | bytes 786440 | tf_op jit(solution)/shard_map/ppermute | solution.py:19
  17.5 6.1 %collective-permute-start.10 = (f16[144,128]{1,0:T(8,128)(2,1)S(1)}, f16[144,128]{1,0:T(8,128)(2,1)S(1)}, u32[]{:S(2)}, u32[]{:S(2)}) collective-permute-start(f16[144,128]{1,0:T(8,128)(2,1)S(1)} %convert_element_type.22), channel_id=1, source_target_pairs={{0,24},{8,16},{16,8},{24,0},{1,25},{9,17},{17,9},{25,1},{2,26},{10... | collective-permute-start | bytes 110600 | tf_op jit(solution)/shard_map/ppermute | solution.py:19
  19.1 5.4 %collective-permute-start.9 = (f16[144,128]{1,0:T(8,128)(2,1)S(1)}, f16[144,128]{1,0:T(8,128)(2,1)S(1)}, u32[]{:S(2)}, u32[]{:S(2)}) collective-permute-start(f16[144,128]{1,0:T(8,128)(2,1)S(1)} %convert_element_type.20), channel_id=1, source_target_pairs={{0,16},{8,24},{16,0},{24,8},{1,17},{9,25},{17,1},{25,9},{2,18},{10... | collective-permute-start | bytes 110600 | tf_op jit(solution)/shard_map/ppermute | solution.py:19
  19.5 5.0 %collective-permute-start.8 = (f16[144,128]{1,0:T(8,128)(2,1)S(1)}, f16[144,128]{1,0:T(8,128)(2,1)S(1)}, u32[]{:S(2)}, u32[]{:S(2)}) collective-permute-start(f16[144,128]{1,0:T(8,128)(2,1)S(1)} %convert_element_type.18), channel_id=1, source_target_pairs={{0,8},{8,0},{16,24},{24,16},{1,9},{9,1},{17,25},{25,17},{2,10},{10... | collective-permute-start | bytes 110600 | tf_op jit(solution)/shard_map/ppermute | solution.py:19

commit v11 on v8

--- a/solution.py
+++ b/solution.py
@@ -166,8 +166,9 @@
     own, blocks = fetch(integrals, amplitudes, rows)
     residual, owner = fetch_late(residual_in, panel_owner)
     panels = [exchange(own, "col", step) if step else own for step in range(0, columns, 2)]
-    amps = [exchange(blocks[step], "row", step) if step else blocks[0] for step in steps]
-    nears, lhs, residual, owner = assemble(steps, residual, owner, panels, amps)
+    order = (rows // 2, *(step for step in steps if step != rows // 2))
+    amps = [exchange(blocks[step], "row", step) if step else blocks[0] for step in order]
+    nears, lhs, residual, owner = assemble(order, residual, owner, panels, amps)
     *fars, last = [exchange(near, "col", 1) for near in nears]
     parts = contract(steps, owner, residual, lhs, products(lhs, nears), products(lhs, fars), last)
     total = parts[-1]

time: 25.4 us -> 25.5 us (level)
  transfers between devices with their start and end apart: 11 -> 11, of which waited for: 5 -> 7; matrix products, arithmetic and copies ran while one was open for 0% -> 0% of each run, Pallas kernels for 5% -> 5%
where the time goes in v11:
time: 25.5 us; the launch traced here: 25.3 us
  starting transfers between devices  14.3 us (56%)
  waiting for transfers between devices  7.34 us (29%)
  Pallas kernels  2.86 us (11%)
  other arithmetic  0.73 us (3%)
    ppermute x11, starting transfers between devices, exchange(): return lax.ppermute(value, axis, [(i, i ^ step) for i in range(n)])  14.3 us
    ppermute x11, waiting for transfers between devices, exchange(): return lax.ppermute(value, axis, [(i, i ^ step) for i in range(n)])  7.34 us
    pallas_call x6, Pallas kernels, call(): pl.pallas_call(kernel, out_shape=outs, in_specs=specs, out_specs=[VMEM] *...  2.86 us
    add x1, other arithmetic, shards(): total = total + exchange_partial(part, step)  0.66 us
  transfers between devices with their start and end apart: 11, of which 7 were waited for; matrix products, arithmetic and copies ran while one was open for 0% of the time, Pallas kernels for 5%

profile of v11, /device:TPU:0, one launch (start us, length us, event | category | flops | bytes accessed | tf_op | source)
XLA Modules:
  0.0 25.3 jit_solution(8057859532848016979)
XLA Ops:
  0.0 1.0 %shard_map.47 = (bf16[64,1024]{1,0:T(8,128)(2,1)S(1)}, bf16[32,1024]{1,0:T(8,128)(2,1)S(1)}, bf16[32,1024]{1,0:T(8,128)(2,1)S(1)}, bf16[32,1024]{1,0:T(8,128)(2,1)S(1)}, bf16[32,1024]{1,0:T(8,128)(2,1)S(1)}) custom-call(bf16[64,1024]{1,0:T(8,128)(2,1)} %panel_ref.1, bf16[1,32,4096]{2,1,0:T(8,128)(2,1)} %amp_ref.1), custom_call_target="tpu_custom_call" | custom-call | tf_op jit(solution)/shard_map/pallas_call | solution.py:28
  1.0 4.1 %collective-permute-start.3 = (bf16[32,1024]{1,0:T(8,128)(2,1)S(1)}, bf16[32,1024]{1,0:T(8,128)(2,1)S(1)}, u32[]{:S(2)}, u32[]{:S(2)}) collective-permute-start(bf16[32,1024]{1,0:T(8,128)(2,1)S(1)} %get-tuple-element.24), channel_id=1, source_target_pairs={{0,16},{8,24},{16,0},{24,8},{1,17},{9,25},{17,1},{25,9},{2,18},{10... | collective-permute-start | bytes 196616 | tf_op jit(solution)/shard_map/ppermute | solution.py:19
  5.2 2.4 %collective-permute-start.2 = (bf16[64,1024]{1,0:T(8,128)(2,1)S(1)}, bf16[64,1024]{1,0:T(8,128)(2,1)S(1)}, u32[]{:S(2)}, u32[]{:S(2)}) collective-permute-start(bf16[64,1024]{1,0:T(8,128)(2,1)S(1)} %get-tuple-element.23.refs_0_), channel_id=1, source_target_pairs={{0,6},{1,7},{2,4},{3,5},{4,2},{5,3},{6,0},{7,1},{8,14},{9,15},{10,... | collective-permute-start | bytes 393224 | tf_op jit(solution)/shard_map/ppermute | solution.py:19
  7.6 0.5 %collective-permute-start.1 = (bf16[64,1024]{1,0:T(8,128)(2,1)S(1)}, bf16[64,1024]{1,0:T(8,128)(2,1)S(1)}, u32[]{:S(2)}, u32[]{:S(2)}) collective-permute-start(bf16[64,1024]{1,0:T(8,128)(2,1)S(1)} %get-tuple-element.23.refs_0_), channel_id=1, source_target_pairs={{0,4},{1,5},{2,6},{3,7},{4,0},{5,1},{6,2},{7,3},{8,12},{9,13},{10,... | collective-permute-start | bytes 393224 | tf_op jit(solution)/shard_map/ppermute | solution.py:19
  8.1 0.5 %collective-permute-start = (bf16[64,1024]{1,0:T(8,128)(2,1)S(1)}, bf16[64,1024]{1,0:T(8,128)(2,1)S(1)}, u32[]{:S(2)}, u32[]{:S(2)}) collective-permute-start(bf16[64,1024]{1,0:T(8,128)(2,1)S(1)} %get-tuple-element.23.refs_0_), channel_id=1, source_target_pairs={{0,2},{1,3},{2,0},{3,1},{4,6},{5,7},{6,4},{7,5},{8,10},{9,11},{10,... | collective-permute-start | bytes 393224 | tf_op jit(solution)/shard_map/ppermute | solution.py:19
  8.6 1.3 %collective-permute-start.4 = (bf16[32,1024]{1,0:T(8,128)(2,1)S(1)}, bf16[32,1024]{1,0:T(8,128)(2,1)S(1)}, u32[]{:S(2)}, u32[]{:S(2)}) collective-permute-start(bf16[32,1024]{1,0:T(8,128)(2,1)S(1)} %get-tuple-element.25), channel_id=1, source_target_pairs={{0,24},{8,16},{16,8},{24,0},{1,25},{9,17},{17,9},{25,1},{2,26},{10... | collective-permute-start | bytes 196616 | tf_op jit(solution)/shard_map/ppermute | solution.py:19
  10.0 0.0 collective-permute-done.3.refs_4_
  10.0 0.2 collective-permute-start.5
  10.2 0.9 %shard_map.46 = (f32[4,32,128]{2,1,0:T(8,128)S(1)}, s32[1,8]{1,0:T(1,128)S(1)}) custom-call(f32[4,32,128]{2,1,0:T(8,128)} %residual_ref.1, s32[1,8]{1,0:T(1,128)} %owner_ref.1), custom_call_target="tpu_custom_call" | custom-call | bytes 16777216 | tf_op jit(solution)/shard_map/pallas_call | solution.py:28
  11.1 3.7 %collective-permute-done.4.refs_5_ = bf16[32,1024]{1,0:T(8,128)(2,1)S(1)} collective-permute-done((bf16[32,1024]{1,0:T(8,128)(2,1)S(1)}, bf16[32,1024]{1,0:T(8,128)(2,1)S(1)}, u32[]{:S(2)}, u32[]{:S(2)}) %collective-permute-start.4) | collective-permute-done | bytes 65568 | tf_op jit(solution)/shard_map/ppermute | solution.py:19
  14.8 0.1 collective-permute-done.5.refs_6_
  15.0 0.0 collective-permute-done.2.refs_3_
  15.0 0.0 collective-permute-done.1.refs_2_
  15.0 0.0 collective-permute-done.refs_1_
  15.0 0.1 shard_map.48
  15.0 0.1 collective-permute-start.6
  15.1 0.5 %collective-permute-start.7 = (bf16[128,1024]{1,0:T(8,128)(2,1)S(1)}, bf16[128,1024]{1,0:T(8,128)(2,1)S(1)}, u32[]{:S(2)}, u32[]{:S(2)}) collective-permute-start(bf16[128,1024]{1,0:T(8,128)(2,1)S(1)} %get-tuple-element.32.refs_1_), channel_id=1, source_target_pairs={{0,1},{1,0},{2,3},{3,2},{4,5},{5,4},{6,7},{7,6},{8,9},{9,8},{10,11... | collective-permute-start | bytes 786440 | tf_op jit(solution)/shard_map/ppermute | solution.py:19
  15.6 0.3 %shard_map.49.near_part = f32[256,128]{1,0:T(8,128)S(1)} custom-call(bf16[128,1024]{1,0:T(8,128)(2,1)S(1)} %get-tuple-element.30.lhs, bf16[128,1024]{1,0:T(8,128)(2,1)S(1)} %get-tuple-element.31.refs_0_, bf16[128,1024]{1,0:T(8,128)(2,1)S(1)} %get-tuple-element.32.refs_1_), custom_call_target="tpu_custom_call" | custom-call | tf_op jit(solution)/shard_map/pallas_call | solution.py:28
  15.9 0.7 %collective-permute-done.6.refs_0_ = bf16[128,1024]{1,0:T(8,128)(2,1)S(1)} collective-permute-done((bf16[128,1024]{1,0:T(8,128)(2,1)S(1)}, bf16[128,1024]{1,0:T(8,128)(2,1)S(1)}, u32[]{:S(2)}, u32[]{:S(2)}) %collective-permute-start.6) | collective-permute-done | bytes 262176 | tf_op jit(solution)/shard_map/ppermute | solution.py:19
  16.6 0.2 shard_map.50.far_part
  16.9 0.1 collective-permute-done.7.last
  17.0 0.4 %shard_map.51 = (f32[144,128]{1,0:T(8,128)S(1)}, f32[144,128]{1,0:T(8,128)S(1)}, f32[144,128]{1,0:T(8,128)S(1)}, f32[128,128]{1,0:T(8,128)S(1)}) custom-call(s32[1,8]{1,0:T(1,128)S(1)} %get-tuple-element.28.owner_ref, f32[4,32,128]{2,1,0:T(8,128)S(1)} %get-tuple-element.29.residual_ref, bf16[128,1024]{1,0:T(8,128)(2,1)S(1)} %get-tuple-element.30.lhs, ...), custom_call_target="tpu_custom_call" | custom-call | tf_op jit(solution)/shard_map/pallas_call | solution.py:28
  17.4 1.9 %collective-permute-start.10 = (f16[144,128]{1,0:T(8,128)(2,1)S(1)}, f16[144,128]{1,0:T(8,128)(2,1)S(1)}, u32[]{:S(2)}, u32[]{:S(2)}) collective-permute-start(f16[144,128]{1,0:T(8,128)(2,1)S(1)} %convert_element_type.22), channel_id=1, source_target_pairs={{0,24},{8,16},{16,8},{24,0},{1,25},{9,17},{17,9},{25,1},{2,26},{10... | collective-permute-start | bytes 110600 | tf_op jit(solution)/shard_map/ppermute | solution.py:19
  19.3 0.2 collective-permute-start.9
  19.5 2.4 %collective-permute-start.8 = (f16[144,128]{1,0:T(8,128)(2,1)S(1)}, f16[144,128]{1,0:T(8,128)(2,1)S(1)}, u32[]{:S(2)}, u32[]{:S(2)}) collective-permute-start(f16[144,128]{1,0:T(8,128)(2,1)S(1)} %convert_element_type.18), channel_id=1, source_target_pairs={{0,8},{8,0},{16,24},{24,16},{1,9},{9,1},{17,25},{25,17},{2,10},{10... | collective-permute-start | bytes 110600 | tf_op jit(solution)/shard_map/ppermute | solution.py:19
  22.0 1.3 %collective-permute-done.10 = f16[144,128]{1,0:T(8,128)(2,1)S(1)} collective-permute-done((f16[144,128]{1,0:T(8,128)(2,1)S(1)}, f16[144,128]{1,0:T(8,128)(2,1)S(1)}, u32[]{:S(2)}, u32[]{:S(2)}) %collective-permute-start.10) | collective-permute-done | bytes 36896 | tf_op jit(solution)/shard_map/ppermute | solution.py:19
  23.3 1.1 %collective-permute-done.9 = f16[144,128]{1,0:T(8,128)(2,1)S(1)} collective-permute-done((f16[144,128]{1,0:T(8,128)(2,1)S(1)}, f16[144,128]{1,0:T(8,128)(2,1)S(1)}, u32[]{:S(2)}, u32[]{:S(2)}) %collective-permute-start.9) | collective-permute-done | bytes 36896 | tf_op jit(solution)/shard_map/ppermute | solution.py:19
  24.5 0.1 collective-permute-done.8
  24.6 0.7 %fusion = f32[128,128]{1,0:T(8,128)} fusion(f32[144,128]{1,0:T(8,128)S(1)} %convert_element_type.23, f32[144,128]{1,0:T(8,128)S(1)} %convert_element_type.21, f32[128,128]{1,0:T(8,128)S(1)} %get-tuple-element.33, f32[144,128]{1,0:T(8,128)S(1)} %convert_element_type.19, f32[128]{0:T(128)S(1)} %fusion.5, f32[128]{0:T(128)S(1)} %fusion.8, f32[128]{0:T(128)S(1)} %fusion.11), kind=kLoop, calls=%fused_computation.1 | loop fusion | flops 98304 | bytes 329216 | tf_op jit(solution)/shard_map/add | solution.py:176
  (9 shorter events, 0.1 us)
Async XLA Ops:
  1.0 8.9 %collective-permute-start.3 = (bf16[32,1024]{1,0:T(8,128)(2,1)S(1)}, bf16[32,1024]{1,0:T(8,128)(2,1)S(1)}, u32[]{:S(2)}, u32[]{:S(2)}) collective-permute-start(bf16[32,1024]{1,0:T(8,128)(2,1)S(1)} %get-tuple-element.24), channel_id=1, source_target_pairs={{0,16},{8,24},{16,0},{24,8},{1,17},{9,25},{17,1},{25,9},{2,18},{10... | collective-permute-start | bytes 196616 | tf_op jit(solution)/shard_map/ppermute | solution.py:19
  5.2 9.8 %collective-permute-start.2 = (bf16[64,1024]{1,0:T(8,128)(2,1)S(1)}, bf16[64,1024]{1,0:T(8,128)(2,1)S(1)}, u32[]{:S(2)}, u32[]{:S(2)}) collective-permute-start(bf16[64,1024]{1,0:T(8,128)(2,1)S(1)} %get-tuple-element.23.refs_0_), channel_id=1, source_target_pairs={{0,6},{1,7},{2,4},{3,5},{4,2},{5,3},{6,0},{7,1},{8,14},{9,15},{10,... | collective-permute-start | bytes 393224 | tf_op jit(solution)/shard_map/ppermute | solution.py:19
  7.6 7.4 %collective-permute-start.1 = (bf16[64,1024]{1,0:T(8,128)(2,1)S(1)}, bf16[64,1024]{1,0:T(8,128)(2,1)S(1)}, u32[]{:S(2)}, u32[]{:S(2)}) collective-permute-start(bf16[64,1024]{1,0:T(8,128)(2,1)S(1)} %get-tuple-element.23.refs_0_), channel_id=1, source_target_pairs={{0,4},{1,5},{2,6},{3,7},{4,0},{5,1},{6,2},{7,3},{8,12},{9,13},{10,... | collective-permute-start | bytes 393224 | tf_op jit(solution)/shard_map/ppermute | solution.py:19
  8.1 6.9 %collective-permute-start = (bf16[64,1024]{1,0:T(8,128)(2,1)S(1)}, bf16[64,1024]{1,0:T(8,128)(2,1)S(1)}, u32[]{:S(2)}, u32[]{:S(2)}) collective-permute-start(bf16[64,1024]{1,0:T(8,128)(2,1)S(1)} %get-tuple-element.23.refs_0_), channel_id=1, source_target_pairs={{0,2},{1,3},{2,0},{3,1},{4,6},{5,7},{6,4},{7,5},{8,10},{9,11},{10,... | collective-permute-start | bytes 393224 | tf_op jit(solution)/shard_map/ppermute | solution.py:19
  8.6 6.2 %collective-permute-start.4 = (bf16[32,1024]{1,0:T(8,128)(2,1)S(1)}, bf16[32,1024]{1,0:T(8,128)(2,1)S(1)}, u32[]{:S(2)}, u32[]{:S(2)}) collective-permute-start(bf16[32,1024]{1,0:T(8,128)(2,1)S(1)} %get-tuple-element.25), channel_id=1, source_target_pairs={{0,24},{8,16},{16,8},{24,0},{1,25},{9,17},{17,9},{25,1},{2,26},{10... | collective-permute-start | bytes 196616 | tf_op jit(solution)/shard_map/ppermute | solution.py:19
  10.0 5.0 %collective-permute-start.5 = (bf16[32,1024]{1,0:T(8,128)(2,1)S(1)}, bf16[32,1024]{1,0:T(8,128)(2,1)S(1)}, u32[]{:S(2)}, u32[]{:S(2)}) collective-permute-start(bf16[32,1024]{1,0:T(8,128)(2,1)S(1)} %get-tuple-element.26), channel_id=1, source_target_pairs={{0,8},{8,0},{16,24},{24,16},{1,9},{9,1},{17,25},{25,17},{2,10},{10... | collective-permute-start | bytes 196616 | tf_op jit(solution)/shard_map/ppermute | solution.py:19
  15.0 1.6 %collective-permute-start.6 = (bf16[128,1024]{1,0:T(8,128)(2,1)S(1)}, bf16[128,1024]{1,0:T(8,128)(2,1)S(1)}, u32[]{:S(2)}, u32[]{:S(2)}) collective-permute-start(bf16[128,1024]{1,0:T(8,128)(2,1)S(1)} %get-tuple-element.31.refs_0_), channel_id=1, source_target_pairs={{0,1},{1,0},{2,3},{3,2},{4,5},{5,4},{6,7},{7,6},{8,9},{9,8},{10,11... | collective-permute-start | bytes 786440 | tf_op jit(solution)/shard_map/ppermute | solution.py:19
  15.1 1.9 %collective-permute-start.7 = (bf16[128,1024]{1,0:T(8,128)(2,1)S(1)}, bf16[128,1024]{1,0:T(8,128)(2,1)S(1)}, u32[]{:S(2)}, u32[]{:S(2)}) collective-permute-start(bf16[128,1024]{1,0:T(8,128)(2,1)S(1)} %get-tuple-element.32.refs_1_), channel_id=1, source_target_pairs={{0,1},{1,0},{2,3},{3,2},{4,5},{5,4},{6,7},{7,6},{8,9},{9,8},{10,11... | collective-permute-start | bytes 786440 | tf_op jit(solution)/shard_map/ppermute | solution.py:19
  17.4 5.9 %collective-permute-start.10 = (f16[144,128]{1,0:T(8,128)(2,1)S(1)}, f16[144,128]{1,0:T(8,128)(2,1)S(1)}, u32[]{:S(2)}, u32[]{:S(2)}) collective-permute-start(f16[144,128]{1,0:T(8,128)(2,1)S(1)} %convert_element_type.22), channel_id=1, source_target_pairs={{0,24},{8,16},{16,8},{24,0},{1,25},{9,17},{17,9},{25,1},{2,26},{10... | collective-permute-start | bytes 110600 | tf_op jit(solution)/shard_map/ppermute | solution.py:19
  19.3 5.1 %collective-permute-start.9 = (f16[144,128]{1,0:T(8,128)(2,1)S(1)}, f16[144,128]{1,0:T(8,128)(2,1)S(1)}, u32[]{:S(2)}, u32[]{:S(2)}) collective-permute-start(f16[144,128]{1,0:T(8,128)(2,1)S(1)} %convert_element_type.20), channel_id=1, source_target_pairs={{0,16},{8,24},{16,0},{24,8},{1,17},{9,25},{17,1},{25,9},{2,18},{10... | collective-permute-start | bytes 110600 | tf_op jit(solution)/shard_map/ppermute | solution.py:19
  19.5 5.1 %collective-permute-start.8 = (f16[144,128]{1,0:T(8,128)(2,1)S(1)}, f16[144,128]{1,0:T(8,128)(2,1)S(1)}, u32[]{:S(2)}, u32[]{:S(2)}) collective-permute-start(f16[144,128]{1,0:T(8,128)(2,1)S(1)} %convert_element_type.18), channel_id=1, source_target_pairs={{0,8},{8,0},{16,24},{24,16},{1,9},{9,1},{17,25},{25,17},{2,10},{10... | collective-permute-start | bytes 110600 | tf_op jit(solution)/shard_map/ppermute | solution.py:19

commit v12 on v8

--- a/solution.py
+++ b/solution.py
@@ -171,8 +171,9 @@
     *fars, last = [exchange(near, "col", 1) for near in nears]
     parts = contract(steps, owner, residual, lhs, products(lhs, nears), products(lhs, fars), last)
     total = parts[-1]
-    for step, part in zip(steps[-2::-1], parts[-2::-1]):
-        total = total + exchange_partial(part, step)
+    middle_last = sorted(range(1, rows), key=lambda step: (step == rows // 2, step))
+    for step in middle_last:
+        total = total + exchange_partial(parts[steps.index(step)], step)
     return total.reshape(residual_in.shape)
 
 

time: 25.4 us -> 26.1 us (1.028)
  waiting for transfers between devices: 7.14 us -> 8.81 us
  starting transfers between devices: 14.3 us -> 13.4 us
    ppermute x11, waiting for transfers between devices: 7.14 us -> 8.81 us  [exchange(): return lax.ppermute(value, axis, [(i, i ^ step) for i in range(n)])]
    ppermute x11, starting transfers between devices: 14.3 us -> 13.4 us  [exchange(): return lax.ppermute(value, axis, [(i, i ^ step) for i in range(n)])]
where the time goes in v12:
time: 26.1 us; the launch traced here: 26 us
  starting transfers between devices  13.4 us (51%)
  waiting for transfers between devices  8.81 us (34%)
  Pallas kernels  2.87 us (11%)
  other arithmetic  0.73 us (3%)
    ppermute x11, starting transfers between devices, exchange(): return lax.ppermute(value, axis, [(i, i ^ step) for i in range(n)])  13.4 us
    ppermute x11, waiting for transfers between devices, exchange(): return lax.ppermute(value, axis, [(i, i ^ step) for i in range(n)])  8.81 us
    pallas_call x6, Pallas kernels, call(): pl.pallas_call(kernel, out_shape=outs, in_specs=specs, out_specs=[VMEM] *...  2.87 us
    add x1, other arithmetic, shards(): total = total + exchange_partial(parts[steps.index(step)], step)  0.65 us
  transfers between devices with their start and end apart: 11, of which 5 were waited for; matrix products, arithmetic and copies ran while one was open for 0% of the time, Pallas kernels for 5%

profile of v12, /device:TPU:0, one launch (start us, length us, event | category | flops | bytes accessed | tf_op | source)
XLA Modules:
  0.0 26.0 jit_solution(2296587318146443258)
XLA Ops:
  0.0 1.0 %shard_map.47 = (bf16[64,1024]{1,0:T(8,128)(2,1)S(1)}, bf16[32,1024]{1,0:T(8,128)(2,1)S(1)}, bf16[32,1024]{1,0:T(8,128)(2,1)S(1)}, bf16[32,1024]{1,0:T(8,128)(2,1)S(1)}, bf16[32,1024]{1,0:T(8,128)(2,1)S(1)}) custom-call(bf16[64,1024]{1,0:T(8,128)(2,1)} %panel_ref.1, bf16[1,32,4096]{2,1,0:T(8,128)(2,1)} %amp_ref.1), custom_call_target="tpu_custom_call" | custom-call | tf_op jit(solution)/shard_map/pallas_call | solution.py:28
  1.0 5.1 %collective-permute-start.3 = (bf16[32,1024]{1,0:T(8,128)(2,1)S(1)}, bf16[32,1024]{1,0:T(8,128)(2,1)S(1)}, u32[]{:S(2)}, u32[]{:S(2)}) collective-permute-start(bf16[32,1024]{1,0:T(8,128)(2,1)S(1)} %get-tuple-element.24), channel_id=1, source_target_pairs={{0,24},{8,16},{16,8},{24,0},{1,25},{9,17},{17,9},{25,1},{2,26},{10... | collective-permute-start | bytes 196616 | tf_op jit(solution)/shard_map/ppermute | solution.py:19
  6.2 2.4 %collective-permute-start.2 = (bf16[64,1024]{1,0:T(8,128)(2,1)S(1)}, bf16[64,1024]{1,0:T(8,128)(2,1)S(1)}, u32[]{:S(2)}, u32[]{:S(2)}) collective-permute-start(bf16[64,1024]{1,0:T(8,128)(2,1)S(1)} %get-tuple-element.23.refs_0_), channel_id=1, source_target_pairs={{0,6},{1,7},{2,4},{3,5},{4,2},{5,3},{6,0},{7,1},{8,14},{9,15},{10,... | collective-permute-start | bytes 393224 | tf_op jit(solution)/shard_map/ppermute | solution.py:19
  8.6 0.5 %collective-permute-start.1 = (bf16[64,1024]{1,0:T(8,128)(2,1)S(1)}, bf16[64,1024]{1,0:T(8,128)(2,1)S(1)}, u32[]{:S(2)}, u32[]{:S(2)}) collective-permute-start(bf16[64,1024]{1,0:T(8,128)(2,1)S(1)} %get-tuple-element.23.refs_0_), channel_id=1, source_target_pairs={{0,4},{1,5},{2,6},{3,7},{4,0},{5,1},{6,2},{7,3},{8,12},{9,13},{10,... | collective-permute-start | bytes 393224 | tf_op jit(solution)/shard_map/ppermute | solution.py:19
  9.1 0.5 %collective-permute-start = (bf16[64,1024]{1,0:T(8,128)(2,1)S(1)}, bf16[64,1024]{1,0:T(8,128)(2,1)S(1)}, u32[]{:S(2)}, u32[]{:S(2)}) collective-permute-start(bf16[64,1024]{1,0:T(8,128)(2,1)S(1)} %get-tuple-element.23.refs_0_), channel_id=1, source_target_pairs={{0,2},{1,3},{2,0},{3,1},{4,6},{5,7},{6,4},{7,5},{8,10},{9,11},{10,... | collective-permute-start | bytes 393224 | tf_op jit(solution)/shard_map/ppermute | solution.py:19
  9.7 0.0 collective-permute-start.4
  9.7 0.0 collective-permute-done.3.refs_4_
  9.7 0.6 %collective-permute-start.5 = (bf16[32,1024]{1,0:T(8,128)(2,1)S(1)}, bf16[32,1024]{1,0:T(8,128)(2,1)S(1)}, u32[]{:S(2)}, u32[]{:S(2)}) collective-permute-start(bf16[32,1024]{1,0:T(8,128)(2,1)S(1)} %get-tuple-element.26), channel_id=1, source_target_pairs={{0,8},{8,0},{16,24},{24,16},{1,9},{9,1},{17,25},{25,17},{2,10},{10... | collective-permute-start | bytes 196616 | tf_op jit(solution)/shard_map/ppermute | solution.py:19
  10.3 0.9 %shard_map.46 = (f32[4,32,128]{2,1,0:T(8,128)S(1)}, s32[1,8]{1,0:T(1,128)S(1)}) custom-call(f32[4,32,128]{2,1,0:T(8,128)} %residual_ref.1, s32[1,8]{1,0:T(1,128)} %owner_ref.1), custom_call_target="tpu_custom_call" | custom-call | bytes 16777216 | tf_op jit(solution)/shard_map/pallas_call | solution.py:28
  11.2 3.9 %collective-permute-done.4.refs_5_ = bf16[32,1024]{1,0:T(8,128)(2,1)S(1)} collective-permute-done((bf16[32,1024]{1,0:T(8,128)(2,1)S(1)}, bf16[32,1024]{1,0:T(8,128)(2,1)S(1)}, u32[]{:S(2)}, u32[]{:S(2)}) %collective-permute-start.4) | collective-permute-done | bytes 65568 | tf_op jit(solution)/shard_map/ppermute | solution.py:19
  15.0 0.0 collective-permute-done.5.refs_6_
  15.0 0.0 collective-permute-done.2.refs_3_
  15.0 0.0 collective-permute-done.1.refs_2_
  15.0 0.0 collective-permute-done.refs_1_
  15.0 0.1 shard_map.48
  15.1 0.1 collective-permute-start.6
  15.2 0.5 %collective-permute-start.7 = (bf16[128,1024]{1,0:T(8,128)(2,1)S(1)}, bf16[128,1024]{1,0:T(8,128)(2,1)S(1)}, u32[]{:S(2)}, u32[]{:S(2)}) collective-permute-start(bf16[128,1024]{1,0:T(8,128)(2,1)S(1)} %get-tuple-element.32.refs_1_), channel_id=1, source_target_pairs={{0,1},{1,0},{2,3},{3,2},{4,5},{5,4},{6,7},{7,6},{8,9},{9,8},{10,11... | collective-permute-start | bytes 786440 | tf_op jit(solution)/shard_map/ppermute | solution.py:19
  15.7 0.3 %shard_map.49.near_part = f32[256,128]{1,0:T(8,128)S(1)} custom-call(bf16[128,1024]{1,0:T(8,128)(2,1)S(1)} %get-tuple-element.30.lhs, bf16[128,1024]{1,0:T(8,128)(2,1)S(1)} %get-tuple-element.31.refs_0_, bf16[128,1024]{1,0:T(8,128)(2,1)S(1)} %get-tuple-element.32.refs_1_), custom_call_target="tpu_custom_call" | custom-call | tf_op jit(solution)/shard_map/pallas_call | solution.py:28
  16.0 0.7 %collective-permute-done.6.refs_0_ = bf16[128,1024]{1,0:T(8,128)(2,1)S(1)} collective-permute-done((bf16[128,1024]{1,0:T(8,128)(2,1)S(1)}, bf16[128,1024]{1,0:T(8,128)(2,1)S(1)}, u32[]{:S(2)}, u32[]{:S(2)}) %collective-permute-start.6) | collective-permute-done | bytes 262176 | tf_op jit(solution)/shard_map/ppermute | solution.py:19
  16.7 0.2 shard_map.50.far_part
  16.9 0.1 collective-permute-done.7.last
  17.1 0.4 %shard_map.51 = (f32[144,128]{1,0:T(8,128)S(1)}, f32[144,128]{1,0:T(8,128)S(1)}, f32[144,128]{1,0:T(8,128)S(1)}, f32[128,128]{1,0:T(8,128)S(1)}) custom-call(s32[1,8]{1,0:T(1,128)S(1)} %get-tuple-element.28.owner_ref, f32[4,32,128]{2,1,0:T(8,128)S(1)} %get-tuple-element.29.residual_ref, bf16[128,1024]{1,0:T(8,128)(2,1)S(1)} %get-tuple-element.30.lhs, ...), custom_call_target="tpu_custom_call" | custom-call | tf_op jit(solution)/shard_map/pallas_call | solution.py:28
  17.5 1.9 %collective-permute-start.10 = (f16[144,128]{1,0:T(8,128)(2,1)S(1)}, f16[144,128]{1,0:T(8,128)(2,1)S(1)}, u32[]{:S(2)}, u32[]{:S(2)}) collective-permute-start(f16[144,128]{1,0:T(8,128)(2,1)S(1)} %convert_element_type.22), channel_id=1, source_target_pairs={{0,16},{8,24},{16,0},{24,8},{1,17},{9,25},{17,1},{25,9},{2,18},{10... | collective-permute-start | bytes 110600 | tf_op jit(solution)/shard_map/ppermute | solution.py:19
  19.4 0.7 %collective-permute-start.9 = (f16[144,128]{1,0:T(8,128)(2,1)S(1)}, f16[144,128]{1,0:T(8,128)(2,1)S(1)}, u32[]{:S(2)}, u32[]{:S(2)}) collective-permute-start(f16[144,128]{1,0:T(8,128)(2,1)S(1)} %convert_element_type.20), channel_id=1, source_target_pairs={{0,24},{8,16},{16,8},{24,0},{1,25},{9,17},{17,9},{25,1},{2,26},{10... | collective-permute-start | bytes 110600 | tf_op jit(solution)/shard_map/ppermute | solution.py:19
  20.1 1.0 %collective-permute-start.8 = (f16[144,128]{1,0:T(8,128)(2,1)S(1)}, f16[144,128]{1,0:T(8,128)(2,1)S(1)}, u32[]{:S(2)}, u32[]{:S(2)}) collective-permute-start(f16[144,128]{1,0:T(8,128)(2,1)S(1)} %convert_element_type.18), channel_id=1, source_target_pairs={{0,8},{8,0},{16,24},{24,16},{1,9},{9,1},{17,25},{25,17},{2,10},{10... | collective-permute-start | bytes 110600 | tf_op jit(solution)/shard_map/ppermute | solution.py:19
  21.1 1.7 %collective-permute-done.10 = f16[144,128]{1,0:T(8,128)(2,1)S(1)} collective-permute-done((f16[144,128]{1,0:T(8,128)(2,1)S(1)}, f16[144,128]{1,0:T(8,128)(2,1)S(1)}, u32[]{:S(2)}, u32[]{:S(2)}) %collective-permute-start.10) | collective-permute-done | bytes 36896 | tf_op jit(solution)/shard_map/ppermute | solution.py:19
  22.9 2.3 %collective-permute-done.9 = f16[144,128]{1,0:T(8,128)(2,1)S(1)} collective-permute-done((f16[144,128]{1,0:T(8,128)(2,1)S(1)}, f16[144,128]{1,0:T(8,128)(2,1)S(1)}, u32[]{:S(2)}, u32[]{:S(2)}) %collective-permute-start.9) | collective-permute-done | bytes 36896 | tf_op jit(solution)/shard_map/ppermute | solution.py:19
  25.3 0.0 collective-permute-done.8
  25.3 0.7 %fusion = f32[128,128]{1,0:T(8,128)} fusion(f32[144,128]{1,0:T(8,128)S(1)} %convert_element_type.23, f32[144,128]{1,0:T(8,128)S(1)} %convert_element_type.21, f32[128,128]{1,0:T(8,128)S(1)} %get-tuple-element.33, f32[144,128]{1,0:T(8,128)S(1)} %convert_element_type.19, f32[128]{0:T(128)S(1)} %fusion.5, f32[128]{0:T(128)S(1)} %fusion.8, f32[128]{0:T(128)S(1)} %fusion.11), kind=kLoop, calls=%fused_computation.1 | loop fusion | flops 98304 | bytes 329216 | tf_op jit(solution)/shard_map/add | solution.py:176
  (9 shorter events, 0.1 us)
Async XLA Ops:
  1.0 8.6 %collective-permute-start.3 = (bf16[32,1024]{1,0:T(8,128)(2,1)S(1)}, bf16[32,1024]{1,0:T(8,128)(2,1)S(1)}, u32[]{:S(2)}, u32[]{:S(2)}) collective-permute-start(bf16[32,1024]{1,0:T(8,128)(2,1)S(1)} %get-tuple-element.24), channel_id=1, source_target_pairs={{0,24},{8,16},{16,8},{24,0},{1,25},{9,17},{17,9},{25,1},{2,26},{10... | collective-permute-start | bytes 196616 | tf_op jit(solution)/shard_map/ppermute | solution.py:19
  6.2 8.9 %collective-permute-start.2 = (bf16[64,1024]{1,0:T(8,128)(2,1)S(1)}, bf16[64,1024]{1,0:T(8,128)(2,1)S(1)}, u32[]{:S(2)}, u32[]{:S(2)}) collective-permute-start(bf16[64,1024]{1,0:T(8,128)(2,1)S(1)} %get-tuple-element.23.refs_0_), channel_id=1, source_target_pairs={{0,6},{1,7},{2,4},{3,5},{4,2},{5,3},{6,0},{7,1},{8,14},{9,15},{10,... | collective-permute-start | bytes 393224 | tf_op jit(solution)/shard_map/ppermute | solution.py:19
  8.6 6.4 %collective-permute-start.1 = (bf16[64,1024]{1,0:T(8,128)(2,1)S(1)}, bf16[64,1024]{1,0:T(8,128)(2,1)S(1)}, u32[]{:S(2)}, u32[]{:S(2)}) collective-permute-start(bf16[64,1024]{1,0:T(8,128)(2,1)S(1)} %get-tuple-element.23.refs_0_), channel_id=1, source_target_pairs={{0,4},{1,5},{2,6},{3,7},{4,0},{5,1},{6,2},{7,3},{8,12},{9,13},{10,... | collective-permute-start | bytes 393224 | tf_op jit(solution)/shard_map/ppermute | solution.py:19
  9.1 5.9 %collective-permute-start = (bf16[64,1024]{1,0:T(8,128)(2,1)S(1)}, bf16[64,1024]{1,0:T(8,128)(2,1)S(1)}, u32[]{:S(2)}, u32[]{:S(2)}) collective-permute-start(bf16[64,1024]{1,0:T(8,128)(2,1)S(1)} %get-tuple-element.23.refs_0_), channel_id=1, source_target_pairs={{0,2},{1,3},{2,0},{3,1},{4,6},{5,7},{6,4},{7,5},{8,10},{9,11},{10,... | collective-permute-start | bytes 393224 | tf_op jit(solution)/shard_map/ppermute | solution.py:19
  9.7 5.4 %collective-permute-start.4 = (bf16[32,1024]{1,0:T(8,128)(2,1)S(1)}, bf16[32,1024]{1,0:T(8,128)(2,1)S(1)}, u32[]{:S(2)}, u32[]{:S(2)}) collective-permute-start(bf16[32,1024]{1,0:T(8,128)(2,1)S(1)} %get-tuple-element.25), channel_id=1, source_target_pairs={{0,16},{8,24},{16,0},{24,8},{1,17},{9,25},{17,1},{25,9},{2,18},{10... | collective-permute-start | bytes 196616 | tf_op jit(solution)/shard_map/ppermute | solution.py:19
  9.7 5.4 %collective-permute-start.5 = (bf16[32,1024]{1,0:T(8,128)(2,1)S(1)}, bf16[32,1024]{1,0:T(8,128)(2,1)S(1)}, u32[]{:S(2)}, u32[]{:S(2)}) collective-permute-start(bf16[32,1024]{1,0:T(8,128)(2,1)S(1)} %get-tuple-element.26), channel_id=1, source_target_pairs={{0,8},{8,0},{16,24},{24,16},{1,9},{9,1},{17,25},{25,17},{2,10},{10... | collective-permute-start | bytes 196616 | tf_op jit(solution)/shard_map/ppermute | solution.py:19
  15.1 1.6 %collective-permute-start.6 = (bf16[128,1024]{1,0:T(8,128)(2,1)S(1)}, bf16[128,1024]{1,0:T(8,128)(2,1)S(1)}, u32[]{:S(2)}, u32[]{:S(2)}) collective-permute-start(bf16[128,1024]{1,0:T(8,128)(2,1)S(1)} %get-tuple-element.31.refs_0_), channel_id=1, source_target_pairs={{0,1},{1,0},{2,3},{3,2},{4,5},{5,4},{6,7},{7,6},{8,9},{9,8},{10,11... | collective-permute-start | bytes 786440 | tf_op jit(solution)/shard_map/ppermute | solution.py:19
  15.2 1.9 %collective-permute-start.7 = (bf16[128,1024]{1,0:T(8,128)(2,1)S(1)}, bf16[128,1024]{1,0:T(8,128)(2,1)S(1)}, u32[]{:S(2)}, u32[]{:S(2)}) collective-permute-start(bf16[128,1024]{1,0:T(8,128)(2,1)S(1)} %get-tuple-element.32.refs_1_), channel_id=1, source_target_pairs={{0,1},{1,0},{2,3},{3,2},{4,5},{5,4},{6,7},{7,6},{8,9},{9,8},{10,11... | collective-permute-start | bytes 786440 | tf_op jit(solution)/shard_map/ppermute | solution.py:19
  17.5 5.4 %collective-permute-start.10 = (f16[144,128]{1,0:T(8,128)(2,1)S(1)}, f16[144,128]{1,0:T(8,128)(2,1)S(1)}, u32[]{:S(2)}, u32[]{:S(2)}) collective-permute-start(f16[144,128]{1,0:T(8,128)(2,1)S(1)} %convert_element_type.22), channel_id=1, source_target_pairs={{0,16},{8,24},{16,0},{24,8},{1,17},{9,25},{17,1},{25,9},{2,18},{10... | collective-permute-start | bytes 110600 | tf_op jit(solution)/shard_map/ppermute | solution.py:19
  19.4 5.8 %collective-permute-start.9 = (f16[144,128]{1,0:T(8,128)(2,1)S(1)}, f16[144,128]{1,0:T(8,128)(2,1)S(1)}, u32[]{:S(2)}, u32[]{:S(2)}) collective-permute-start(f16[144,128]{1,0:T(8,128)(2,1)S(1)} %convert_element_type.20), channel_id=1, source_target_pairs={{0,24},{8,16},{16,8},{24,0},{1,25},{9,17},{17,9},{25,1},{2,26},{10... | collective-permute-start | bytes 110600 | tf_op jit(solution)/shard_map/ppermute | solution.py:19
  20.1 5.1 %collective-permute-start.8 = (f16[144,128]{1,0:T(8,128)(2,1)S(1)}, f16[144,128]{1,0:T(8,128)(2,1)S(1)}, u32[]{:S(2)}, u32[]{:S(2)}) collective-permute-start(f16[144,128]{1,0:T(8,128)(2,1)S(1)} %convert_element_type.18), channel_id=1, source_target_pairs={{0,8},{8,0},{16,24},{24,16},{1,9},{9,1},{17,25},{25,17},{2,10},{10... | collective-permute-start | bytes 110600 | tf_op jit(solution)/shard_map/ppermute | solution.py:19
